TPU v7x, 128 devices: a whole 4x4x4 slice. The times are simulated.
128 devices in a mesh: grid: 8 (over z, core), mesh: 16 (over x, y).
Axes of the slice: x: 4, y: 4, z: 4, core: 2. Of those that a mesh axis runs over, the one named last changes fastest.
Arguments:
- grid_latent: bfloat16 [393216, 512], P(('grid', 'mesh')), may hold values from -6 to 6
- mesh_latent: bfloat16 [32768, 512], P('mesh'), may hold values from -6 to 6
- mesh_cotangent: bfloat16 [32768, 512], P('mesh'), may hold values from -18 to 18
- w_send: bfloat16 [512, 512], replicated, may hold values from -0.25 to 0.25
- w_self_enc: bfloat16 [512, 512], replicated, may hold values from -0.25 to 0.25
- w_agg_enc: bfloat16 [512, 512], replicated, may hold values from -0.0078125 to 0.0078125
- w_out_enc: bfloat16 [512, 512], replicated, may hold values from -0.25 to 0.25
- w_pass: bfloat16 [512, 512], replicated, may hold values from -0.25 to 0.25
- w_self_proc: bfloat16 [512, 512], replicated, may hold values from -0.25 to 0.25
- w_agg_proc: bfloat16 [512, 512], replicated, may hold values from -0.01171875 to 0.01171875
- w_out_proc: bfloat16 [512, 512], replicated, may hold values from -0.25 to 0.25
- enc_source: int32 [4096], P(('grid', 'mesh')), may hold values from 0 to 23
- enc_part: int32 [4096, 1], P(('grid', 'mesh')), may hold values from 0 to 15; in each aligned block of 32 rows (0 to 31, 32 to 63, ...) at most 3 rows name the same one
- enc_block: int32 [4096], P(('grid', 'mesh')), may hold values from 0 to 15
- enc_mask: int32 [4096, 128, 128], P(('grid', 'mesh')), may hold values 0 or 1
- proc_source: int32 [2048], P(('grid', 'mesh')), may hold values from 0 to 47
- proc_target: int32 [2048], P(('grid', 'mesh')), may hold values from 0 to 15
- proc_mask: int32 [2048, 128, 128], P(('grid', 'mesh')), may hold values 0 or 1
Outputs:
- mesh_out: bfloat16 [32768, 512], P('mesh')
- grid_grad: bfloat16 [393216, 512], P(('grid', 'mesh'))
Inputs may be any that keep to these rules, and one draw needn't show every extreme that they name: `enc_part`: within the rows of one device, no partition is named by more than 3 rows.
All inputs are finite; a program needn't handle non-finite values. No bound on the sum of `enc_mask` or of `proc_mask` on one device may be relied on, other than what follows from the above.
Results may differ from a plain program's by a relative error of at most 0.033.
Values may be sent and summed in bfloat16 or wider, within the bound.
No kernel may reach another device: no remote copies, remote signals or barrier semaphores. Data moves between devices by JAX's collectives and lax.ppermute only.
A program may use at most 192 MiB of HBM per device.

v0:
```python
import jax
import jax.numpy as jnp
from jax import lax
from jax.sharding import PartitionSpec as P


def padded(cells, sides, width):
    for axis, dim in sides:
        count = lax.axis_size(axis)
        head = lax.slice_in_dim(cells, 0, width, axis=dim)
        tail = lax.slice_in_dim(cells, cells.shape[dim] - width, cells.shape[dim], axis=dim)
        cells = jnp.concatenate(
            [
                lax.ppermute(tail, axis, [(i, (i + 1) % count) for i in range(count)]),
                cells,
                lax.ppermute(head, axis, [((i + 1) % count, i) for i in range(count)]),
            ],
            axis=dim,
        )
    return cells


def shifted(array, axis, by):
    devices = lax.axis_size(axis)
    return lax.ppermute(array, axis, [(i, (i + by) % devices) for i in range(devices)])


def silu_slope(values):
    sigmoid_v = jax.nn.sigmoid(values)
    return sigmoid_v * (1.0 + values * (1.0 - sigmoid_v))


def mesh_mlp(node_rows, summed, w_self, w_agg, w_out):
    summed_b = summed.astype(jnp.bfloat16)
    pre_act = jnp.dot(node_rows, w_self, preferred_element_type=jnp.float32) + jnp.dot(
        summed_b, w_agg, preferred_element_type=jnp.float32
    )
    hidden = jax.nn.silu(pre_act).astype(jnp.bfloat16)
    result = (
        node_rows.astype(jnp.float32) + jnp.dot(hidden, w_out, preferred_element_type=jnp.float32)
    ).astype(jnp.bfloat16)
    return (pre_act, result)


def mlp_back(upper_grad, pre_act, w_agg, w_out):
    g_hidden = jnp.dot(upper_grad, w_out.T, preferred_element_type=jnp.float32).astype(jnp.bfloat16)
    g_hidden = lax.optimization_barrier(g_hidden).astype(jnp.float32)
    g_pre = (g_hidden * silu_slope(pre_act)).astype(jnp.bfloat16)
    g_summed = jnp.dot(g_pre, w_agg.T, preferred_element_type=jnp.float32).astype(jnp.bfloat16)
    return (g_pre, g_summed)


def place_sum(row_index, seg_count, values):
    picker = (jnp.arange(seg_count, dtype=jnp.int32)[:, None] == row_index[None, :]).astype(
        jnp.float32
    )
    flat_terms = values.reshape(values.shape[0], -1)
    return jnp.dot(
        picker, flat_terms, precision=lax.Precision.HIGHEST, preferred_element_type=jnp.float32
    )


def per_device(
    grid_latent,
    mesh_latent,
    mesh_cotangent,
    w_send,
    w_self_enc,
    w_agg_enc,
    w_out_enc,
    w_pass,
    w_self_proc,
    w_agg_proc,
    w_out_proc,
    enc_source,
    enc_part,
    enc_block,
    enc_mask,
    proc_source,
    proc_target,
    proc_mask,
):
    part_count = lax.axis_size("mesh")
    model_width = grid_latent.shape[1]
    block_size = enc_mask.shape[1]
    grid_blocks = grid_latent.shape[0] // block_size
    edge_count = enc_source.shape[0]
    mesh_blocks = mesh_latent.shape[0] // block_size
    capacity = 3 * edge_count // (2 * part_count)
    sent_rows = jnp.dot(grid_latent, w_send, preferred_element_type=jnp.float32).astype(
        jnp.bfloat16
    )
    sent_blocks = sent_rows.reshape(grid_blocks, block_size, model_width)
    enc_masks = enc_mask.astype(jnp.bfloat16)
    src_rows = jnp.take(sent_blocks, enc_source, axis=0)
    messages = jnp.einsum(
        "eij,eid->ejd", enc_masks, src_rows, preferred_element_type=jnp.float32
    ).astype(jnp.bfloat16)
    part_ids = enc_part[:, 0]
    part_hits = (part_ids[:, None] == jnp.arange(part_count, dtype=jnp.int32)[None, :]).astype(
        jnp.int32
    )
    slot_rank = jnp.sum((jnp.cumsum(part_hits, axis=0) - 1) * part_hits, axis=1)
    slot_index = part_ids * capacity + slot_rank
    outgoing = (
        jnp.zeros((part_count * capacity, block_size, model_width), jnp.bfloat16)
        .at[slot_index]
        .set(messages)
    )
    targets = jnp.zeros((part_count * capacity,), jnp.int32).at[slot_index].set(enc_block)
    arrived, arrived_blocks = (
        lax.all_to_all(
            outgoing.reshape(part_count, capacity, block_size, model_width),
            "mesh",
            split_axis=0,
            concat_axis=0,
            tiled=True,
        ),
        lax.all_to_all(
            targets.reshape(part_count, capacity), "mesh", split_axis=0, concat_axis=0, tiled=True
        ),
    )
    arrived_flat = arrived_blocks.reshape(part_count * capacity)
    picker = (jnp.arange(mesh_blocks, dtype=jnp.int32)[:, None] == arrived_flat[None, :]).astype(
        jnp.bfloat16
    )
    band_sum = jnp.dot(
        picker,
        arrived.reshape(part_count * capacity, block_size * model_width),
        preferred_element_type=jnp.float32,
    ).reshape(mesh_blocks * block_size, model_width)
    enc_sum = lax.psum(band_sum.astype(jnp.bfloat16), "grid").astype(jnp.float32)
    pre_enc, first = mesh_mlp(mesh_latent, enc_sum, w_self_enc, w_agg_enc, w_out_enc)
    passed_own = jnp.dot(first, w_pass, preferred_element_type=jnp.float32).astype(jnp.bfloat16)
    halo_width = passed_own.shape[0]
    extended = padded(passed_own, (("mesh", 0),), halo_width)
    ext_blocks = extended.reshape(3 * mesh_blocks, block_size, model_width)
    proc_masks = proc_mask.astype(jnp.bfloat16)
    proc_rows = jnp.take(ext_blocks, proc_source, axis=0)
    proc_messages = jnp.einsum(
        "eij,eid->ejd", proc_masks, proc_rows, preferred_element_type=jnp.float32
    )
    proc_band = place_sum(proc_target, mesh_blocks, proc_messages).reshape(
        mesh_blocks * block_size, model_width
    )
    proc_sum = lax.psum(proc_band.astype(jnp.bfloat16), "grid").astype(jnp.float32)
    pre_proc, out_own = mesh_mlp(first, proc_sum, w_self_proc, w_agg_proc, w_out_proc)
    g_pre_proc, g_agg_own = mlp_back(mesh_cotangent, pre_proc, w_agg_proc, w_out_proc)
    g_first_part = mesh_cotangent.astype(jnp.float32) + jnp.dot(
        g_pre_proc, w_self_proc.T, preferred_element_type=jnp.float32
    )
    g_blocks = g_agg_own.reshape(mesh_blocks, block_size, model_width)
    dst_rows = jnp.take(g_blocks, proc_target, axis=0)
    contrib = jnp.einsum("eij,ejd->eid", proc_masks, dst_rows, preferred_element_type=jnp.float32)
    spread = (
        place_sum(proc_source, 3 * mesh_blocks, contrib)
        .reshape(3, mesh_blocks * block_size, model_width)
        .astype(jnp.bfloat16)
    )
    spread = lax.optimization_barrier(spread)
    from_upper = shifted(spread[0], "mesh", -1)
    from_lower = shifted(spread[2], "mesh", 1)
    grad_local = (
        from_upper.astype(jnp.float32)
        + spread[1].astype(jnp.float32)
        + from_lower.astype(jnp.float32)
    )
    g_pass = lax.psum(grad_local.astype(jnp.bfloat16), "grid")
    g_first = (g_first_part + jnp.dot(g_pass, w_pass.T, preferred_element_type=jnp.float32)).astype(
        jnp.bfloat16
    )
    g_pre_enc, g_enc_own = mlp_back(g_first, pre_enc, w_agg_enc, w_out_enc)
    enc_table = g_enc_own.reshape(mesh_blocks, block_size, model_width)
    requested = jnp.take(enc_table, arrived_flat, axis=0).reshape(
        part_count, capacity, block_size, model_width
    )
    returned = lax.all_to_all(requested, "mesh", split_axis=0, concat_axis=0, tiled=True)
    wanted = jnp.take(
        returned.reshape(part_count * capacity, block_size, model_width), slot_index, axis=0
    )
    grid_terms = jnp.einsum("eij,ejd->eid", enc_masks, wanted, preferred_element_type=jnp.float32)
    grid_sum = place_sum(enc_source, grid_blocks, grid_terms).reshape(
        grid_blocks * block_size, model_width
    )
    grid_grad = jnp.dot(
        grid_sum.astype(jnp.bfloat16), w_send.T, preferred_element_type=jnp.float32
    ).astype(jnp.bfloat16)
    return (out_own, grid_grad)


def solution(mesh):
    return jax.shard_map(
        per_device,
        mesh=mesh,
        in_specs=(
            P(("grid", "mesh"), None),
            P("mesh", None),
            P("mesh", None),
            P(),
            P(),
            P(),
            P(),
            P(),
            P(),
            P(),
            P(),
            P(("grid", "mesh")),
            P(("grid", "mesh"), None),
            P(("grid", "mesh")),
            P(("grid", "mesh"), None, None),
            P(("grid", "mesh")),
            P(("grid", "mesh")),
            P(("grid", "mesh"), None, None),
        ),
        out_specs=(P("mesh", None), P(("grid", "mesh"), None)),
        check_vma=False,
    )
```

profile of v0, /device:TPU:117, one launch (start us, length us, event | category | flops | bytes accessed | tf_op | source)
XLA Modules:
  0.0 750.5 jit_solution(8814621482758195684)
XLA Ops:
  7.2 0.9 fusion.25
  8.1 0.8 select_reduce_fusion
  9.0 0.7 and_bitcast_fusion
  9.6 0.8 scatter_custom_fusion
  10.4 0.7 all_to_all.12
  11.1 6.7 all-to-all-start
  17.8 0.7 compare_and_fusion.3
  18.5 0.7 compare_select_fusion.4
  19.1 4.5 convolution_convert_fusion.5
  23.6 4.8 gather_fusion
  28.5 5.7 convert_bitcast_fusion
  34.2 6.6 copy.35
  40.8 3.4 broadcast_in_dim.73
  44.2 11.4 %scatter_fusion = bf16[48,128,512]{2,1,0:T(8,128)(2,1)} fusion(bf16[48,128,512]{2,1,0:T(8,128)(2,1)} %broadcast_in_dim.73, s32[32]{0:T(128)S(1)} %bitcast.100, bf16[32,128,512]{2,1,0:T(8,128)(2,1)} %copy.35), kind=kCustom, calls=%fused_computation.6 | custom fusion | bytes 12583040 | tf_op jit(solution)/shard_map/scatter | solution.py:108
  55.6 6.7 all-to-all-start.1
  62.8 0.7 reduce.5
  63.6 98.7 %all-to-all-done.1 = bf16[16,3,128,512]{3,2,1,0:T(8,128)(2,1)} async-done(((bf16[16,3,128,512]{3,2,1,0:T(8,128)(2,1)}), bf16[16,3,128,512]{3,2,1,0:T(8,128)(2,1)}, u32[]{:S(2)}, u32[]{:S(2)}) %all-to-all-start.1) | async-done | bytes 6291488 | tf_op jit(solution)/shard_map/all_to_all | solution.py:112
  162.3 6.5 copy.48
  168.9 0.9 convolution_convert_fusion.3
  169.8 2.0 convert_element_type.126
  172.1 4.8 fusion.40
  176.9 62.9 %all-reduce.4.cloned.1.call-done = bf16[2048,512]{1,0:T(8,128)(2,1)} async-done(((bf16[2048,512]{1,0:T(8,128)(2,1)}), bf16[2048,512]{1,0:T(8,128)(2,1)}) %all-reduce.4.cloned.1.call-update) | async-done | bytes 2097168 | tf_op jit(solution)/shard_map/psum | solution.py:132
  239.8 4.1 convolution_add_fusion.1
  244.0 1.6 add_convert_fusion.2
  245.9 1.3 convolution_convert_fusion.10
  247.5 1.2 collective-permute-start
  248.8 45.7 %collective-permute-done.1 = bf16[2048,512]{1,0:T(8,128)(2,1)S(1)} collective-permute-done((bf16[2048,512]{1,0:T(8,128)(2,1)S(1)}, bf16[2048,512]{1,0:T(8,128)(2,1)S(1)}, u32[]{:S(2)}, u32[]{:S(2)}) %collective-permute-start.1) | collective-permute-done | bytes 2097184 | tf_op jit(solution)/shard_map/ppermute | solution.py:16
  294.9 17.6 %pad_maximum_fusion = bf16[6144,512]{1,0:T(8,128)(2,1)} fusion(bf16[2048,512]{1,0:T(8,128)(2,1)S(1)} %collective-permute-done.1, bf16[2048,512]{1,0:T(8,128)(2,1)S(1)} %convolution_convert_fusion.10, bf16[2048,512]{1,0:T(8,128)(2,1)S(1)} %collective-permute-done), kind=kLoop, calls=%fused_computation.11 | loop fusion | flops 18874368 | bytes 12582912 | tf_op jit(solution)/shard_map/concatenate | solution.py:12
  312.5 3.6 gather_fusion.1
  316.0 2.8 convolution_bitcast_fusion.1
  318.8 5.6 copy.49
  324.4 4.3 convolution_convert_fusion.2
  328.7 2.0 convert_element_type.133
  330.7 8.2 %all-reduce.8.cloned.1.call-start = ((), (), s32[]{:S(2)}) async-start(), calls=%async_computation.5 | async-start | bytes 4194304 | tf_op jit(solution)/shard_map/psum | solution.py:168
  339.0 4.3 convolution_convert_fusion.9
  343.4 3.2 fusion.41
  346.6 52.7 %all-reduce.6.cloned.1.call-done = bf16[2048,512]{1,0:T(8,128)(2,1)} async-done(((bf16[2048,512]{1,0:T(8,128)(2,1)}), bf16[2048,512]{1,0:T(8,128)(2,1)}) %all-reduce.6.cloned.1.call-update) | async-done | bytes 2097168 | tf_op jit(solution)/shard_map/psum | solution.py:146
  399.3 8.0 %multiply_convert_fusion.1 = (bf16[2048,512]{1,0:T(8,128)(2,1)S(1)}, f32[2048,512]{1,0:T(8,128)}) fusion(bf16[2048,512]{1,0:T(8,128)(2,1)} %convolution_convert_fusion.9, f32[2048,512]{1,0:T(8,128)} %fusion.41, bf16[2048,512]{1,0:T(8,128)(2,1)} %all-reduce.6.cloned.1.call-done, bf16[512,512]{1,0:T(8,128)(2,1)} %param.27), kind=kOutput, calls=%fused_computation.22 | convolution fusion | flops 1085276160 | bytes 15204352 | tf_op jit(solution)/shard_map/dot_general | solution.py:35
  407.3 2.6 convolution_convert_fusion.8
  409.9 2.3 gather_fusion.2
  412.2 2.8 convolution_bitcast_fusion
  415.0 5.5 copy.50
  420.5 9.5 %convolution_convert_fusion = bf16[48,65536]{1,0:T(8,128)(2,1)} fusion(f32[16,65536]{1,0:T(8,128)} %bitcast.94, s32[16]{0:T(128)S(1)} %copy-done.19), kind=kOutput, calls=%fused_computation.7 | convolution fusion | flops 607126272 | bytes 10485824 | tf_op jit(solution)/shard_map/dot_general | solution.py:58
  429.9 8.1 %convert_element_type.142 = bf16[3,2048,512]{2,1,0:T(8,128)(2,1)} reshape(bf16[48,65536]{1,0:T(8,128)(2,1)} %convolution_convert_fusion) | data formatting | bytes 12582912 | tf_op jit(solution)/shard_map/convert_element_type | solution.py:158
  438.1 2.5 slice_bitcast_fusion.2
  440.9 1.4 collective-permute-start.3
  442.3 45.6 %collective-permute-done.2 = bf16[2048,512]{1,0:T(8,128)(2,1)S(1)} collective-permute-done((bf16[2048,512]{1,0:T(8,128)(2,1)S(1)}, bf16[2048,512]{1,0:T(8,128)(2,1)S(1)}, u32[]{:S(2)}, u32[]{:S(2)}) %collective-permute-start.2) | collective-permute-done | bytes 2097184 | tf_op jit(solution)/shard_map/ppermute | solution.py:25
  487.9 0.6 collective-permute-done.3
  488.4 3.9 fusion.1
  492.6 3.2 fusion.42
  495.9 65.0 %all-reduce.8.cloned.1.call-done = bf16[2048,512]{1,0:T(8,128)(2,1)} async-done(((bf16[2048,512]{1,0:T(8,128)(2,1)}), bf16[2048,512]{1,0:T(8,128)(2,1)}) %all-reduce.8.cloned.1.call-update) | async-done | bytes 2097168 | tf_op jit(solution)/shard_map/psum | solution.py:168
  560.9 7.4 convolution_convert_fusion.7
  568.3 4.7 convolution_convert_fusion.6
  573.1 4.9 gather_fusion.3
  578.0 6.1 broadcast_select_fusion
  584.1 7.3 all-to-all-start.2
  591.4 5.0 add_convert_fusion.1
  596.4 104.7 %all-to-all-done.2 = bf16[16,3,128,512]{3,2,1,0:T(8,128)(2,1)} async-done(((bf16[16,3,128,512]{3,2,1,0:T(8,128)(2,1)}), bf16[16,3,128,512]{3,2,1,0:T(8,128)(2,1)}, u32[]{:S(2)}, u32[]{:S(2)}) %all-to-all-start.2) | async-done | bytes 6291488 | tf_op jit(solution)/shard_map/all_to_all | solution.py:177
  701.1 5.7 gather_fusion.4
  706.9 6.9 fusion.8
  713.8 10.3 %copy.51 = f32[4,8,128,512]{3,1,2,0:T(8,128)} copy(f32[4,8,128,512]{2,3,1,0:T(8,128)} %bitcast.86) | data formatting | bytes 16777216
  724.1 8.7 %convolution_convert_fusion.1 = bf16[24,65536]{1,0:T(8,128)(2,1)} fusion(f32[32,65536]{1,0:T(8,128)} %bitcast.87, s32[32]{0:T(128)S(1)} %copy-done.18), kind=kOutput, calls=%fused_computation.8 | convolution fusion | flops 605553408 | bytes 11534464 | tf_op jit(solution)/shard_map/dot_general | solution.py:58
  732.8 5.3 convert_element_type.154
  738.1 5.5 convolution_convert_fusion.4
  (74 shorter events, 2.9 us)
Async XLA Ops:
  7.2 12.0 %copy-start = (bf16[3072,512]{1,0:T(8,128)(2,1)S(1)}, bf16[3072,512]{1,0:T(8,128)(2,1)}, u32[]{:S(2)}) copy-start(bf16[3072,512]{1,0:T(8,128)(2,1)} %param.18) | copy-start | bytes 9437188
  11.1 44.5 %all-to-all-start = ((s32[16,1,3]{2,1,0:T(1,128)}), s32[16,1,3]{2,1,0:T(1,128)S(1)}, u32[]{:S(2)}, u32[]{:S(2)}) async-start(s32[16,1,3]{2,1,0:T(1,128)} %bitcast.3), calls=%async_computation | async-start | bytes 16384 | tf_op jit(solution)/shard_map/all_to_all | solution.py:119
  23.6 4.9 copy-start.3
  55.6 106.7 %all-to-all-start.1 = ((bf16[16,3,128,512]{3,2,1,0:T(8,128)(2,1)}), bf16[16,3,128,512]{3,2,1,0:T(8,128)(2,1)}, u32[]{:S(2)}, u32[]{:S(2)}) async-start(bf16[16,3,128,512]{3,2,1,0:T(8,128)(2,1)} %bitcast.85), calls=%async_computation.1 | async-start | bytes 12582912 | tf_op jit(solution)/shard_map/all_to_all | solution.py:112
  62.3 177.5 %all-reduce.4.cloned.1.call-start = ((), (), s32[]{:S(2)}) async-start(), calls=%async_computation.3 | async-start | bytes 4194304 | tf_op jit(solution)/shard_map/psum | solution.py:132
  169.8 2.3 copy-start.14
  171.8 68.0 %copy-start.15 = (bf16[512,512]{1,0:T(8,128)(2,1)S(1)}, bf16[512,512]{1,0:T(8,128)(2,1)}, u32[]{:S(2)}) copy-start(bf16[512,512]{1,0:T(8,128)(2,1)} %param.23) | copy-start | bytes 1572868
  171.8 227.5 %all-reduce.6.cloned.1.call-start = ((), (), s32[]{:S(2)}) async-start(), calls=%async_computation.4 | async-start | bytes 4194304 | tf_op jit(solution)/shard_map/psum | solution.py:146
  176.9 67.0 %copy-start.8 = (bf16[2048,512]{1,0:T(8,128)(2,1)S(1)}, bf16[2048,512]{1,0:T(8,128)(2,1)}, u32[]{:S(2)}) copy-start(bf16[2048,512]{1,0:T(8,128)(2,1)} %param.19) | copy-start | bytes 6291460
  176.9 67.0 %copy-start.21 = (bf16[512,512]{1,0:T(8,128)(2,1)S(1)}, bf16[512,512]{1,0:T(8,128)(2,1)}, u32[]{:S(2)}) copy-start(bf16[512,512]{1,0:T(8,128)(2,1)} %param.24) | copy-start | bytes 1572868
  244.0 1.9 copy-start.2
  244.0 1.9 copy-start.22
  245.9 1.3 copy-start.9
  245.9 2.8 copy-start.19
  247.2 47.3 %collective-permute-start.1 = (bf16[2048,512]{1,0:T(8,128)(2,1)S(1)}, bf16[2048,512]{1,0:T(8,128)(2,1)S(1)}, u32[]{:S(2)}, u32[]{:S(2)}) collective-permute-start(bf16[2048,512]{1,0:T(8,128)(2,1)S(1)} %convolution_convert_fusion.10), channel_id=1, source_target_pairs={{1,0},{2,1},{3,2},{4,3},{5,4},{6,5},{7,6},{8,7},{9,8},{10,9},{11,1... | collective-permute-start | bytes 6291464 | tf_op jit(solution)/shard_map/ppermute | solution.py:16
  247.5 47.4 %collective-permute-start = (bf16[2048,512]{1,0:T(8,128)(2,1)S(1)}, bf16[2048,512]{1,0:T(8,128)(2,1)S(1)}, u32[]{:S(2)}, u32[]{:S(2)}) collective-permute-start(bf16[2048,512]{1,0:T(8,128)(2,1)S(1)} %convolution_convert_fusion.10), channel_id=1, source_target_pairs={{0,1},{1,2},{2,3},{3,4},{4,5},{5,6},{6,7},{7,8},{8,9},{9,10},{10,1... | collective-permute-start | bytes 6291464 | tf_op jit(solution)/shard_map/ppermute | solution.py:14
  312.5 3.6 copy-start.7
  318.8 5.6 copy-start.17
  330.7 12.6 %copy-start.10 = (bf16[2048,512]{1,0:T(8,128)(2,1)S(1)}, bf16[2048,512]{1,0:T(8,128)(2,1)}, u32[]{:S(2)}) copy-start(bf16[2048,512]{1,0:T(8,128)(2,1)} %copy-done.9) | copy-start | bytes 6291460
  330.7 230.2 %all-reduce.8.cloned.1.call-start = ((), (), s32[]{:S(2)}) async-start(), calls=%async_computation.5 | async-start | bytes 4194304 | tf_op jit(solution)/shard_map/psum | solution.py:168
  339.0 4.4 copy-start.12
  399.3 8.0 %copy-start.20 = (bf16[512,512]{1,0:T(8,128)(2,1)S(1)}, bf16[512,512]{1,0:T(8,128)(2,1)}, u32[]{:S(2)}) copy-start(bf16[512,512]{1,0:T(8,128)(2,1)} %param.27) | copy-start | bytes 1572868
  407.3 2.6 copy-start.5
  440.6 47.3 %collective-permute-start.2 = (bf16[2048,512]{1,0:T(8,128)(2,1)S(1)}, bf16[2048,512]{1,0:T(8,128)(2,1)S(1)}, u32[]{:S(2)}, u32[]{:S(2)}) collective-permute-start(bf16[2048,512]{1,0:T(8,128)(2,1)S(1)} %get-tuple-element.4), channel_id=1, source_target_pairs={{0,15},{1,0},{2,1},{3,2},{4,3},{5,4},{6,5},{7,6},{8,7},{9,8},{10,9... | collective-permute-start | bytes 6291464 | tf_op jit(solution)/shard_map/ppermute | solution.py:25
  440.9 51.7 %copy-start.6 = (bf16[2048,512]{1,0:T(8,128)(2,1)S(1)}, bf16[2048,512]{1,0:T(8,128)(2,1)}, u32[]{:S(2)}) copy-start(bf16[2048,512]{1,0:T(8,128)(2,1)} %copy-done.5) | copy-start | bytes 6291460
  440.9 51.7 %copy-start.13 = (bf16[512,512]{1,0:T(8,128)(2,1)S(1)}, bf16[512,512]{1,0:T(8,128)(2,1)}, u32[]{:S(2)}) copy-start(bf16[512,512]{1,0:T(8,128)(2,1)} %param.26) | copy-start | bytes 1572868
  440.9 47.5 %collective-permute-start.3 = (bf16[2048,512]{1,0:T(8,128)(2,1)S(1)}, bf16[2048,512]{1,0:T(8,128)(2,1)S(1)}, u32[]{:S(2)}, u32[]{:S(2)}) collective-permute-start(bf16[2048,512]{1,0:T(8,128)(2,1)S(1)} %get-tuple-element.5), channel_id=1, source_target_pairs={{0,1},{1,2},{2,3},{3,4},{4,5},{5,6},{6,7},{7,8},{8,9},{9,10},{10,1... | collective-permute-start | bytes 6291464 | tf_op jit(solution)/shard_map/ppermute | solution.py:25
  495.9 72.4 %copy-start.16 = (bf16[512,512]{1,0:T(8,128)(2,1)S(1)}, bf16[512,512]{1,0:T(8,128)(2,1)}, u32[]{:S(2)}) copy-start(bf16[512,512]{1,0:T(8,128)(2,1)} %param.23) | copy-start | bytes 1572868
  584.1 7.3 copy-start.11
  584.1 7.4 copy-start.23
  584.1 117.1 %all-to-all-start.2 = ((bf16[16,3,128,512]{3,2,1,0:T(8,128)(2,1)}), bf16[16,3,128,512]{3,2,1,0:T(8,128)(2,1)}, u32[]{:S(2)}, u32[]{:S(2)}) async-start(bf16[16,3,128,512]{3,2,1,0:T(8,128)(2,1)} %broadcast_select_fusion), calls=%async_computation.2 | async-start | bytes 12582912 | tf_op jit(solution)/shard_map/all_to_all | solution.py:177
  701.1 5.7 copy-start.4
  713.7 10.3 %copy-start.18 = (s32[32]{0:T(128)S(1)}, s32[32]{0:T(128)}, u32[]{:S(2)}) copy-start(s32[32]{0:T(128)} %param.29) | copy-start | bytes 388
  732.8 10.8 %copy-start.1 = (bf16[3072,512]{1,0:T(8,128)(2,1)S(1)}, bf16[3072,512]{1,0:T(8,128)(2,1)}, u32[]{:S(2)}) copy-start(bf16[3072,512]{1,0:T(8,128)(2,1)} %param.18) | copy-start | bytes 9437188
Sparse Core Ops, SparseCore 0:
  171.9 67.8 all-reduce.3
  330.8 68.3 all-reduce.5
  492.5 68.4 all-reduce.7
where the time goes:
time: 760 us; the launch traced here: 751 us
  waiting for transfers between devices  476 us (63%)
  matrix products  102 us (13%)
  local copies, waits for them, and re-layouts  93.3 us (12%)
  starting transfers between devices  32.4 us (4%)
  other arithmetic  32 us (4%)
  between operations  14.5 us (2%)
    all_to_all x1, waiting for transfers between devices, per_device(): lax.all_to_all(requested, 'mesh', split_axis=0, concat_axis=0, tiled=True)  105 us
    all_to_all x1, waiting for transfers between devices, per_device(): lax.all_to_all(outgoing.reshape(part_count, capacity, block_size, model_w...  98.7 us
    psum x1, waiting for transfers between devices, per_device(): g_pass = lax.psum(grad_local.astype(jnp.bfloat16), 'grid')  65 us
    psum x1, waiting for transfers between devices, per_device(): lax.psum(band_sum.astype(jnp.bfloat16), 'grid').astype(jnp.float32)  62.9 us
    psum x1, waiting for transfers between devices, per_device(): lax.psum(proc_band.astype(jnp.bfloat16), 'grid').astype(jnp.float32)  52.7 us
    ppermute x2, waiting for transfers between devices, shifted(): lax.ppermute(array, axis, [(i, (i + by) % devices) for i in range(devices)])  46.2 us
    ppermute x1, waiting for transfers between devices, padded(): lax.ppermute(head, axis, [((i + 1) % count, i) for i in range(count)])  45.7 us
    unnamed x52, local copies, waits for them, and re-layouts  28.4 us
  transfers between devices with their start and end apart: 10, of which 9 were waited for; matrix products, arithmetic and copies ran while one was open for 8% of the time, Pallas kernels for 0%

commit v1 on v0

v1 whole, which is shorter than its diff:
```python
import functools

import jax
import jax.numpy as jnp
from jax import lax
from jax.experimental import pallas as pl
from jax.experimental.pallas import tpu as pltpu
from jax.sharding import PartitionSpec as P

BF16 = jnp.bfloat16
F32 = jnp.float32
MIB = 1024 * 1024
SMEM = pl.BlockSpec(memory_space=pltpu.SMEM)
VMEM = pl.BlockSpec(memory_space=pltpu.VMEM)
PIECES = [(dz, dc) for dz in range(4) for dc in range(2)]


def over_z(array, by):
    return lax.ppermute(array, "grid", [(2 * z + c, 2 * ((z + by) % 4) + c) for z in range(4) for c in range(2)])


def over_column(array, dz, dc):
    return lax.ppermute(
        array, "grid", [(2 * z + c, 2 * ((z + dz) % 4) + (c ^ dc)) for z in range(4) for c in range(2)]
    )


def over_x(array, by):
    return lax.ppermute(array, "mesh", [(4 * x + y, 4 * ((x + by) % 4) + y) for x in range(4) for y in range(4)])


def over_y(array, by):
    return lax.ppermute(array, "mesh", [(4 * x + y, 4 * x + (y + by) % 4) for x in range(4) for y in range(4)])


def over_mesh(array, by):
    return lax.ppermute(array, "mesh", [(p, (p + by) % 16) for p in range(16)])


def local(body, outs, ins, smem=1, scratch=(), limit=24, cost=None):
    return pl.pallas_call(
        body,
        out_shape=[jax.ShapeDtypeStruct(shape, dtype) for shape, dtype in outs],
        in_specs=[SMEM] * smem + [VMEM] * (len(ins) - smem),
        out_specs=[VMEM] * len(outs),
        scratch_shapes=list(scratch),
        compiler_params=pltpu.CompilerParams(vmem_limit_bytes=limit * MIB),
    )(*ins)


def lanes(index):
    return pl.ds(pl.multiple_of((index & 3) * 128, 128), 128)


def dot(a, b):
    return jnp.dot(a, b, preferred_element_type=F32)


def dot_t(a, b):
    return lax.dot_general(a, b, (((1,), (1,)), ((), ())), preferred_element_type=F32)


def silu_slope(values):
    sigmoid_v = jax.nn.sigmoid(values)
    return sigmoid_v * (1.0 + values * (1.0 - sigmoid_v))


def messages_body(ids, source, latent, w_send, mask, *rest):
    outs, (sent, msg) = rest[:16], rest[16:]
    step = pl.program_id(0)
    z, c = ids[0], ids[1]

    @pl.when(step == 0)
    def _():
        def rows(i, _):
            at = pl.ds(pl.multiple_of(i * 256, 256), 256)
            sent[at, :] = dot(latent[at, :], w_send[...]).astype(BF16)
            return 0

        lax.fori_loop(0, 12, rows, 0)

    for k in range(4):
        block = source[step * 4 + k]
        rows = sent[pl.ds(pl.multiple_of(block * 128, 128), 128), :]
        weights = mask[k].astype(F32).astype(BF16)
        msg[k] = lax.dot_general(weights, rows, (((0,), (0,)), ((), ())), preferred_element_type=F32).astype(BF16)
        for h in range(2):
            for n, (dz, dc) in enumerate(PIECES):
                at = pl.ds(pl.multiple_of(64 * (c ^ dc) + 32 * h, 32), 32)
                outs[8 * h + n][k] = msg[k, at, lanes(z + dz)]


def send_messages(ids, source, latent, w_send, mask):
    whole = lambda i: (0, 0)
    return pl.pallas_call(
        messages_body,
        grid=(8,),
        out_shape=[jax.ShapeDtypeStruct((32, 32, 128), BF16)] * 16,
        in_specs=[
            SMEM,
            SMEM,
            pl.BlockSpec((3072, 512), whole, pipeline_mode=pl.Buffered(1)),
            pl.BlockSpec((512, 512), whole, pipeline_mode=pl.Buffered(1)),
            pl.BlockSpec((4, 128, 128), lambda i: (i, 0, 0)),
        ],
        out_specs=[pl.BlockSpec((4, 32, 128), lambda i: (i, 0, 0))] * 16,
        scratch_shapes=[pltpu.VMEM((3072, 512), BF16), pltpu.VMEM((4, 128, 512), BF16)],
        compiler_params=pltpu.CompilerParams(vmem_limit_bytes=24 * MIB),
    )(ids, source, latent, w_send, mask)


def combine_body(y_first, ids, meta, *rest):
    pieces, outs, acc = rest[:8], rest[8:12], rest[12]
    z, c, x, y = ids[0], ids[1], ids[2], ids[3]
    acc[...] = jnp.zeros_like(acc)
    for (dz, dc), piece in zip(PIECES, pieces):
        row = (2 * ((z - dz) & 3) + (c ^ dc)) * 64

        def add(e, _):
            slot = meta[row + e]
            acc[slot] += piece[e].astype(F32)
            return 0

        lax.fori_loop(0, 32, add, 0, unroll=4)
    for k in range(4):
        for j in range(4):
            kx, ky = (j, k) if y_first else (k, j)
            part = 4 * ((x + kx) & 3) + ((y + ky) & 3)
            outs[k][j] = acc[pl.ds(part * 16, 16)].astype(BF16)


def combine(y_first, ids, meta, pieces):
    return local(
        functools.partial(combine_body, y_first),
        [((4, 16, 32, 128), BF16)] * 4,
        [ids, meta, *pieces],
        smem=2,
        scratch=[pltpu.VMEM((256, 32, 128), F32)],
    )


def add_rows_body(a, b, c, d, *outs):
    for j in range(4):
        outs[j][...] = (
            a[j].astype(F32) + b[j].astype(F32) + c[j].astype(F32) + d[j].astype(F32)
        ).astype(BF16)


def add_rows(parts):
    return local(add_rows_body, [((16, 32, 128), BF16)] * 4, parts, smem=0)


def add_last_body(ids, *rest):
    halves, outs, acc = (rest[:4], rest[4:8]), rest[8:12], rest[12]
    z = ids[0]
    for h, half in enumerate(halves):
        total = half[0][...].astype(F32)
        for more in half[1:]:
            total += more[...].astype(F32)
        acc[:, 32 * h : 32 * h + 32, :] = total.astype(BF16)
    for k in range(4):
        outs[k][...] = acc[pl.ds(4 * ((z + k) & 3), 4)]


def add_last(ids, first_half, second_half):
    return local(
        add_last_body,
        [((4, 64, 128), BF16)] * 4,
        [ids, *first_half, *second_half],
        scratch=[pltpu.VMEM((16, 64, 128), BF16)],
    )


def to_rows(z, pieces, wide):
    for k in range(4):
        wide[:, lanes(z - k)] = pieces[k][...].reshape(256, 128)
    return wide[...]


def from_rows(z, wide, outs):
    for k in range(4):
        outs[k][...] = wide[:, lanes(z + k)].reshape(4, 64, 128)


def enc_mlp_body(ids, p0, p1, p2, p3, pre_self, rows, w_agg, w_out, w_pass, pre_ref, first_ref, *rest):
    outs, wide = rest[:4], rest[4]
    z = ids[0]
    summed = to_rows(z, (p0, p1, p2, p3), wide)
    pre = pre_self[...] + dot(summed, w_agg[...])
    pre_ref[...] = pre
    hidden = jax.nn.silu(pre).astype(BF16)
    first = (rows[...].astype(F32) + dot(hidden, w_out[...])).astype(BF16)
    first_ref[...] = first
    wide[...] = dot(first, w_pass[...]).astype(BF16)
    from_rows(z, wide, outs)


def proc_mlp_body(ids, p0, p1, p2, p3, pre_self, rows, g_hidden, w_agg, w_out, out_ref, g_pre_ref, *rest):
    outs, wide = rest[:4], rest[4]
    z = ids[0]
    summed = to_rows(z, (p0, p1, p2, p3), wide)
    pre = pre_self[...] + dot(summed, w_agg[...])
    g_pre = (g_hidden[...].astype(F32) * silu_slope(pre)).astype(BF16)
    g_pre_ref[...] = g_pre
    wide[...] = dot_t(g_pre, w_agg[...]).astype(BF16)
    from_rows(z, wide, outs)
    hidden = jax.nn.silu(pre).astype(BF16)
    out_ref[...] = (rows[...].astype(F32) + dot(hidden, w_out[...])).astype(BF16)


def enc_back_body(ids, p0, p1, p2, p3, g_part, pre, w_pass, w_out, w_agg, *rest):
    outs, wide = rest[:4], rest[4]
    z = ids[0]
    g_pass = to_rows(z, (p0, p1, p2, p3), wide)
    g_first = (g_part[...] + dot_t(g_pass, w_pass[...])).astype(BF16)
    g_hidden = dot_t(g_first, w_out[...]).astype(BF16)
    g_pre = (g_hidden.astype(F32) * silu_slope(pre[...])).astype(BF16)
    wide[...] = dot_t(g_pre, w_agg[...]).astype(BF16)
    from_rows(z, wide, outs)


ROWS = ((256, 512), BF16)
ROWS32 = ((256, 512), F32)
PIECE = ((4, 64, 128), BF16)
WIDE = pltpu.VMEM((256, 512), BF16)


def table_body(ids, p0, p1, p2, p3, out):
    for k, piece in enumerate((p0, p1, p2, p3)):
        out[pl.ds(4 * ((ids[0] - k) & 3), 4)] = piece[...]


def table(ids, pieces):
    return local(table_body, [((16, 64, 128), BF16)], [ids, *pieces])[0]


def halves_body(ids, p0, p1, p2, p3, low, high):
    for k, piece in enumerate((p0, p1, p2, p3)):
        at = pl.ds(4 * ((ids[0] - k) & 3), 4)
        low[at] = piece[:, :32, :]
        high[at] = piece[:, 32:, :]


def halves(ids, pieces):
    return local(halves_body, [((16, 32, 128), BF16)] * 2, [ids, *pieces])


def spread_z(pieces):
    return [pieces[0]] + [over_z(pieces[k], k) for k in (1, 2, 3)]


def edge_loop(c, meta, one):
    def band(n, _):
        row = (2 * (n >> 2) + c) * 64 + (n & 3) * 4
        one(n * 4, [(meta[row + 32 + e], meta[row + 48 + e]) for e in range(4)])
        return 0

    lax.fori_loop(0, 16, band, 0)


def proc_body(ids, meta, masks, *rest):
    tables, (own, other, ext, acc) = rest[:6], rest[6:]
    c = ids[1]
    at_own = pl.ds(pl.multiple_of(64 * c, 64), 64)
    at_other = pl.ds(pl.multiple_of(64 * (1 - c), 64), 64)
    for k in range(3):
        ext[16 * k : 16 * k + 16, at_own, :] = tables[2 * k][...]
        ext[16 * k : 16 * k + 16, at_other, :] = tables[2 * k + 1][...]
    acc[...] = jnp.zeros_like(acc)

    def one(base, edges):
        terms = [dot(masks[base + e], ext[source]) for e, (source, _) in enumerate(edges)]
        for term, (_, target) in zip(terms, edges):
            acc[target] += term

    edge_loop(c, meta, one)
    own[...] = acc[:, at_own, :]
    other[...] = acc[:, at_other, :].astype(BF16)


def proc_back_body(ids, meta, masks, mine, theirs, own, other, grads, acc):
    c = ids[1]
    at_own = pl.ds(pl.multiple_of(64 * c, 64), 64)
    at_other = pl.ds(pl.multiple_of(64 * (1 - c), 64), 64)
    grads[:, at_own, :] = mine[...]
    grads[:, at_other, :] = theirs[...]
    acc[...] = jnp.zeros_like(acc)

    def one(base, edges):
        terms = [dot(masks[base + e], grads[target]) for e, (_, target) in enumerate(edges)]
        for term, (source, _) in zip(terms, edges):
            acc[source] += term

    edge_loop(c, meta, one)
    own[...] = acc[:, at_own, :]
    other[...] = acc[:, at_other, :].astype(BF16)


def pair_sum_body(ids, own, other, *outs):
    for k in range(4):
        at = pl.ds(4 * ((ids[0] + k) & 3), 4)
        outs[k][...] = (own[at] + other[at].astype(F32)).astype(BF16)


def part_sum_body(own, other, *outs):
    for k in range(3):
        at = slice(16 * k, 16 * k + 16)
        outs[k][...] = (own[at] + other[at].astype(F32)).astype(BF16)


def three_sum_body(ids, a, b, c, *outs):
    for k in range(4):
        at = pl.ds(4 * ((ids[0] + k) & 3), 4)
        outs[k][...] = (a[at].astype(F32) + b[at].astype(F32) + c[at].astype(F32)).astype(BF16)


def fetch_body(y_first, ids, meta, t0, t1, t2, t3, *rest):
    outs, tab = rest[:8], rest[8]
    z, c, x, y = ids[0], ids[1], ids[2], ids[3]
    for k, part in enumerate((t0, t1, t2, t3)):
        tab[64 * k : 64 * k + 64] = part[...].reshape(64, 32, 128)
    for (dz, dc), out in zip(PIECES, outs):
        row = (2 * ((z + dz) & 3) + (c ^ dc)) * 64

        def take(e, _):
            slot = meta[row + e]
            kx = (x - (slot >> 6)) & 3
            ky = (y - ((slot >> 4) & 3)) & 3
            at = (kx * 4 + ky) if y_first else (ky * 4 + kx)
            out[e] = tab[at * 16 + (slot & 15)]
            return 0

        lax.fori_loop(0, 32, take, 0, unroll=4)


def fetch(y_first, ids, meta, tables):
    return local(
        functools.partial(fetch_body, y_first),
        [((32, 32, 128), BF16)] * 8,
        [ids, meta, *tables],
        smem=2,
        scratch=[pltpu.VMEM((256, 32, 128), BF16)],
    )


def grid_body(ids, source, w_send, mask, *rest):
    pieces, (out, acc, wide) = rest[:16], rest[16:]
    step = pl.program_id(0)
    z, c = ids[0], ids[1]

    @pl.when(step == 0)
    def _():
        acc[...] = jnp.zeros_like(acc)

    for k in range(4):
        for h in range(2):
            for n, (dz, dc) in enumerate(PIECES):
                at = pl.ds(pl.multiple_of(64 * (c ^ dc) + 32 * h, 32), 32)
                wide[k, at, lanes(z - dz)] = pieces[8 * h + n][k]
        at = pl.ds(pl.multiple_of(source[step * 4 + k] * 128, 128), 128)
        acc[at, :] += dot(mask[k].astype(F32).astype(BF16), wide[k])

    @pl.when(step == 7)
    def _():
        def rows(i, _):
            at = pl.ds(pl.multiple_of(i * 256, 256), 256)
            out[at, :] = dot_t(acc[at, :].astype(BF16), w_send[...]).astype(BF16)
            return 0

        lax.fori_loop(0, 12, rows, 0)


def grid_gradient(ids, source, w_send, mask, pieces):
    whole = lambda i: (0, 0)
    return pl.pallas_call(
        grid_body,
        grid=(8,),
        out_shape=jax.ShapeDtypeStruct((3072, 512), BF16),
        in_specs=[
            SMEM,
            SMEM,
            pl.BlockSpec((512, 512), whole, pipeline_mode=pl.Buffered(1)),
            pl.BlockSpec((4, 128, 128), lambda i: (i, 0, 0)),
        ]
        + [pl.BlockSpec((4, 32, 128), lambda i: (i, 0, 0))] * 16,
        out_specs=pl.BlockSpec((3072, 512), whole),
        scratch_shapes=[pltpu.VMEM((3072, 512), F32), pltpu.VMEM((4, 128, 512), BF16)],
        compiler_params=pltpu.CompilerParams(vmem_limit_bytes=32 * MIB),
    )(ids, source, w_send, mask, *pieces)


def column_exchange(pieces):
    return [pieces[0]] + [over_column(pieces[n], dz, dc) for n, (dz, dc) in enumerate(PIECES) if n]


def own_rows(array, z, c):
    cut = lax.dynamic_slice(array.reshape(4, 4, 2, 64, 512), (z, 0, c, 0, 0), (1, 4, 1, 64, 512))
    return cut.reshape(256, 512)


def per_device(
    grid_latent,
    mesh_latent,
    mesh_cotangent,
    w_send,
    w_self_enc,
    w_agg_enc,
    w_out_enc,
    w_pass,
    w_self_proc,
    w_agg_proc,
    w_out_proc,
    enc_source,
    enc_part,
    enc_block,
    enc_mask,
    proc_source,
    proc_target,
    proc_mask,
):
    g, p = lax.axis_index("grid"), lax.axis_index("mesh")
    z, c = g // 2, g % 2
    ids = jnp.stack([z, c, p // 4, p % 4]).astype(jnp.int32)
    slots = enc_part[:, 0] * 16 + enc_block
    meta = lax.all_gather(jnp.concatenate([slots, proc_source, proc_target]), "grid", axis=0, tiled=True)

    messages = send_messages(ids, enc_source, grid_latent, w_send, enc_mask)
    arrived = column_exchange(messages[:8])
    masks = lax.all_gather(
        proc_mask.astype(BF16),
        "grid",
        axis=0,
        tiled=True,
        axis_index_groups=[[2 * i + j for i in range(4)] for j in range(2)],
    )
    masks_t = jnp.swapaxes(masks, 1, 2)
    second, arrived = lax.optimization_barrier((tuple(messages[8:]), tuple(arrived)))
    arrived_2 = column_exchange(second)
    a = combine(True, ids, meta, arrived)
    a = add_rows([a[0]] + [over_y(a[k], k) for k in (1, 2, 3)])
    a = [a[0]] + [over_x(a[k], k) for k in (1, 2, 3)]
    b = combine(False, ids, meta, arrived_2)
    b = add_rows([b[0]] + [over_x(b[k], k) for k in (1, 2, 3)])
    b = [b[0]] + [over_y(b[k], k) for k in (1, 2, 3)]
    summed = spread_z(add_last(ids, a, b))

    rows = own_rows(mesh_latent, z, c)
    cotangent = own_rows(mesh_cotangent, z, c)
    pre_self = dot(rows, w_self_enc)
    g_hid_proc = lax.dot_general(
        cotangent, w_out_proc, (((1,), (1,)), ((), ())), preferred_element_type=F32
    ).astype(BF16)
    pre_enc, first, *passed = local(
        enc_mlp_body,
        [ROWS32, ROWS] + [PIECE] * 4,
        [ids, *summed, pre_self, rows, w_agg_enc, w_out_enc, w_pass],
        scratch=[WIDE],
    )

    own = table(ids, spread_z(passed))
    tables = [over_mesh(own, 1), own, over_mesh(own, -1)]
    both = []
    for one in tables:
        both += [one, over_column(one, 0, 1)]
    mine, theirs = local(
        proc_body,
        [((16, 64, 128), F32), ((16, 64, 128), BF16)],
        [ids, meta, masks_t, *both],
        smem=2,
        scratch=[pltpu.VMEM((48, 128, 128), BF16), pltpu.VMEM((16, 128, 128), F32)],
    )
    summed = local(pair_sum_body, [PIECE] * 4, [ids, mine, over_column(theirs, 0, 1)])
    pre_self_proc = dot(first, w_self_proc)
    out_rows, g_pre_proc, *g_agg = local(
        proc_mlp_body,
        [ROWS, ROWS] + [PIECE] * 4,
        [ids, *spread_z(summed), pre_self_proc, first, g_hid_proc, w_agg_proc, w_out_proc],
        scratch=[WIDE],
    )
    mesh_out = lax.all_gather(out_rows.reshape(1, 4, 64, 512), "grid", axis=0, tiled=True)
    mesh_out = jnp.swapaxes(mesh_out.reshape(4, 2, 4, 64, 512), 1, 2).reshape(2048, 512)

    g_first_part = cotangent.astype(F32) + dot_t(g_pre_proc, w_self_proc)
    own = table(ids, spread_z(g_agg))
    mine, theirs = local(
        proc_back_body,
        [((48, 64, 128), F32), ((48, 64, 128), BF16)],
        [ids, meta, masks, own, over_column(own, 0, 1)],
        smem=2,
        scratch=[pltpu.VMEM((16, 128, 128), BF16), pltpu.VMEM((48, 128, 128), F32)],
    )
    parts = local(part_sum_body, [((16, 64, 128), BF16)] * 3, [mine, over_column(theirs, 0, 1)], smem=0)
    g_pass = local(
        three_sum_body, [PIECE] * 4, [ids, over_mesh(parts[0], -1), parts[1], over_mesh(parts[2], 1)]
    )
    g_agg = local(
        enc_back_body,
        [PIECE] * 4,
        [ids, *spread_z(g_pass), g_first_part, pre_enc, w_pass, w_out_enc, w_agg_enc],
        scratch=[WIDE],
    )

    a, b = halves(ids, spread_z(g_agg))
    a = jnp.stack([a] + [over_x(a, k) for k in (1, 2, 3)])
    a = fetch(False, ids, meta, [a] + [over_y(a, k) for k in (1, 2, 3)])
    back = column_exchange(a)
    b = jnp.stack([b] + [over_y(b, k) for k in (1, 2, 3)])
    b = fetch(True, ids, meta, [b] + [over_x(b, k) for k in (1, 2, 3)])
    b, back = lax.optimization_barrier((tuple(b), tuple(back)))
    back_2 = column_exchange(b)
    grid_grad = grid_gradient(ids, enc_source, w_send, enc_mask, [*back, *back_2])
    return (mesh_out, grid_grad)


def solution(mesh):
    return jax.shard_map(
        per_device,
        mesh=mesh,
        in_specs=(
            P(("grid", "mesh"), None),
            P("mesh", None),
            P("mesh", None),
            P(),
            P(),
            P(),
            P(),
            P(),
            P(),
            P(),
            P(),
            P(("grid", "mesh")),
            P(("grid", "mesh"), None),
            P(("grid", "mesh")),
            P(("grid", "mesh"), None, None),
            P(("grid", "mesh")),
            P(("grid", "mesh")),
            P(("grid", "mesh"), None, None),
        ),
        out_specs=(P("mesh", None), P(("grid", "mesh"), None)),
        check_vma=False,
    )
```

time: 760 us -> 412 us (0.54)
  the two profiles are of different devices: /device:TPU:117 before, /device:TPU:1 now
where the time goes in v1:
time: 412 us; the launch traced here: 406 us
  waiting for transfers between devices  155 us (38%)
  starting transfers between devices  145 us (35%)
  Pallas kernels  47.7 us (12%)
  local copies, waits for them, and re-layouts  32.4 us (8%)
  between operations  15.5 us (4%)
  blocking collectives  4.66 us (1%)
    ppermute x34, waiting for transfers between devices, over_column(): lax.ppermute(array, 'grid', [(2 * z + c, 2 * ((z + dz) % 4) + (c ^ dc)) f...  81.7 us
    ppermute x34, starting transfers between devices, over_column(): lax.ppermute(array, 'grid', [(2 * z + c, 2 * ((z + dz) % 4) + (c ^ dc)) f...  70 us
    ppermute x18, starting transfers between devices, over_z(): lax.ppermute(array, 'grid', [(2 * z + c, 2 * ((z + by) % 4) + c) for z in...  31.3 us
    ppermute x12, waiting for transfers between devices, over_y(): lax.ppermute(array, 'mesh', [(4 * x + y, 4 * x + (y + by) % 4) for x in r...  29.4 us
    pallas_call x18, Pallas kernels, local(): pl.pallas_call(body, out_shape=[jax.ShapeDtypeStruct(shape, dtype) for sh...  29.3 us
    unnamed x114, local copies, waits for them, and re-layouts  24.9 us
    ppermute x12, waiting for transfers between devices, over_x(): lax.ppermute(array, 'mesh', [(4 * x + y, 4 * ((x + by) % 4) + y) for x in...  18.1 us
    ppermute x12, starting transfers between devices, over_x(): lax.ppermute(array, 'mesh', [(4 * x + y, 4 * ((x + by) % 4) + y) for x in...  16 us
  transfers between devices with their start and end apart: 82, of which 47 were waited for; matrix products, arithmetic and copies ran while one was open for 2% of the time, Pallas kernels for 10%

profile of v1, /device:TPU:1, one launch (start us, length us, event | category | flops | bytes accessed | tf_op | source)
XLA Modules:
  0.0 405.5 jit_solution(16727837707624643506)
XLA Ops:
  7.2 2.3 convert_element_type.9
  13.2 8.6 %shard_map.185 = (bf16[32,32,128]{2,1,0:T(8,128)(2,1)S(1)}, bf16[32,32,128]{2,1,0:T(8,128)(2,1)S(1)}, bf16[32,32,128]{2,1,0:T(8,128)(2,1)S(1)}, bf16[32,32,128]{...) custom-call(s32[4]{0:T(128)S(1)} %pad_add_fusion.ids, ...), custom_call_target="tpu_custom_call" | custom-call | tf_op jit(solution)/shard_map/pallas_call | solution.py:95
  34.7 7.7 %collective-permute-done.1.rest_2_ = bf16[32,32,128]{2,1,0:T(8,128)(2,1)S(1)} collective-permute-done((bf16[32,32,128]{2,1,0:T(8,128)(2,1)S(1)}, bf16[32,32,128]{2,1,0:T(8,128)(2,1)S(1)}, u32[]{:S(2)}, u32[]{:S(2)}) %collective-permute-start.1) | collective-permute-done | bytes 262176 | tf_op jit(solution)/shard_map/ppermute | solution.py:23
  43.1 2.1 collective-permute-start.6
  45.3 8.6 %collective-permute-done.2.rest_3_ = bf16[32,32,128]{2,1,0:T(8,128)(2,1)S(1)} collective-permute-done((bf16[32,32,128]{2,1,0:T(8,128)(2,1)S(1)}, bf16[32,32,128]{2,1,0:T(8,128)(2,1)S(1)}, u32[]{:S(2)}, u32[]{:S(2)}) %collective-permute-start.2) | collective-permute-done | bytes 262176 | tf_op jit(solution)/shard_map/ppermute | solution.py:23
  54.5 6.8 %collective-permute-done.3.rest_4_ = bf16[32,32,128]{2,1,0:T(8,128)(2,1)S(1)} collective-permute-done((bf16[32,32,128]{2,1,0:T(8,128)(2,1)S(1)}, bf16[32,32,128]{2,1,0:T(8,128)(2,1)S(1)}, u32[]{:S(2)}, u32[]{:S(2)}) %collective-permute-start.3) | collective-permute-done | bytes 262176 | tf_op jit(solution)/shard_map/ppermute | solution.py:23
  62.1 4.9 %collective-permute-done.4.rest_5_ = bf16[32,32,128]{2,1,0:T(8,128)(2,1)S(1)} collective-permute-done((bf16[32,32,128]{2,1,0:T(8,128)(2,1)S(1)}, bf16[32,32,128]{2,1,0:T(8,128)(2,1)S(1)}, u32[]{:S(2)}, u32[]{:S(2)}) %collective-permute-start.4) | collective-permute-done | bytes 262176 | tf_op jit(solution)/shard_map/ppermute | solution.py:23
  71.0 4.7 %all-reduce.meta = s32[512]{0:T(512)S(1)} all-reduce(s32[512]{0:T(512)S(1)} %add_dynamic-update-slice_fusion), channel_id=1, replica_groups=mesh['grid'=8,'mesh'=16] {'grid'}, use_global_device_ids=true, to_apply=%add | all-reduce | flops 512 | bytes 4096
  76.0 4.0 collective-permute-start.15
  86.7 2.2 shard_map.186
  95.7 4.0 collective-permute-done.16.rest_4_
  99.7 2.4 collective-permute-start.8
  102.1 2.5 collective-permute-done.17.rest_5_
  106.1 3.5 collective-permute-done.18.rest_6_
  109.6 5.9 %collective-permute-done.19.rest_7_ = bf16[32,32,128]{2,1,0:T(8,128)(2,1)S(1)} collective-permute-done((bf16[32,32,128]{2,1,0:T(8,128)(2,1)S(1)}, bf16[32,32,128]{2,1,0:T(8,128)(2,1)S(1)}, u32[]{:S(2)}, u32[]{:S(2)}) %collective-permute-start.19) | collective-permute-done | bytes 262176 | tf_op jit(solution)/shard_map/ppermute | solution.py:23
  115.5 2.2 shard_map.188
  119.0 2.4 collective-permute-start.21
  122.6 2.7 collective-permute-done.9.d
  127.4 2.4 collective-permute-start.11
  129.8 2.7 collective-permute-done.20.b
  133.7 11.0 %collective-permute-done.21.c = bf16[4,16,32,128]{3,2,1,0:T(8,128)(2,1)S(1)} collective-permute-done((bf16[4,16,32,128]{3,2,1,0:T(8,128)(2,1)S(1)}, bf16[4,16,32,128]{3,2,1,0:T(8,128)(2,1)S(1)}, u32[]{:S(2)}, u32[]{:S(2)}) %collective-permute-start.21) | collective-permute-done | bytes 524320 | tf_op jit(solution)/shard_map/ppermute | solution.py:29
  148.9 2.1 collective-permute-start.25
  151.6 2.6 collective-permute-done.24.rest_6_
  166.2 2.9 collective-permute-start.30
  175.2 6.6 %collective-permute-start.35 = (bf16[16,64,128]{2,1,0:T(8,128)(2,1)}, bf16[16,64,128]{2,1,0:T(8,128)(2,1)}, u32[]{:S(2)}, u32[]{:S(2)}) collective-permute-start(bf16[16,64,128]{2,1,0:T(8,128)(2,1)} %shard_map.192.rest_2_), channel_id=1, source_target_pairs={{0,15},{1,0},{2,1},{3,2},{4,3},{5,4},{6,5},{7,6},{8,7},{9,8},{10,9... | collective-permute-start | bytes 786440 | tf_op jit(solution)/shard_map/ppermute | solution.py:37
  181.8 3.8 collective-permute-start.34
  185.8 4.4 %collective-permute-start.33 = (bf16[16,64,128]{2,1,0:T(8,128)(2,1)}, bf16[16,64,128]{2,1,0:T(8,128)(2,1)}, u32[]{:S(2)}, u32[]{:S(2)}) collective-permute-start(bf16[16,64,128]{2,1,0:T(8,128)(2,1)} %collective-permute-done.32.rest_0_), channel_id=1, source_target_pairs={{0,16},{16,0},{32,48},{48,32},{64,80},{80,64},{96,112},{112,96},{1... | collective-permute-start | bytes 786440 | tf_op jit(solution)/shard_map/ppermute | solution.py:23
  190.3 3.2 copy.24
  193.6 4.6 %shard_map.193 = (f32[16,64,128]{2,1,0:T(8,128)S(1)}, bf16[16,64,128]{2,1,0:T(8,128)(2,1)S(1)}) custom-call(s32[4]{0:T(128)S(1)} %pad_add_fusion.ids, s32[512]{0:T(512)S(1)} %all-reduce.meta, bf16[64,128,128]{2,1,0:T(8,128)(2,1)S(1)} %bitcast.38, bf16[16,64,128]{2,1,0:T(8,128)(2,1)} %collective-permute-done.32.rest_0_, ...), custom_call_target="tpu_custom_call" | custom-call | tf_op jit(solution)/shard_map/pallas_call | solution.py:41
  200.8 2.4 collective-permute-start.39
  207.2 2.1 shard_map.195
  211.1 2.9 collective-permute-start.42
  224.8 4.0 shard_map.197
  229.3 2.3 collective-permute-done.45.other
  231.7 4.8 %collective-permute-start.46 = (bf16[16,64,128]{2,1,0:T(8,128)(2,1)S(1)}, bf16[16,64,128]{2,1,0:T(8,128)(2,1)S(1)}, u32[]{:S(2)}, u32[]{:S(2)}) collective-permute-start(bf16[16,64,128]{2,1,0:T(8,128)(2,1)S(1)} %get-tuple-element.189), channel_id=1, source_target_pairs={{0,15},{1,0},{2,1},{3,2},{4,3},{5,4},{6,5},{7,6},{8,7},{9,8},{10,9... | collective-permute-start | bytes 786440 | tf_op jit(solution)/shard_map/ppermute | solution.py:37
  236.6 5.3 %collective-permute-done.46.a = bf16[16,64,128]{2,1,0:T(8,128)(2,1)S(1)} collective-permute-done((bf16[16,64,128]{2,1,0:T(8,128)(2,1)S(1)}, bf16[16,64,128]{2,1,0:T(8,128)(2,1)S(1)}, u32[]{:S(2)}, u32[]{:S(2)}) %collective-permute-start.46) | collective-permute-done | bytes 262176 | tf_op jit(solution)/shard_map/ppermute | solution.py:37
  241.9 5.2 %collective-permute-done.47.c = bf16[16,64,128]{2,1,0:T(8,128)(2,1)S(1)} collective-permute-done((bf16[16,64,128]{2,1,0:T(8,128)(2,1)S(1)}, bf16[16,64,128]{2,1,0:T(8,128)(2,1)S(1)}, u32[]{:S(2)}, u32[]{:S(2)}) %collective-permute-start.47) | collective-permute-done | bytes 262176 | tf_op jit(solution)/shard_map/ppermute | solution.py:37
  247.8 2.1 collective-permute-start.49
  249.9 9.8 %collective-permute-start.50 = (bf16[4,64,128]{2,1,0:T(8,128)(2,1)S(1)}, bf16[4,64,128]{2,1,0:T(8,128)(2,1)S(1)}, u32[]{:S(2)}, u32[]{:S(2)}) collective-permute-start(bf16[4,64,128]{2,1,0:T(8,128)(2,1)S(1)} %get-tuple-element.195), channel_id=1, source_target_pairs={{0,96},{16,112},{32,0},{48,16},{64,32},{80,48},{96,64},{112,80},{1... | collective-permute-start | bytes 196616 | tf_op jit(solution)/shard_map/ppermute | solution.py:19
  264.6 2.1 collective-permute-start.52
  270.7 2.4 collective-permute-start.62
  273.1 3.8 collective-permute-done.60
  277.7 3.8 collective-permute-start.64
  282.8 11.4 %collective-permute-done.54 = bf16[16,32,128]{2,1,0:T(8,128)(2,1)S(1)} collective-permute-done((bf16[16,32,128]{2,1,0:T(8,128)(2,1)S(1)}, bf16[16,32,128]{2,1,0:T(8,128)(2,1)S(1)}, u32[]{:S(2)}, u32[]{:S(2)}) %collective-permute-start.54) | collective-permute-done | bytes 131104 | tf_op jit(solution)/shard_map/ppermute | solution.py:33
  294.2 5.7 %collective-permute-done.55 = bf16[16,32,128]{2,1,0:T(8,128)(2,1)S(1)} collective-permute-done((bf16[16,32,128]{2,1,0:T(8,128)(2,1)S(1)}, bf16[16,32,128]{2,1,0:T(8,128)(2,1)S(1)}, u32[]{:S(2)}, u32[]{:S(2)}) %collective-permute-start.55) | collective-permute-done | bytes 131104 | tf_op jit(solution)/shard_map/ppermute | solution.py:33
  299.9 5.9 %collective-permute-done.56 = bf16[16,32,128]{2,1,0:T(8,128)(2,1)S(1)} collective-permute-done((bf16[16,32,128]{2,1,0:T(8,128)(2,1)S(1)}, bf16[16,32,128]{2,1,0:T(8,128)(2,1)S(1)}, u32[]{:S(2)}, u32[]{:S(2)}) %collective-permute-start.56) | collective-permute-done | bytes 131104 | tf_op jit(solution)/shard_map/ppermute | solution.py:33
  305.9 3.2 collective-permute-start.58
  309.4 2.2 shard_map.203
  311.7 9.7 %collective-permute-start.66 = (bf16[32,32,128]{2,1,0:T(8,128)(2,1)S(1)}, bf16[32,32,128]{2,1,0:T(8,128)(2,1)S(1)}, u32[]{:S(2)}, u32[]{:S(2)}) collective-permute-start(bf16[32,32,128]{2,1,0:T(8,128)(2,1)S(1)} %get-tuple-element.213), channel_id=1, source_target_pairs={{0,16},{16,0},{32,48},{48,32},{64,80},{80,64},{96,112},{112,96},{1... | collective-permute-start | bytes 786440 | tf_op jit(solution)/shard_map/ppermute | solution.py:23
  321.6 6.4 %collective-permute-start.68 = (bf16[32,32,128]{2,1,0:T(8,128)(2,1)S(1)}, bf16[32,32,128]{2,1,0:T(8,128)(2,1)S(1)}, u32[]{:S(2)}, u32[]{:S(2)}) collective-permute-start(bf16[32,32,128]{2,1,0:T(8,128)(2,1)S(1)} %get-tuple-element.215), channel_id=1, source_target_pairs={{0,48},{16,32},{32,80},{48,64},{64,112},{80,96},{96,16},{112,0},{1... | collective-permute-start | bytes 786440 | tf_op jit(solution)/shard_map/ppermute | solution.py:23
  327.9 2.7 collective-permute-start.69
  330.6 5.7 %collective-permute-start.70 = (bf16[32,32,128]{2,1,0:T(8,128)(2,1)S(1)}, bf16[32,32,128]{2,1,0:T(8,128)(2,1)S(1)}, u32[]{:S(2)}, u32[]{:S(2)}) collective-permute-start(bf16[32,32,128]{2,1,0:T(8,128)(2,1)S(1)} %get-tuple-element.217), channel_id=1, source_target_pairs={{0,80},{16,64},{32,112},{48,96},{64,16},{80,0},{96,48},{112,32},{1... | collective-permute-start | bytes 786440 | tf_op jit(solution)/shard_map/ppermute | solution.py:23
  338.3 2.3 shard_map.202
  340.9 6.7 %collective-permute-done.70.rest_5_ = bf16[32,32,128]{2,1,0:T(8,128)(2,1)S(1)} collective-permute-done((bf16[32,32,128]{2,1,0:T(8,128)(2,1)S(1)}, bf16[32,32,128]{2,1,0:T(8,128)(2,1)S(1)}, u32[]{:S(2)}, u32[]{:S(2)}) %collective-permute-start.70) | collective-permute-done | bytes 262176 | tf_op jit(solution)/shard_map/ppermute | solution.py:23
  347.6 3.0 collective-permute-done.71.rest_6_
  350.6 6.3 %collective-permute-done.72.rest_7_ = bf16[32,32,128]{2,1,0:T(8,128)(2,1)S(1)} collective-permute-done((bf16[32,32,128]{2,1,0:T(8,128)(2,1)S(1)}, bf16[32,32,128]{2,1,0:T(8,128)(2,1)S(1)}, u32[]{:S(2)}, u32[]{:S(2)}) %collective-permute-start.72) | collective-permute-done | bytes 262176 | tf_op jit(solution)/shard_map/ppermute | solution.py:23
  358.7 2.7 collective-permute-start.76
  362.0 2.6 collective-permute-start.78
  366.2 2.7 collective-permute-start.79
  368.9 3.2 collective-permute-done.75.rest_11_
  372.1 6.7 %collective-permute-done.76.rest_12_ = bf16[32,32,128]{2,1,0:T(8,128)(2,1)S(1)} collective-permute-done((bf16[32,32,128]{2,1,0:T(8,128)(2,1)S(1)}, bf16[32,32,128]{2,1,0:T(8,128)(2,1)S(1)}, u32[]{:S(2)}, u32[]{:S(2)}) %collective-permute-start.76) | collective-permute-done | bytes 262176 | tf_op jit(solution)/shard_map/ppermute | solution.py:23
  378.8 5.7 %collective-permute-done.77.rest_13_ = bf16[32,32,128]{2,1,0:T(8,128)(2,1)S(1)} collective-permute-done((bf16[32,32,128]{2,1,0:T(8,128)(2,1)S(1)}, bf16[32,32,128]{2,1,0:T(8,128)(2,1)S(1)}, u32[]{:S(2)}, u32[]{:S(2)}) %collective-permute-start.77) | collective-permute-done | bytes 262176 | tf_op jit(solution)/shard_map/ppermute | solution.py:23
  385.4 9.9 %shard_map.204 = bf16[3072,512]{1,0:T(8,128)(2,1)} custom-call(s32[4]{0:T(128)S(1)} %pad_add_fusion.ids, s32[32]{0:T(128)S(1)} %copy-done.36, bf16[512,512]{1,0:T(8,128)(2,1)S(1)} %copy-done.6, s32[32,128,128]{2,1,0:T(8,128)S(1)} %copy-done.3, bf16[32,32,128]{2,1,0:T(8,128)(2,1)S(1)} %get-tuple-element.220.rest_0_, ...), custom_call_target="tpu_custom_call" | custom-call | tf_op jit(solution)/shard_map/pallas_call | solution.py:375
  395.2 3.3 copy.27
  (251 shorter events, 105.3 us)
Async XLA Ops:
  7.2 183.1 %all-gather.3.cloned.1.call-start = ((), (), s32[]{:S(2)}) async-start(), calls=%async_computation | async-start | bytes 2621440 | tf_op jit(solution)/shard_map/all_gather | solution.py:429
  9.6 385.7 %all-gather.5.cloned.1.call-start = ((), (), s32[]{:S(2)}) async-start(), calls=%async_computation.1 | async-start | bytes 2359296 | tf_op jit(solution)/shard_map/all_gather | solution.py:480
  24.7 8.3 %collective-permute-start = (bf16[32,32,128]{2,1,0:T(8,128)(2,1)S(1)}, bf16[32,32,128]{2,1,0:T(8,128)(2,1)S(1)}, u32[]{:S(2)}, u32[]{:S(2)}) collective-permute-start(bf16[32,32,128]{2,1,0:T(8,128)(2,1)S(1)} %get-tuple-element.128), channel_id=1, source_target_pairs={{0,16},{16,0},{32,48},{48,32},{64,80},{80,64},{96,112},{112,96},{1... | collective-permute-start | bytes 786440 | tf_op jit(solution)/shard_map/ppermute | solution.py:23
  26.1 16.3 %collective-permute-start.1 = (bf16[32,32,128]{2,1,0:T(8,128)(2,1)S(1)}, bf16[32,32,128]{2,1,0:T(8,128)(2,1)S(1)}, u32[]{:S(2)}, u32[]{:S(2)}) collective-permute-start(bf16[32,32,128]{2,1,0:T(8,128)(2,1)S(1)} %get-tuple-element.129), channel_id=1, source_target_pairs={{0,32},{16,48},{32,64},{48,80},{64,96},{80,112},{96,0},{112,16},{1... | collective-permute-start | bytes 786440 | tf_op jit(solution)/shard_map/ppermute | solution.py:23
  27.8 26.0 %collective-permute-start.2 = (bf16[32,32,128]{2,1,0:T(8,128)(2,1)S(1)}, bf16[32,32,128]{2,1,0:T(8,128)(2,1)S(1)}, u32[]{:S(2)}, u32[]{:S(2)}) collective-permute-start(bf16[32,32,128]{2,1,0:T(8,128)(2,1)S(1)} %get-tuple-element.130), channel_id=1, source_target_pairs={{0,48},{16,32},{32,80},{48,64},{64,112},{80,96},{96,16},{112,0},{1... | collective-permute-start | bytes 786440 | tf_op jit(solution)/shard_map/ppermute | solution.py:23
  29.6 31.7 %collective-permute-start.3 = (bf16[32,32,128]{2,1,0:T(8,128)(2,1)S(1)}, bf16[32,32,128]{2,1,0:T(8,128)(2,1)S(1)}, u32[]{:S(2)}, u32[]{:S(2)}) collective-permute-start(bf16[32,32,128]{2,1,0:T(8,128)(2,1)S(1)} %get-tuple-element.131), channel_id=1, source_target_pairs={{0,64},{16,80},{32,96},{48,112},{64,0},{80,16},{96,32},{112,48},{1... | collective-permute-start | bytes 786440 | tf_op jit(solution)/shard_map/ppermute | solution.py:23
  31.1 35.8 %collective-permute-start.4 = (bf16[32,32,128]{2,1,0:T(8,128)(2,1)S(1)}, bf16[32,32,128]{2,1,0:T(8,128)(2,1)S(1)}, u32[]{:S(2)}, u32[]{:S(2)}) collective-permute-start(bf16[32,32,128]{2,1,0:T(8,128)(2,1)S(1)} %get-tuple-element.132), channel_id=1, source_target_pairs={{0,80},{16,64},{32,112},{48,96},{64,16},{80,0},{96,48},{112,32},{1... | collective-permute-start | bytes 786440 | tf_op jit(solution)/shard_map/ppermute | solution.py:23
  33.7 34.0 %collective-permute-start.5 = (bf16[32,32,128]{2,1,0:T(8,128)(2,1)S(1)}, bf16[32,32,128]{2,1,0:T(8,128)(2,1)S(1)}, u32[]{:S(2)}, u32[]{:S(2)}) collective-permute-start(bf16[32,32,128]{2,1,0:T(8,128)(2,1)S(1)} %get-tuple-element.133), channel_id=1, source_target_pairs={{0,96},{16,112},{32,0},{48,16},{64,32},{80,48},{96,64},{112,80},{1... | collective-permute-start | bytes 786440 | tf_op jit(solution)/shard_map/ppermute | solution.py:23
  43.1 25.2 %collective-permute-start.6 = (bf16[32,32,128]{2,1,0:T(8,128)(2,1)S(1)}, bf16[32,32,128]{2,1,0:T(8,128)(2,1)S(1)}, u32[]{:S(2)}, u32[]{:S(2)}) collective-permute-start(bf16[32,32,128]{2,1,0:T(8,128)(2,1)S(1)} %get-tuple-element.134), channel_id=1, source_target_pairs={{0,112},{16,96},{32,16},{48,0},{64,48},{80,32},{96,80},{112,64},{1... | collective-permute-start | bytes 786440 | tf_op jit(solution)/shard_map/ppermute | solution.py:23
  69.1 22.7 %collective-permute-start.13 = (bf16[32,32,128]{2,1,0:T(8,128)(2,1)}, bf16[32,32,128]{2,1,0:T(8,128)(2,1)S(1)}, u32[]{:S(2)}, u32[]{:S(2)}) collective-permute-start(bf16[32,32,128]{2,1,0:T(8,128)(2,1)} %get-tuple-element.152), channel_id=1, source_target_pairs={{0,16},{16,0},{32,48},{48,32},{64,80},{80,64},{96,112},{112,96},{1... | collective-permute-start | bytes 786440 | tf_op jit(solution)/shard_map/ppermute | solution.py:23
  75.6 16.8 %collective-permute-start.14 = (bf16[32,32,128]{2,1,0:T(8,128)(2,1)}, bf16[32,32,128]{2,1,0:T(8,128)(2,1)S(1)}, u32[]{:S(2)}, u32[]{:S(2)}) collective-permute-start(bf16[32,32,128]{2,1,0:T(8,128)(2,1)} %copy-done.46), channel_id=1, source_target_pairs={{0,32},{16,48},{32,64},{48,80},{64,96},{80,112},{96,0},{112,16},{1... | collective-permute-start | bytes 786440 | tf_op jit(solution)/shard_map/ppermute | solution.py:23
  76.0 18.2 %collective-permute-start.15 = (bf16[32,32,128]{2,1,0:T(8,128)(2,1)}, bf16[32,32,128]{2,1,0:T(8,128)(2,1)S(1)}, u32[]{:S(2)}, u32[]{:S(2)}) collective-permute-start(bf16[32,32,128]{2,1,0:T(8,128)(2,1)} %copy-done.45), channel_id=1, source_target_pairs={{0,48},{16,32},{32,80},{48,64},{64,112},{80,96},{96,16},{112,0},{1... | collective-permute-start | bytes 786440 | tf_op jit(solution)/shard_map/ppermute | solution.py:23
  88.9 32.4 %collective-permute-start.7 = (bf16[4,16,32,128]{3,2,1,0:T(8,128)(2,1)S(1)}, bf16[4,16,32,128]{3,2,1,0:T(8,128)(2,1)S(1)}, u32[]{:S(2)}, u32[]{:S(2)}) collective-permute-start(bf16[4,16,32,128]{3,2,1,0:T(8,128)(2,1)S(1)} %get-tuple-element.144), channel_id=1, source_target_pairs={{0,1},{1,2},{2,3},{3,0},{4,5},{5,6},{6,7},{7,4},{8,9},{9,10},{10,1... | collective-permute-start | bytes 1572872 | tf_op jit(solution)/shard_map/ppermute | solution.py:33
  90.2 9.5 %collective-permute-start.16 = (bf16[32,32,128]{2,1,0:T(8,128)(2,1)S(1)}, bf16[32,32,128]{2,1,0:T(8,128)(2,1)S(1)}, u32[]{:S(2)}, u32[]{:S(2)}) collective-permute-start(bf16[32,32,128]{2,1,0:T(8,128)(2,1)S(1)} %copy-done.44), channel_id=1, source_target_pairs={{0,64},{16,80},{32,96},{48,112},{64,0},{80,16},{96,32},{112,48},{1... | collective-permute-start | bytes 786440 | tf_op jit(solution)/shard_map/ppermute | solution.py:23
  91.8 12.8 %collective-permute-start.17 = (bf16[32,32,128]{2,1,0:T(8,128)(2,1)S(1)}, bf16[32,32,128]{2,1,0:T(8,128)(2,1)S(1)}, u32[]{:S(2)}, u32[]{:S(2)}) collective-permute-start(bf16[32,32,128]{2,1,0:T(8,128)(2,1)S(1)} %copy-done.42), channel_id=1, source_target_pairs={{0,80},{16,64},{32,112},{48,96},{64,16},{80,0},{96,48},{112,32},{1... | collective-permute-start | bytes 786440 | tf_op jit(solution)/shard_map/ppermute | solution.py:23
  92.4 17.1 %collective-permute-start.18 = (bf16[32,32,128]{2,1,0:T(8,128)(2,1)S(1)}, bf16[32,32,128]{2,1,0:T(8,128)(2,1)S(1)}, u32[]{:S(2)}, u32[]{:S(2)}) collective-permute-start(bf16[32,32,128]{2,1,0:T(8,128)(2,1)S(1)} %copy-done.40), channel_id=1, source_target_pairs={{0,96},{16,112},{32,0},{48,16},{64,32},{80,48},{96,64},{112,80},{1... | collective-permute-start | bytes 786440 | tf_op jit(solution)/shard_map/ppermute | solution.py:23
  94.2 21.3 %collective-permute-start.19 = (bf16[32,32,128]{2,1,0:T(8,128)(2,1)S(1)}, bf16[32,32,128]{2,1,0:T(8,128)(2,1)S(1)}, u32[]{:S(2)}, u32[]{:S(2)}) collective-permute-start(bf16[32,32,128]{2,1,0:T(8,128)(2,1)S(1)} %copy-done.38), channel_id=1, source_target_pairs={{0,112},{16,96},{32,16},{48,0},{64,48},{80,32},{96,80},{112,64},{1... | collective-permute-start | bytes 786440 | tf_op jit(solution)/shard_map/ppermute | solution.py:23
  99.7 22.9 %collective-permute-start.8 = (bf16[4,16,32,128]{3,2,1,0:T(8,128)(2,1)S(1)}, bf16[4,16,32,128]{3,2,1,0:T(8,128)(2,1)S(1)}, u32[]{:S(2)}, u32[]{:S(2)}) collective-permute-start(bf16[4,16,32,128]{3,2,1,0:T(8,128)(2,1)S(1)} %get-tuple-element.145), channel_id=1, source_target_pairs={{0,2},{1,3},{2,0},{3,1},{4,6},{5,7},{6,4},{7,5},{8,10},{9,11},{10,... | collective-permute-start | bytes 1572872 | tf_op jit(solution)/shard_map/ppermute | solution.py:33
  104.6 20.7 %collective-permute-start.9 = (bf16[4,16,32,128]{3,2,1,0:T(8,128)(2,1)S(1)}, bf16[4,16,32,128]{3,2,1,0:T(8,128)(2,1)S(1)}, u32[]{:S(2)}, u32[]{:S(2)}) collective-permute-start(bf16[4,16,32,128]{3,2,1,0:T(8,128)(2,1)S(1)} %get-tuple-element.146), channel_id=1, source_target_pairs={{0,3},{1,0},{2,1},{3,2},{4,7},{5,4},{6,5},{7,6},{8,11},{9,8},{10,9... | collective-permute-start | bytes 1572872 | tf_op jit(solution)/shard_map/ppermute | solution.py:33
  117.7 14.8 %collective-permute-start.20 = (bf16[4,16,32,128]{3,2,1,0:T(8,128)(2,1)S(1)}, bf16[4,16,32,128]{3,2,1,0:T(8,128)(2,1)S(1)}, u32[]{:S(2)}, u32[]{:S(2)}) collective-permute-start(bf16[4,16,32,128]{3,2,1,0:T(8,128)(2,1)S(1)} %get-tuple-element.160), channel_id=1, source_target_pairs={{0,4},{1,5},{2,6},{3,7},{4,8},{5,9},{6,10},{7,11},{8,12},{9,13},{1... | collective-permute-start | bytes 1572872 | tf_op jit(solution)/shard_map/ppermute | solution.py:29
  119.0 25.7 %collective-permute-start.21 = (bf16[4,16,32,128]{3,2,1,0:T(8,128)(2,1)S(1)}, bf16[4,16,32,128]{3,2,1,0:T(8,128)(2,1)S(1)}, u32[]{:S(2)}, u32[]{:S(2)}) collective-permute-start(bf16[4,16,32,128]{3,2,1,0:T(8,128)(2,1)S(1)} %get-tuple-element.161), channel_id=1, source_target_pairs={{0,8},{1,9},{2,10},{3,11},{4,12},{5,13},{6,14},{7,15},{8,0},{9,1},... | collective-permute-start | bytes 1572872 | tf_op jit(solution)/shard_map/ppermute | solution.py:29
  121.4 23.3 %collective-permute-start.22 = (bf16[4,16,32,128]{3,2,1,0:T(8,128)(2,1)S(1)}, bf16[4,16,32,128]{3,2,1,0:T(8,128)(2,1)S(1)}, u32[]{:S(2)}, u32[]{:S(2)}) collective-permute-start(bf16[4,16,32,128]{3,2,1,0:T(8,128)(2,1)S(1)} %get-tuple-element.162), channel_id=1, source_target_pairs={{0,12},{1,13},{2,14},{3,15},{4,0},{5,1},{6,2},{7,3},{8,4},{9,5},{1... | collective-permute-start | bytes 1572872 | tf_op jit(solution)/shard_map/ppermute | solution.py:29
  126.2 22.7 %collective-permute-start.10 = (bf16[16,32,128]{2,1,0:T(8,128)(2,1)S(1)}, bf16[16,32,128]{2,1,0:T(8,128)(2,1)S(1)}, u32[]{:S(2)}, u32[]{:S(2)}) collective-permute-start(bf16[16,32,128]{2,1,0:T(8,128)(2,1)S(1)} %get-tuple-element.148), channel_id=1, source_target_pairs={{0,4},{1,5},{2,6},{3,7},{4,8},{5,9},{6,10},{7,11},{8,12},{9,13},{1... | collective-permute-start | bytes 393224 | tf_op jit(solution)/shard_map/ppermute | solution.py:29
  127.4 23.6 %collective-permute-start.11 = (bf16[16,32,128]{2,1,0:T(8,128)(2,1)}, bf16[16,32,128]{2,1,0:T(8,128)(2,1)S(1)}, u32[]{:S(2)}, u32[]{:S(2)}) collective-permute-start(bf16[16,32,128]{2,1,0:T(8,128)(2,1)} %get-tuple-element.149), channel_id=1, source_target_pairs={{0,8},{1,9},{2,10},{3,11},{4,12},{5,13},{6,14},{7,15},{8,0},{9,1},... | collective-permute-start | bytes 393224 | tf_op jit(solution)/shard_map/ppermute | solution.py:29
  132.5 18.6 %collective-permute-start.12 = (bf16[16,32,128]{2,1,0:T(8,128)(2,1)}, bf16[16,32,128]{2,1,0:T(8,128)(2,1)}, u32[]{:S(2)}, u32[]{:S(2)}) collective-permute-start(bf16[16,32,128]{2,1,0:T(8,128)(2,1)} %get-tuple-element.150), channel_id=1, source_target_pairs={{0,12},{1,13},{2,14},{3,15},{4,0},{5,1},{6,2},{7,3},{8,4},{9,5},{1... | collective-permute-start | bytes 393224 | tf_op jit(solution)/shard_map/ppermute | solution.py:29
  146.2 5.3 %collective-permute-start.23 = (bf16[16,32,128]{2,1,0:T(8,128)(2,1)}, bf16[16,32,128]{2,1,0:T(8,128)(2,1)}, u32[]{:S(2)}, u32[]{:S(2)}) collective-permute-start(bf16[16,32,128]{2,1,0:T(8,128)(2,1)} %get-tuple-element.164), channel_id=1, source_target_pairs={{0,1},{1,2},{2,3},{3,0},{4,5},{5,6},{6,7},{7,4},{8,9},{9,10},{10,1... | collective-permute-start | bytes 393224 | tf_op jit(solution)/shard_map/ppermute | solution.py:33
  147.4 6.7 %collective-permute-start.24 = (bf16[16,32,128]{2,1,0:T(8,128)(2,1)}, bf16[16,32,128]{2,1,0:T(8,128)(2,1)}, u32[]{:S(2)}, u32[]{:S(2)}) collective-permute-start(bf16[16,32,128]{2,1,0:T(8,128)(2,1)} %get-tuple-element.165), channel_id=1, source_target_pairs={{0,2},{1,3},{2,0},{3,1},{4,6},{5,7},{6,4},{7,5},{8,10},{9,11},{10,... | collective-permute-start | bytes 393224 | tf_op jit(solution)/shard_map/ppermute | solution.py:33
  148.9 5.8 %collective-permute-start.25 = (bf16[16,32,128]{2,1,0:T(8,128)(2,1)}, bf16[16,32,128]{2,1,0:T(8,128)(2,1)}, u32[]{:S(2)}, u32[]{:S(2)}) collective-permute-start(bf16[16,32,128]{2,1,0:T(8,128)(2,1)} %get-tuple-element.166), channel_id=1, source_target_pairs={{0,3},{1,0},{2,1},{3,2},{4,7},{5,4},{6,5},{7,6},{8,11},{9,8},{10,9... | collective-permute-start | bytes 393224 | tf_op jit(solution)/shard_map/ppermute | solution.py:33
  156.9 5.9 %collective-permute-start.26 = (bf16[4,64,128]{2,1,0:T(8,128)(2,1)S(1)}, bf16[4,64,128]{2,1,0:T(8,128)(2,1)S(1)}, u32[]{:S(2)}, u32[]{:S(2)}) collective-permute-start(bf16[4,64,128]{2,1,0:T(8,128)(2,1)S(1)} %get-tuple-element.168), channel_id=1, source_target_pairs={{0,32},{16,48},{32,64},{48,80},{64,96},{80,112},{96,0},{112,16},{1... | collective-permute-start | bytes 196616 | tf_op jit(solution)/shard_map/ppermute | solution.py:19
  173.5 12.3 %collective-permute-start.32 = (bf16[16,64,128]{2,1,0:T(8,128)(2,1)}, bf16[16,64,128]{2,1,0:T(8,128)(2,1)}, u32[]{:S(2)}, u32[]{:S(2)}) collective-permute-start(bf16[16,64,128]{2,1,0:T(8,128)(2,1)} %shard_map.192.rest_2_), channel_id=1, source_target_pairs={{0,1},{1,2},{2,3},{3,4},{4,5},{5,6},{6,7},{7,8},{8,9},{9,10},{10,1... | collective-permute-start | bytes 786440 | tf_op jit(solution)/shard_map/ppermute | solution.py:37
  175.2 15.1 %collective-permute-start.35 = (bf16[16,64,128]{2,1,0:T(8,128)(2,1)}, bf16[16,64,128]{2,1,0:T(8,128)(2,1)}, u32[]{:S(2)}, u32[]{:S(2)}) collective-permute-start(bf16[16,64,128]{2,1,0:T(8,128)(2,1)} %shard_map.192.rest_2_), channel_id=1, source_target_pairs={{0,15},{1,0},{2,1},{3,2},{4,3},{5,4},{6,5},{7,6},{8,7},{9,8},{10,9... | collective-permute-start | bytes 786440 | tf_op jit(solution)/shard_map/ppermute | solution.py:37
  181.8 11.8 %collective-permute-start.34 = (bf16[16,64,128]{2,1,0:T(8,128)(2,1)}, bf16[16,64,128]{2,1,0:T(8,128)(2,1)}, u32[]{:S(2)}, u32[]{:S(2)}) collective-permute-start(bf16[16,64,128]{2,1,0:T(8,128)(2,1)} %shard_map.192.rest_2_), channel_id=1, source_target_pairs={{0,16},{16,0},{32,48},{48,32},{64,80},{80,64},{96,112},{112,96},{1... | collective-permute-start | bytes 786440 | tf_op jit(solution)/shard_map/ppermute | solution.py:23
  185.8 7.7 %collective-permute-start.33 = (bf16[16,64,128]{2,1,0:T(8,128)(2,1)}, bf16[16,64,128]{2,1,0:T(8,128)(2,1)}, u32[]{:S(2)}, u32[]{:S(2)}) collective-permute-start(bf16[16,64,128]{2,1,0:T(8,128)(2,1)} %collective-permute-done.32.rest_0_), channel_id=1, source_target_pairs={{0,16},{16,0},{32,48},{48,32},{64,80},{80,64},{96,112},{112,96},{1... | collective-permute-start | bytes 786440 | tf_op jit(solution)/shard_map/ppermute | solution.py:23
  200.8 5.9 %collective-permute-start.39 = (bf16[4,64,128]{2,1,0:T(8,128)(2,1)S(1)}, bf16[4,64,128]{2,1,0:T(8,128)(2,1)S(1)}, u32[]{:S(2)}, u32[]{:S(2)}) collective-permute-start(bf16[4,64,128]{2,1,0:T(8,128)(2,1)S(1)} %get-tuple-element.179), channel_id=1, source_target_pairs={{0,64},{16,80},{32,96},{48,112},{64,0},{80,16},{96,32},{112,48},{1... | collective-permute-start | bytes 196616 | tf_op jit(solution)/shard_map/ppermute | solution.py:19
  231.7 10.1 %collective-permute-start.46 = (bf16[16,64,128]{2,1,0:T(8,128)(2,1)S(1)}, bf16[16,64,128]{2,1,0:T(8,128)(2,1)S(1)}, u32[]{:S(2)}, u32[]{:S(2)}) collective-permute-start(bf16[16,64,128]{2,1,0:T(8,128)(2,1)S(1)} %get-tuple-element.189), channel_id=1, source_target_pairs={{0,15},{1,0},{2,1},{3,2},{4,3},{5,4},{6,5},{7,6},{8,7},{9,8},{10,9... | collective-permute-start | bytes 786440 | tf_op jit(solution)/shard_map/ppermute | solution.py:37
  236.6 10.5 %collective-permute-start.47 = (bf16[16,64,128]{2,1,0:T(8,128)(2,1)S(1)}, bf16[16,64,128]{2,1,0:T(8,128)(2,1)S(1)}, u32[]{:S(2)}, u32[]{:S(2)}) collective-permute-start(bf16[16,64,128]{2,1,0:T(8,128)(2,1)S(1)} %get-tuple-element.191), channel_id=1, source_target_pairs={{0,1},{1,2},{2,3},{3,4},{4,5},{5,6},{6,7},{7,8},{8,9},{9,10},{10,1... | collective-permute-start | bytes 786440 | tf_op jit(solution)/shard_map/ppermute | solution.py:37
  247.7 12.3 %collective-permute-start.48 = (bf16[4,64,128]{2,1,0:T(8,128)(2,1)S(1)}, bf16[4,64,128]{2,1,0:T(8,128)(2,1)S(1)}, u32[]{:S(2)}, u32[]{:S(2)}) collective-permute-start(bf16[4,64,128]{2,1,0:T(8,128)(2,1)S(1)} %get-tuple-element.193), channel_id=1, source_target_pairs={{0,32},{16,48},{32,64},{48,80},{64,96},{80,112},{96,0},{112,16},{1... | collective-permute-start | bytes 196616 | tf_op jit(solution)/shard_map/ppermute | solution.py:19
  247.8 12.2 %collective-permute-start.49 = (bf16[4,64,128]{2,1,0:T(8,128)(2,1)S(1)}, bf16[4,64,128]{2,1,0:T(8,128)(2,1)S(1)}, u32[]{:S(2)}, u32[]{:S(2)}) collective-permute-start(bf16[4,64,128]{2,1,0:T(8,128)(2,1)S(1)} %get-tuple-element.194), channel_id=1, source_target_pairs={{0,64},{16,80},{32,96},{48,112},{64,0},{80,16},{96,32},{112,48},{1... | collective-permute-start | bytes 196616 | tf_op jit(solution)/shard_map/ppermute | solution.py:19
  249.9 12.1 %collective-permute-start.50 = (bf16[4,64,128]{2,1,0:T(8,128)(2,1)S(1)}, bf16[4,64,128]{2,1,0:T(8,128)(2,1)S(1)}, u32[]{:S(2)}, u32[]{:S(2)}) collective-permute-start(bf16[4,64,128]{2,1,0:T(8,128)(2,1)S(1)} %get-tuple-element.195), channel_id=1, source_target_pairs={{0,96},{16,112},{32,0},{48,16},{64,32},{80,48},{96,64},{112,80},{1... | collective-permute-start | bytes 196616 | tf_op jit(solution)/shard_map/ppermute | solution.py:19
  270.4 6.5 %collective-permute-start.60 = (bf16[16,32,128]{2,1,0:T(8,128)(2,1)S(1)}, bf16[16,32,128]{2,1,0:T(8,128)(2,1)S(1)}, u32[]{:S(2)}, u32[]{:S(2)}) collective-permute-start(bf16[16,32,128]{2,1,0:T(8,128)(2,1)S(1)} %get-tuple-element.211), channel_id=1, source_target_pairs={{0,4},{1,5},{2,6},{3,7},{4,8},{5,9},{6,10},{7,11},{8,12},{9,13},{1... | collective-permute-start | bytes 393224 | tf_op jit(solution)/shard_map/ppermute | solution.py:29
  270.4 6.4 %collective-permute-start.61 = (bf16[16,32,128]{2,1,0:T(8,128)(2,1)S(1)}, bf16[16,32,128]{2,1,0:T(8,128)(2,1)S(1)}, u32[]{:S(2)}, u32[]{:S(2)}) collective-permute-start(bf16[16,32,128]{2,1,0:T(8,128)(2,1)S(1)} %get-tuple-element.211), channel_id=1, source_target_pairs={{0,8},{1,9},{2,10},{3,11},{4,12},{5,13},{6,14},{7,15},{8,0},{9,1},... | collective-permute-start | bytes 393224 | tf_op jit(solution)/shard_map/ppermute | solution.py:29
  270.7 6.8 %collective-permute-start.62 = (bf16[16,32,128]{2,1,0:T(8,128)(2,1)S(1)}, bf16[16,32,128]{2,1,0:T(8,128)(2,1)S(1)}, u32[]{:S(2)}, u32[]{:S(2)}) collective-permute-start(bf16[16,32,128]{2,1,0:T(8,128)(2,1)S(1)} %get-tuple-element.211), channel_id=1, source_target_pairs={{0,12},{1,13},{2,14},{3,15},{4,0},{5,1},{6,2},{7,3},{8,4},{9,5},{1... | collective-permute-start | bytes 393224 | tf_op jit(solution)/shard_map/ppermute | solution.py:29
  277.6 31.6 %collective-permute-start.63 = (bf16[4,16,32,128]{3,2,1,0:T(8,128)(2,1)S(1)}, bf16[4,16,32,128]{3,2,1,0:T(8,128)(2,1)S(1)}, u32[]{:S(2)}, u32[]{:S(2)}) collective-permute-start(bf16[4,16,32,128]{3,2,1,0:T(8,128)(2,1)S(1)} %pad_maximum_fusion.1.t0), channel_id=1, source_target_pairs={{0,1},{1,2},{2,3},{3,0},{4,5},{5,6},{6,7},{7,4},{8,9},{9,10},{10,1... | collective-permute-start | bytes 1572872 | tf_op jit(solution)/shard_map/ppermute | solution.py:33
  277.6 16.5 %collective-permute-start.54 = (bf16[16,32,128]{2,1,0:T(8,128)(2,1)S(1)}, bf16[16,32,128]{2,1,0:T(8,128)(2,1)S(1)}, u32[]{:S(2)}, u32[]{:S(2)}) collective-permute-start(bf16[16,32,128]{2,1,0:T(8,128)(2,1)S(1)} %get-tuple-element.202), channel_id=1, source_target_pairs={{0,1},{1,2},{2,3},{3,0},{4,5},{5,6},{6,7},{7,4},{8,9},{9,10},{10,1... | collective-permute-start | bytes 393224 | tf_op jit(solution)/shard_map/ppermute | solution.py:33
  277.7 31.7 %collective-permute-start.64 = (bf16[4,16,32,128]{3,2,1,0:T(8,128)(2,1)S(1)}, bf16[4,16,32,128]{3,2,1,0:T(8,128)(2,1)S(1)}, u32[]{:S(2)}, u32[]{:S(2)}) collective-permute-start(bf16[4,16,32,128]{3,2,1,0:T(8,128)(2,1)S(1)} %pad_maximum_fusion.1.t0), channel_id=1, source_target_pairs={{0,2},{1,3},{2,0},{3,1},{4,6},{5,7},{6,4},{7,5},{8,10},{9,11},{10,... | collective-permute-start | bytes 1572872 | tf_op jit(solution)/shard_map/ppermute | solution.py:33
  281.5 27.9 %collective-permute-start.65 = (bf16[4,16,32,128]{3,2,1,0:T(8,128)(2,1)S(1)}, bf16[4,16,32,128]{3,2,1,0:T(8,128)(2,1)S(1)}, u32[]{:S(2)}, u32[]{:S(2)}) collective-permute-start(bf16[4,16,32,128]{3,2,1,0:T(8,128)(2,1)S(1)} %pad_maximum_fusion.1.t0), channel_id=1, source_target_pairs={{0,3},{1,0},{2,1},{3,2},{4,7},{5,4},{6,5},{7,6},{8,11},{9,8},{10,9... | collective-permute-start | bytes 1572872 | tf_op jit(solution)/shard_map/ppermute | solution.py:33
  281.5 18.4 %collective-permute-start.55 = (bf16[16,32,128]{2,1,0:T(8,128)(2,1)S(1)}, bf16[16,32,128]{2,1,0:T(8,128)(2,1)S(1)}, u32[]{:S(2)}, u32[]{:S(2)}) collective-permute-start(bf16[16,32,128]{2,1,0:T(8,128)(2,1)S(1)} %get-tuple-element.202), channel_id=1, source_target_pairs={{0,2},{1,3},{2,0},{3,1},{4,6},{5,7},{6,4},{7,5},{8,10},{9,11},{10,... | collective-permute-start | bytes 393224 | tf_op jit(solution)/shard_map/ppermute | solution.py:33
  294.2 11.6 %collective-permute-start.56 = (bf16[16,32,128]{2,1,0:T(8,128)(2,1)S(1)}, bf16[16,32,128]{2,1,0:T(8,128)(2,1)S(1)}, u32[]{:S(2)}, u32[]{:S(2)}) collective-permute-start(bf16[16,32,128]{2,1,0:T(8,128)(2,1)S(1)} %get-tuple-element.202), channel_id=1, source_target_pairs={{0,3},{1,0},{2,1},{3,2},{4,7},{5,4},{6,5},{7,6},{8,11},{9,8},{10,9... | collective-permute-start | bytes 393224 | tf_op jit(solution)/shard_map/ppermute | solution.py:33
  305.8 15.7 %collective-permute-start.57 = (bf16[4,16,32,128]{3,2,1,0:T(8,128)(2,1)S(1)}, bf16[4,16,32,128]{3,2,1,0:T(8,128)(2,1)S(1)}, u32[]{:S(2)}, u32[]{:S(2)}) collective-permute-start(bf16[4,16,32,128]{3,2,1,0:T(8,128)(2,1)S(1)} %pad_maximum_fusion.t0), channel_id=1, source_target_pairs={{0,4},{1,5},{2,6},{3,7},{4,8},{5,9},{6,10},{7,11},{8,12},{9,13},{1... | collective-permute-start | bytes 1572872 | tf_op jit(solution)/shard_map/ppermute | solution.py:29
  305.9 22.0 %collective-permute-start.58 = (bf16[4,16,32,128]{3,2,1,0:T(8,128)(2,1)S(1)}, bf16[4,16,32,128]{3,2,1,0:T(8,128)(2,1)S(1)}, u32[]{:S(2)}, u32[]{:S(2)}) collective-permute-start(bf16[4,16,32,128]{3,2,1,0:T(8,128)(2,1)S(1)} %pad_maximum_fusion.t0), channel_id=1, source_target_pairs={{0,8},{1,9},{2,10},{3,11},{4,12},{5,13},{6,14},{7,15},{8,0},{9,1},... | collective-permute-start | bytes 1572872 | tf_op jit(solution)/shard_map/ppermute | solution.py:29
  309.1 21.5 %collective-permute-start.59 = (bf16[4,16,32,128]{3,2,1,0:T(8,128)(2,1)S(1)}, bf16[4,16,32,128]{3,2,1,0:T(8,128)(2,1)S(1)}, u32[]{:S(2)}, u32[]{:S(2)}) collective-permute-start(bf16[4,16,32,128]{3,2,1,0:T(8,128)(2,1)S(1)} %pad_maximum_fusion.t0), channel_id=1, source_target_pairs={{0,12},{1,13},{2,14},{3,15},{4,0},{5,1},{6,2},{7,3},{8,4},{9,5},{1... | collective-permute-start | bytes 1572872 | tf_op jit(solution)/shard_map/ppermute | solution.py:29
  311.7 24.7 %collective-permute-start.66 = (bf16[32,32,128]{2,1,0:T(8,128)(2,1)S(1)}, bf16[32,32,128]{2,1,0:T(8,128)(2,1)S(1)}, u32[]{:S(2)}, u32[]{:S(2)}) collective-permute-start(bf16[32,32,128]{2,1,0:T(8,128)(2,1)S(1)} %get-tuple-element.213), channel_id=1, source_target_pairs={{0,16},{16,0},{32,48},{48,32},{64,80},{80,64},{96,112},{112,96},{1... | collective-permute-start | bytes 786440 | tf_op jit(solution)/shard_map/ppermute | solution.py:23
  321.3 17.0 %collective-permute-start.67 = (bf16[32,32,128]{2,1,0:T(8,128)(2,1)S(1)}, bf16[32,32,128]{2,1,0:T(8,128)(2,1)S(1)}, u32[]{:S(2)}, u32[]{:S(2)}) collective-permute-start(bf16[32,32,128]{2,1,0:T(8,128)(2,1)S(1)} %get-tuple-element.214), channel_id=1, source_target_pairs={{0,32},{16,48},{32,64},{48,80},{64,96},{80,112},{96,0},{112,16},{1... | collective-permute-start | bytes 786440 | tf_op jit(solution)/shard_map/ppermute | solution.py:23
  321.6 19.0 %collective-permute-start.68 = (bf16[32,32,128]{2,1,0:T(8,128)(2,1)S(1)}, bf16[32,32,128]{2,1,0:T(8,128)(2,1)S(1)}, u32[]{:S(2)}, u32[]{:S(2)}) collective-permute-start(bf16[32,32,128]{2,1,0:T(8,128)(2,1)S(1)} %get-tuple-element.215), channel_id=1, source_target_pairs={{0,48},{16,32},{32,80},{48,64},{64,112},{80,96},{96,16},{112,0},{1... | collective-permute-start | bytes 786440 | tf_op jit(solution)/shard_map/ppermute | solution.py:23
  327.9 13.0 %collective-permute-start.69 = (bf16[32,32,128]{2,1,0:T(8,128)(2,1)S(1)}, bf16[32,32,128]{2,1,0:T(8,128)(2,1)S(1)}, u32[]{:S(2)}, u32[]{:S(2)}) collective-permute-start(bf16[32,32,128]{2,1,0:T(8,128)(2,1)S(1)} %get-tuple-element.216), channel_id=1, source_target_pairs={{0,64},{16,80},{32,96},{48,112},{64,0},{80,16},{96,32},{112,48},{1... | collective-permute-start | bytes 786440 | tf_op jit(solution)/shard_map/ppermute | solution.py:23
  330.6 17.0 %collective-permute-start.70 = (bf16[32,32,128]{2,1,0:T(8,128)(2,1)S(1)}, bf16[32,32,128]{2,1,0:T(8,128)(2,1)S(1)}, u32[]{:S(2)}, u32[]{:S(2)}) collective-permute-start(bf16[32,32,128]{2,1,0:T(8,128)(2,1)S(1)} %get-tuple-element.217), channel_id=1, source_target_pairs={{0,80},{16,64},{32,112},{48,96},{64,16},{80,0},{96,48},{112,32},{1... | collective-permute-start | bytes 786440 | tf_op jit(solution)/shard_map/ppermute | solution.py:23
  336.4 14.2 %collective-permute-start.71 = (bf16[32,32,128]{2,1,0:T(8,128)(2,1)S(1)}, bf16[32,32,128]{2,1,0:T(8,128)(2,1)S(1)}, u32[]{:S(2)}, u32[]{:S(2)}) collective-permute-start(bf16[32,32,128]{2,1,0:T(8,128)(2,1)S(1)} %get-tuple-element.218), channel_id=1, source_target_pairs={{0,96},{16,112},{32,0},{48,16},{64,32},{80,48},{96,64},{112,80},{1... | collective-permute-start | bytes 786440 | tf_op jit(solution)/shard_map/ppermute | solution.py:23
  338.3 18.5 %collective-permute-start.72 = (bf16[32,32,128]{2,1,0:T(8,128)(2,1)S(1)}, bf16[32,32,128]{2,1,0:T(8,128)(2,1)S(1)}, u32[]{:S(2)}, u32[]{:S(2)}) collective-permute-start(bf16[32,32,128]{2,1,0:T(8,128)(2,1)S(1)} %get-tuple-element.219), channel_id=1, source_target_pairs={{0,112},{16,96},{32,16},{48,0},{64,48},{80,32},{96,80},{112,64},{1... | collective-permute-start | bytes 786440 | tf_op jit(solution)/shard_map/ppermute | solution.py:23
  356.9 9.4 %collective-permute-start.74 = (bf16[32,32,128]{2,1,0:T(8,128)(2,1)S(1)}, bf16[32,32,128]{2,1,0:T(8,128)(2,1)S(1)}, u32[]{:S(2)}, u32[]{:S(2)}) collective-permute-start(bf16[32,32,128]{2,1,0:T(8,128)(2,1)S(1)} %get-tuple-element.230), channel_id=1, source_target_pairs={{0,32},{16,48},{32,64},{48,80},{64,96},{80,112},{96,0},{112,16},{1... | collective-permute-start | bytes 786440 | tf_op jit(solution)/shard_map/ppermute | solution.py:23
  358.4 13.7 %collective-permute-start.75 = (bf16[32,32,128]{2,1,0:T(8,128)(2,1)S(1)}, bf16[32,32,128]{2,1,0:T(8,128)(2,1)S(1)}, u32[]{:S(2)}, u32[]{:S(2)}) collective-permute-start(bf16[32,32,128]{2,1,0:T(8,128)(2,1)S(1)} %get-tuple-element.231), channel_id=1, source_target_pairs={{0,48},{16,32},{32,80},{48,64},{64,112},{80,96},{96,16},{112,0},{1... | collective-permute-start | bytes 786440 | tf_op jit(solution)/shard_map/ppermute | solution.py:23
  358.7 20.1 %collective-permute-start.76 = (bf16[32,32,128]{2,1,0:T(8,128)(2,1)S(1)}, bf16[32,32,128]{2,1,0:T(8,128)(2,1)S(1)}, u32[]{:S(2)}, u32[]{:S(2)}) collective-permute-start(bf16[32,32,128]{2,1,0:T(8,128)(2,1)S(1)} %get-tuple-element.232), channel_id=1, source_target_pairs={{0,64},{16,80},{32,96},{48,112},{64,0},{80,16},{96,32},{112,48},{1... | collective-permute-start | bytes 786440 | tf_op jit(solution)/shard_map/ppermute | solution.py:23
  361.4 23.1 %collective-permute-start.77 = (bf16[32,32,128]{2,1,0:T(8,128)(2,1)S(1)}, bf16[32,32,128]{2,1,0:T(8,128)(2,1)S(1)}, u32[]{:S(2)}, u32[]{:S(2)}) collective-permute-start(bf16[32,32,128]{2,1,0:T(8,128)(2,1)S(1)} %get-tuple-element.233), channel_id=1, source_target_pairs={{0,80},{16,64},{32,112},{48,96},{64,16},{80,0},{96,48},{112,32},{1... | collective-permute-start | bytes 786440 | tf_op jit(solution)/shard_map/ppermute | solution.py:23
  362.0 22.5 %collective-permute-start.78 = (bf16[32,32,128]{2,1,0:T(8,128)(2,1)S(1)}, bf16[32,32,128]{2,1,0:T(8,128)(2,1)S(1)}, u32[]{:S(2)}, u32[]{:S(2)}) collective-permute-start(bf16[32,32,128]{2,1,0:T(8,128)(2,1)S(1)} %get-tuple-element.234), channel_id=1, source_target_pairs={{0,96},{16,112},{32,0},{48,16},{64,32},{80,48},{96,64},{112,80},{1... | collective-permute-start | bytes 786440 | tf_op jit(solution)/shard_map/ppermute | solution.py:23
  366.2 19.1 %collective-permute-start.79 = (bf16[32,32,128]{2,1,0:T(8,128)(2,1)S(1)}, bf16[32,32,128]{2,1,0:T(8,128)(2,1)S(1)}, u32[]{:S(2)}, u32[]{:S(2)}) collective-permute-start(bf16[32,32,128]{2,1,0:T(8,128)(2,1)S(1)} %get-tuple-element.235), channel_id=1, source_target_pairs={{0,112},{16,96},{32,16},{48,0},{64,48},{80,32},{96,80},{112,64},{1... | collective-permute-start | bytes 786440 | tf_op jit(solution)/shard_map/ppermute | solution.py:23
  (74 other events, 976.0 us)
Sparse Core Ops, SparseCore 0:
  10.3 48.9 all-gather.2
  220.6 24.6 all-gather.4

commit v2 on v1

v2 whole, which is shorter than its diff:
```python
import functools

import jax
import jax.numpy as jnp
from jax import lax
from jax.experimental import pallas as pl
from jax.experimental.pallas import tpu as pltpu
from jax.sharding import PartitionSpec as P

BF16 = jnp.bfloat16
F32 = jnp.float32
MIB = 1024 * 1024
SMEM = pl.BlockSpec(memory_space=pltpu.SMEM)
VMEM = pl.BlockSpec(memory_space=pltpu.VMEM)
HBM = pl.BlockSpec(memory_space=pl.ANY)


def over_z(array, by):
    return lax.ppermute(array, "grid", [(2 * z + c, 2 * ((z + by) % 4) + c) for z in range(4) for c in range(2)])


def over_column(array, dz, dc):
    return lax.ppermute(
        array, "grid", [(2 * z + c, 2 * ((z + dz) % 4) + (c ^ dc)) for z in range(4) for c in range(2)]
    )


def over_x(array, by):
    return lax.ppermute(array, "mesh", [(4 * x + y, 4 * ((x + by) % 4) + y) for x in range(4) for y in range(4)])


def over_y(array, by):
    return lax.ppermute(array, "mesh", [(4 * x + y, 4 * x + (y + by) % 4) for x in range(4) for y in range(4)])


def over_mesh(array, by):
    return lax.ppermute(array, "mesh", [(p, (p + by) % 16) for p in range(16)])


def local(body, outs, ins, smem=1, scratch=(), limit=12):
    return pl.pallas_call(
        body,
        out_shape=[jax.ShapeDtypeStruct(shape, dtype) for shape, dtype in outs],
        in_specs=[SMEM] * smem + [VMEM] * (len(ins) - smem),
        out_specs=[VMEM] * len(outs),
        scratch_shapes=list(scratch),
        compiler_params=pltpu.CompilerParams(vmem_limit_bytes=limit * MIB),
    )(*ins)


def lanes(index):
    return pl.ds(pl.multiple_of((index & 3) * 128, 128), 128)


def dot(a, b):
    return jnp.dot(a, b, preferred_element_type=F32)


def dot_t(a, b):
    return lax.dot_general(a, b, (((1,), (1,)), ((), ())), preferred_element_type=F32)


def silu_slope(values):
    sigmoid_v = jax.nn.sigmoid(values)
    return sigmoid_v * (1.0 + values * (1.0 - sigmoid_v))


def move(source, target, sems, i):
    return pltpu.make_async_copy(source, target, sems.at[i])


def messages_body(
    source, latent, w_send, mask, other, out, other_out, x, w, m, o, sent, msg, o_b, s_x, s_w, s_m, s_o, s_out
):
    def x_in(i):
        at = pl.ds(pl.multiple_of(i * 512, 512), 512)
        return move(latent.at[at, :], x.at[at, :], s_x, i)

    def m_in(i):
        return move(mask.at[pl.ds(i * 8, 8)], m.at[pl.ds(i * 8, 8)], s_m, i)

    def out_to(i):
        return move(msg.at[:, pl.ds(i * 8, 8)], out.at[:, pl.ds(i * 8, 8)], s_out, i)

    w_in, o_in, o_to = move(w_send, w, s_w, 0), move(other, o, s_o, 0), move(o_b, other_out, s_o, 1)
    w_in.start()
    for i in range(6):
        x_in(i).start()
    for i in range(4):
        m_in(i).start()
    o_in.start()
    w_in.wait()

    def rows(i, _):
        x_in(i).wait()
        at = pl.ds(pl.multiple_of(i * 512, 512), 512)
        sent[at, :] = dot(x[at, :], w[...]).astype(BF16)
        return 0

    lax.fori_loop(0, 6, rows, 0)

    def edges(i, _):
        m_in(i).wait()
        for k in range(8):
            e = i * 8 + k
            block = sent[pl.ds(pl.multiple_of(source[e] * 128, 128), 128), :]
            message = lax.dot_general(
                m[e].astype(F32).astype(BF16), block, (((0,), (0,)), ((), ())), preferred_element_type=F32
            ).astype(BF16)
            for n in range(8):
                z, c = n // 2, n % 2
                msg[n, e] = message[64 * c : 64 * c + 64, 128 * z : 128 * z + 128]
        out_to(i).start()
        return 0

    lax.fori_loop(0, 4, edges, 0)
    o_in.wait()
    o_b[...] = o[...].astype(F32).astype(BF16)
    o_to.start()
    for i in range(4):
        out_to(i).wait()
    o_to.wait()


def send_messages(source, latent, w_send, mask, other):
    sems = lambda n: pltpu.SemaphoreType.DMA((n,))
    return pl.pallas_call(
        messages_body,
        out_shape=[
            jax.ShapeDtypeStruct((8, 32, 64, 128), BF16),
            jax.ShapeDtypeStruct((16, 128, 128), BF16),
        ],
        in_specs=[SMEM, HBM, HBM, HBM, HBM],
        out_specs=[HBM, HBM],
        scratch_shapes=[
            pltpu.VMEM((3072, 512), BF16),
            pltpu.VMEM((512, 512), BF16),
            pltpu.VMEM((32, 128, 128), jnp.int32),
            pltpu.VMEM((16, 128, 128), jnp.int32),
            pltpu.VMEM((3072, 512), BF16),
            pltpu.VMEM((8, 32, 64, 128), BF16),
            pltpu.VMEM((16, 128, 128), BF16),
            sems(6),
            sems(1),
            sems(4),
            sems(2),
            sems(4),
        ],
        compiler_params=pltpu.CompilerParams(vmem_limit_bytes=56 * MIB),
    )(source, latent, w_send, mask, other)


def combine_body(ids, meta, arrived, *rest):
    outs, acc = rest[:8], rest[8]
    x, y = ids[2], ids[3]
    acc[...] = jnp.zeros_like(acc)

    def add(n, _):
        acc[meta[(n >> 5) * 64 + (n & 31)]] += arrived[n].astype(F32)
        return 0

    lax.fori_loop(0, 256, add, 0, unroll=4)
    for kx in range(4):
        for ky in range(4):
            at = pl.ds((4 * ((x + kx) & 3) + ((y + ky) & 3)) * 16, 16)
            outs[ky][kx] = acc[at, :32, :].astype(BF16)
            outs[4 + kx][ky] = acc[at, 32:, :].astype(BF16)


def combine(ids, meta, arrived):
    outs = local(
        combine_body,
        [((4, 16, 32, 128), BF16)] * 8,
        [ids, meta, arrived.reshape(256, 64, 128)],
        smem=2,
        scratch=[pltpu.VMEM((256, 64, 128), F32)],
        limit=20,
    )
    return outs[:4], outs[4:]


def add_rows_body(*refs):
    for q in range(2):
        a, b, c, d = refs[4 * q : 4 * q + 4]
        for j in range(4):
            refs[8 + 4 * q + j][...] = (
                a[j].astype(F32) + b[j].astype(F32) + c[j].astype(F32) + d[j].astype(F32)
            ).astype(BF16)


def reduce_halves(by_y, by_x):
    by_y = [by_y[0]] + [over_y(by_y[k], k) for k in (1, 2, 3)]
    by_x = [by_x[0]] + [over_x(by_x[k], k) for k in (1, 2, 3)]
    sums = local(add_rows_body, [((16, 32, 128), BF16)] * 8, [*by_y, *by_x], smem=0)
    left, right = sums[:4], sums[4:]
    left = [left[0]] + [over_x(left[k], k) for k in (1, 2, 3)]
    right = [right[0]] + [over_y(right[k], k) for k in (1, 2, 3)]
    return [*left, *right]


def add_last_body(ids, *rest):
    terms, outs, acc = rest[:8], rest[8:12], rest[12]
    z = ids[0]
    for q in range(2):
        total = terms[4 * q][...].astype(F32)
        for more in terms[4 * q + 1 : 4 * q + 4]:
            total += more[...].astype(F32)
        acc[:, 32 * q : 32 * q + 32, :] = total.astype(BF16)
    for k in range(4):
        outs[k][...] = acc[pl.ds(4 * ((z + k) & 3), 4)]


def add_last(ids, terms):
    return local(
        add_last_body,
        [((4, 64, 128), BF16)] * 4,
        [ids, *terms],
        scratch=[pltpu.VMEM((16, 64, 128), BF16)],
    )


def to_rows(z, pieces, wide):
    for k in range(4):
        wide[:, lanes(z - k)] = pieces[k][...].reshape(256, 128)
    return wide[...]


def from_rows(z, wide, outs):
    for k in range(4):
        outs[k][...] = wide[:, lanes(z + k)].reshape(4, 64, 128)


def enc_mlp_body(ids, p0, p1, p2, p3, pre_self, rows, w_agg, w_out, w_pass, pre_ref, first_ref, *rest):
    outs, wide = rest[:4], rest[4]
    z = ids[0]
    summed = to_rows(z, (p0, p1, p2, p3), wide)
    pre = pre_self[...] + dot(summed, w_agg[...])
    pre_ref[...] = pre
    hidden = jax.nn.silu(pre).astype(BF16)
    first = (rows[...].astype(F32) + dot(hidden, w_out[...])).astype(BF16)
    first_ref[...] = first
    wide[...] = dot(first, w_pass[...]).astype(BF16)
    from_rows(z, wide, outs)


def proc_mlp_body(ids, p0, p1, p2, p3, pre_self, rows, g_hidden, w_agg, w_out, out_ref, g_pre_ref, *rest):
    outs, wide = rest[:4], rest[4]
    z = ids[0]
    summed = to_rows(z, (p0, p1, p2, p3), wide)
    pre = pre_self[...] + dot(summed, w_agg[...])
    g_pre = (g_hidden[...].astype(F32) * silu_slope(pre)).astype(BF16)
    g_pre_ref[...] = g_pre
    wide[...] = dot_t(g_pre, w_agg[...]).astype(BF16)
    from_rows(z, wide, outs)
    hidden = jax.nn.silu(pre).astype(BF16)
    out_ref[...] = (rows[...].astype(F32) + dot(hidden, w_out[...])).astype(BF16)


def enc_back_body(ids, p0, p1, p2, p3, g_part, pre, w_pass, w_out, w_agg, *rest):
    outs, wide = rest[:4], rest[4]
    z = ids[0]
    g_pass = to_rows(z, (p0, p1, p2, p3), wide)
    g_first = (g_part[...] + dot_t(g_pass, w_pass[...])).astype(BF16)
    g_hidden = dot_t(g_first, w_out[...]).astype(BF16)
    g_pre = (g_hidden.astype(F32) * silu_slope(pre[...])).astype(BF16)
    wide[...] = dot_t(g_pre, w_agg[...]).astype(BF16)
    from_rows(z, wide, outs)


ROWS = ((256, 512), BF16)
ROWS32 = ((256, 512), F32)
PIECE = ((4, 64, 128), BF16)
WIDE = pltpu.VMEM((256, 512), BF16)


def table_body(ids, p0, p1, p2, p3, out):
    for k, piece in enumerate((p0, p1, p2, p3)):
        out[pl.ds(4 * ((ids[0] - k) & 3), 4)] = piece[...]


def table(ids, pieces):
    return local(table_body, [((16, 64, 128), BF16)], [ids, *pieces])[0]


def halves_body(ids, p0, p1, p2, p3, left, right):
    for k, piece in enumerate((p0, p1, p2, p3)):
        at = pl.ds(4 * ((ids[0] - k) & 3), 4)
        left[at] = piece[:, :32, :]
        right[at] = piece[:, 32:, :]


def halves(ids, pieces):
    return local(halves_body, [((16, 32, 128), BF16)] * 2, [ids, *pieces])


def stack_body(*refs):
    for k in range(4):
        refs[8][k] = refs[k][...]
        refs[9][k] = refs[4 + k][...]


def gather_halves(left, right):
    left = [left] + [over_x(left, k) for k in (1, 2, 3)]
    right = [right] + [over_y(right, k) for k in (1, 2, 3)]
    left, right = local(stack_body, [((4, 16, 32, 128), BF16)] * 2, [*left, *right], smem=0)
    return [left] + [over_y(left, k) for k in (1, 2, 3)] + [right] + [over_x(right, k) for k in (1, 2, 3)]


def spread_z(pieces):
    return [pieces[0]] + [over_z(pieces[k], k) for k in (1, 2, 3)]


def edge_loop(c, meta, one):
    def band(n, _):
        row = (2 * (n >> 2) + c) * 64 + (n & 3) * 4
        one(n * 4, [(meta[row + 32 + e], meta[row + 48 + e]) for e in range(4)])
        return 0

    lax.fori_loop(0, 16, band, 0)


def proc_body(ids, meta, masks, *rest):
    tables, (own, other, ext, acc) = rest[:6], rest[6:]
    c = ids[1]
    at_own = pl.ds(pl.multiple_of(64 * c, 64), 64)
    at_other = pl.ds(pl.multiple_of(64 * (1 - c), 64), 64)
    for k in range(3):
        ext[16 * k : 16 * k + 16, at_own, :] = tables[2 * k][...]
        ext[16 * k : 16 * k + 16, at_other, :] = tables[2 * k + 1][...]
    acc[...] = jnp.zeros_like(acc)

    def one(base, edges):
        terms = [
            lax.dot_general(masks[base + e], ext[source], (((0,), (0,)), ((), ())), preferred_element_type=F32)
            for e, (source, _) in enumerate(edges)
        ]
        for term, (_, target) in zip(terms, edges):
            acc[target] += term

    edge_loop(c, meta, one)
    own[...] = acc[:, at_own, :]
    other[...] = acc[:, at_other, :].astype(BF16)


def proc_back_body(ids, meta, masks, mine, theirs, own, other, grads, acc):
    c = ids[1]
    at_own = pl.ds(pl.multiple_of(64 * c, 64), 64)
    at_other = pl.ds(pl.multiple_of(64 * (1 - c), 64), 64)
    grads[:, at_own, :] = mine[...]
    grads[:, at_other, :] = theirs[...]
    acc[...] = jnp.zeros_like(acc)

    def one(base, edges):
        terms = [dot(masks[base + e], grads[target]) for e, (_, target) in enumerate(edges)]
        for term, (source, _) in zip(terms, edges):
            acc[source] += term

    edge_loop(c, meta, one)
    own[...] = acc[:, at_own, :]
    other[...] = acc[:, at_other, :].astype(BF16)


def pair_sum_body(ids, own, other, *outs):
    for k in range(4):
        at = pl.ds(4 * ((ids[0] + k) & 3), 4)
        outs[k][...] = (own[at] + other[at].astype(F32)).astype(BF16)


def part_sum_body(own, other, *outs):
    for k in range(3):
        at = slice(16 * k, 16 * k + 16)
        outs[k][...] = (own[at] + other[at].astype(F32)).astype(BF16)


def three_sum_body(ids, a, b, c, *outs):
    for k in range(4):
        at = pl.ds(4 * ((ids[0] + k) & 3), 4)
        outs[k][...] = (a[at].astype(F32) + b[at].astype(F32) + c[at].astype(F32)).astype(BF16)


def fetch_body(ids, meta, *rest):
    parts, out, tab = rest[:8], rest[8], rest[9]
    x, y, owner = ids[2], ids[3], pl.program_id(0)

    @pl.when(owner == 0)
    def _():
        for kx in range(4):
            for ky in range(4):
                at = (kx * 4 + ky) * 16
                tab[at : at + 16, :32, :] = parts[ky][kx]
                tab[at : at + 16, 32:, :] = parts[4 + kx][ky]

    def take(e, _):
        slot = meta[owner * 64 + e]
        kx = (x - (slot >> 6)) & 3
        ky = (y - ((slot >> 4) & 3)) & 3
        out[0, e] = tab[(kx * 4 + ky) * 16 + (slot & 15)]
        return 0

    lax.fori_loop(0, 32, take, 0, unroll=4)


def fetch(ids, meta, parts):
    return pl.pallas_call(
        fetch_body,
        grid=(8,),
        out_shape=jax.ShapeDtypeStruct((8, 32, 64, 128), BF16),
        in_specs=[SMEM, SMEM] + [VMEM] * 8,
        out_specs=pl.BlockSpec((1, 32, 64, 128), lambda i: (i, 0, 0, 0)),
        scratch_shapes=[pltpu.VMEM((256, 64, 128), BF16)],
        compiler_params=pltpu.CompilerParams(vmem_limit_bytes=48 * MIB),
    )(ids, meta, *parts)


def grid_body(source, w_send, mask, pieces, out, w, m, p, acc, wide, o, s_w, s_m, s_p, s_out):
    def m_in(i):
        return move(mask.at[pl.ds(i * 8, 8)], m.at[pl.ds(i * 8, 8)], s_m, i)

    def p_in(i):
        return move(pieces.at[:, pl.ds(i * 8, 8)], p.at[:, pl.ds(i * 8, 8)], s_p, i)

    def out_to(i):
        at = pl.ds(pl.multiple_of(i * 512, 512), 512)
        return move(o.at[at, :], out.at[at, :], s_out, i)

    w_in = move(w_send, w, s_w, 0)
    for i in range(4):
        p_in(i).start()
        m_in(i).start()
    w_in.start()
    acc[...] = jnp.zeros_like(acc)

    def edges(i, _):
        p_in(i).wait()
        m_in(i).wait()
        for k in range(8):
            e = i * 8 + k
            for n in range(8):
                z, c = n // 2, n % 2
                wide[k, 64 * c : 64 * c + 64, 128 * z : 128 * z + 128] = p[n, e]
        for k in range(8):
            e = i * 8 + k
            at = pl.ds(pl.multiple_of(source[e] * 128, 128), 128)
            acc[at, :] += dot(m[e].astype(F32).astype(BF16), wide[k])
        return 0

    lax.fori_loop(0, 4, edges, 0)
    w_in.wait()

    def rows(i, _):
        at = pl.ds(pl.multiple_of(i * 512, 512), 512)
        o[at, :] = dot_t(acc[at, :].astype(BF16), w[...]).astype(BF16)
        out_to(i).start()
        return 0

    lax.fori_loop(0, 6, rows, 0)
    for i in range(6):
        out_to(i).wait()


def grid_gradient(source, w_send, mask, pieces):
    sems = lambda n: pltpu.SemaphoreType.DMA((n,))
    return pl.pallas_call(
        grid_body,
        out_shape=jax.ShapeDtypeStruct((3072, 512), BF16),
        in_specs=[SMEM, HBM, HBM, HBM],
        out_specs=HBM,
        scratch_shapes=[
            pltpu.VMEM((512, 512), BF16),
            pltpu.VMEM((32, 128, 128), jnp.int32),
            pltpu.VMEM((8, 32, 64, 128), BF16),
            pltpu.VMEM((3072, 512), F32),
            pltpu.VMEM((8, 128, 512), BF16),
            pltpu.VMEM((3072, 512), BF16),
            sems(1),
            sems(4),
            sems(4),
            sems(6),
        ],
        compiler_params=pltpu.CompilerParams(vmem_limit_bytes=56 * MIB),
    )(source, w_send, mask, pieces)


def column_exchange(pieces):
    return lax.all_to_all(pieces, "grid", 0, 0, tiled=True)


def own_rows(array, z, c):
    cut = lax.dynamic_slice(array.reshape(4, 4, 2, 64, 512), (z, 0, c, 0, 0), (1, 4, 1, 64, 512))
    return cut.reshape(256, 512)


def per_device(
    grid_latent,
    mesh_latent,
    mesh_cotangent,
    w_send,
    w_self_enc,
    w_agg_enc,
    w_out_enc,
    w_pass,
    w_self_proc,
    w_agg_proc,
    w_out_proc,
    enc_source,
    enc_part,
    enc_block,
    enc_mask,
    proc_source,
    proc_target,
    proc_mask,
):
    g, p = lax.axis_index("grid"), lax.axis_index("mesh")
    z, c = g // 2, g % 2
    ids = jnp.stack([z, c, p // 4, p % 4]).astype(jnp.int32)
    slots = enc_part[:, 0] * 16 + enc_block

    labels = jnp.concatenate([slots, proc_source, proc_target])

    messages, proc_mask = send_messages(enc_source, grid_latent, w_send, enc_mask, proc_mask)
    messages, labels, mesh_latent, mesh_cotangent = lax.optimization_barrier(
        (messages, labels, mesh_latent, mesh_cotangent)
    )
    arrived = column_exchange(messages)
    rows = own_rows(mesh_latent, z, c)
    cotangent = own_rows(mesh_cotangent, z, c)
    pre_self = dot(rows, w_self_enc)
    g_hid_proc = dot_t(cotangent, w_out_proc).astype(BF16)
    labels, pre_self, g_hid_proc, rows, cotangent = lax.optimization_barrier(
        (labels, pre_self, g_hid_proc, rows, cotangent)
    )
    meta = lax.all_gather(labels, "grid", axis=0, tiled=True)
    arrived, meta, proc_mask = lax.optimization_barrier((arrived, meta, proc_mask))
    masks = lax.all_gather(
        proc_mask,
        "grid",
        axis=0,
        tiled=True,
        axis_index_groups=[[2 * i + j for i in range(4)] for j in range(2)],
    )
    summed = spread_z(add_last(ids, reduce_halves(*combine(ids, meta, arrived))))
    masks, pre_self = lax.optimization_barrier((masks, pre_self))
    pre_enc, first, *passed = local(
        enc_mlp_body,
        [ROWS32, ROWS] + [PIECE] * 4,
        [ids, *summed, pre_self, rows, w_agg_enc, w_out_enc, w_pass],
        scratch=[WIDE],
    )

    own = table(ids, spread_z(passed))
    tables = [over_mesh(own, 1), own, over_mesh(own, -1)]
    both = []
    for one in tables:
        both += [one, over_column(one, 0, 1)]
    mine, theirs = local(
        proc_body,
        [((16, 64, 128), F32), ((16, 64, 128), BF16)],
        [ids, meta, masks, *both],
        smem=2,
        scratch=[pltpu.VMEM((48, 128, 128), BF16), pltpu.VMEM((16, 128, 128), F32)],
    )
    summed = local(pair_sum_body, [PIECE] * 4, [ids, mine, over_column(theirs, 0, 1)])
    pre_self_proc = dot(first, w_self_proc)
    out_rows, g_pre_proc, *g_agg = local(
        proc_mlp_body,
        [ROWS, ROWS] + [PIECE] * 4,
        [ids, *spread_z(summed), pre_self_proc, first, g_hid_proc, w_agg_proc, w_out_proc],
        scratch=[WIDE],
    )
    g_first_part = cotangent.astype(F32) + dot_t(g_pre_proc, w_self_proc)
    own = table(ids, spread_z(g_agg))
    mine, theirs = local(
        proc_back_body,
        [((48, 64, 128), F32), ((48, 64, 128), BF16)],
        [ids, meta, masks, own, over_column(own, 0, 1)],
        smem=2,
        scratch=[pltpu.VMEM((16, 128, 128), BF16), pltpu.VMEM((48, 128, 128), F32)],
    )
    parts = local(part_sum_body, [((16, 64, 128), BF16)] * 3, [mine, over_column(theirs, 0, 1)], smem=0)
    g_pass = local(
        three_sum_body, [PIECE] * 4, [ids, over_mesh(parts[0], -1), parts[1], over_mesh(parts[2], 1)]
    )
    g_agg = local(
        enc_back_body,
        [PIECE] * 4,
        [ids, *spread_z(g_pass), g_first_part, pre_enc, w_pass, w_out_enc, w_agg_enc],
        scratch=[WIDE],
    )

    left, right = halves(ids, spread_z(g_agg))
    left, out_rows = lax.optimization_barrier((left, out_rows))
    mesh_out = lax.all_gather(out_rows.reshape(1, 4, 64, 512), "grid", axis=0, tiled=True)
    mesh_out = jnp.swapaxes(mesh_out.reshape(4, 2, 4, 64, 512), 1, 2).reshape(2048, 512)
    returned = column_exchange(fetch(ids, meta, gather_halves(left, right)))
    returned, mesh_out = lax.optimization_barrier((returned, mesh_out))
    grid_grad = grid_gradient(enc_source, w_send, enc_mask, returned)
    return (mesh_out, grid_grad)


def solution(mesh):
    return jax.shard_map(
        per_device,
        mesh=mesh,
        in_specs=(
            P(("grid", "mesh"), None),
            P("mesh", None),
            P("mesh", None),
            P(),
            P(),
            P(),
            P(),
            P(),
            P(),
            P(),
            P(),
            P(("grid", "mesh")),
            P(("grid", "mesh"), None),
            P(("grid", "mesh")),
            P(("grid", "mesh"), None, None),
            P(("grid", "mesh")),
            P(("grid", "mesh")),
            P(("grid", "mesh"), None, None),
        ),
        out_specs=(P("mesh", None), P(("grid", "mesh"), None)),
        check_vma=False,
    )
```

time: 412 us -> 347 us (0.84); the launches traced: 406 us -> 347 us
  starting transfers between devices: 145 us -> 99.8 us
  blocking collectives: 4.66 us -> 46.4 us
  local copies, waits for them, and re-layouts: 32.4 us -> 5.18 us
  waiting for transfers between devices: 155 us -> 131 us
    ppermute x34 -> x6, waiting for transfers between devices: 81.7 us -> 5.77 us  [over_column(): lax.ppermute(array, 'grid', [(2 * z + c, 2 * ((z + dz) % 4) + (c ^ dc)) f...]
    ppermute x34 -> x6, starting transfers between devices: 70 us -> 19.5 us  [over_column(): lax.ppermute(array, 'grid', [(2 * z + c, 2 * ((z + dz) % 4) + (c ^ dc)) f...]
    optimization_barrier x0 -> x1, blocking collectives: none -> 46.4 us  [per_device(): lax.optimization_barrier((arrived, meta, proc_mask))]
    all_to_all x0 -> x2, waiting for transfers between devices: none -> 45 us  [column_exchange(): return lax.all_to_all(pieces, 'grid', 0, 0, tiled=True)]
    unnamed x114 -> x29, local copies, waits for them, and re-layouts: 24.9 us -> 0.92 us
    all_to_all x0 -> x2, starting transfers between devices: none -> 21.4 us  [column_exchange(): return lax.all_to_all(pieces, 'grid', 0, 0, tiled=True)]
    ppermute x18, starting transfers between devices: 31.3 us -> 20.7 us  [over_z(): lax.ppermute(array, 'grid', [(2 * z + c, 2 * ((z + by) % 4) + c) for z in...]
    pallas_call x18 -> x15, Pallas kernels: 29.3 us -> 23.3 us  [local(): pl.pallas_call(body, out_shape=[jax.ShapeDtypeStruct(shape, dtype) for sh...]
  transfers between devices with their start and end apart: 82 -> 56, of which waited for: 47 -> 40; matrix products, arithmetic and copies ran while one was open for 2% -> 2% of each run, Pallas kernels for 10% -> 4%
where the time goes in v2:
time: 347 us
  waiting for transfers between devices  131 us (38%)
  starting transfers between devices  99.8 us (29%)
  blocking collectives  46.4 us (13%)
  Pallas kernels  45.7 us (13%)
  between operations  15.1 us (4%)
  local copies, waits for them, and re-layouts  5.18 us (1%)
    optimization_barrier x1, blocking collectives, per_device(): lax.optimization_barrier((arrived, meta, proc_mask))  46.4 us
    all_to_all x2, waiting for transfers between devices, column_exchange(): return lax.all_to_all(pieces, 'grid', 0, 0, tiled=True)  45 us
    ppermute x12, waiting for transfers between devices, over_y(): lax.ppermute(array, 'mesh', [(4 * x + y, 4 * x + (y + by) % 4) for x in r...  32.7 us
    pallas_call x15, Pallas kernels, local(): pl.pallas_call(body, out_shape=[jax.ShapeDtypeStruct(shape, dtype) for sh...  23.3 us
    all_to_all x2, starting transfers between devices, column_exchange(): return lax.all_to_all(pieces, 'grid', 0, 0, tiled=True)  21.4 us
    ppermute x18, starting transfers between devices, over_z(): lax.ppermute(array, 'grid', [(2 * z + c, 2 * ((z + by) % 4) + c) for z in...  20.7 us
    ppermute x6, starting transfers between devices, over_column(): lax.ppermute(array, 'grid', [(2 * z + c, 2 * ((z + dz) % 4) + (c ^ dc)) f...  19.5 us
    ppermute x12, waiting for transfers between devices, over_x(): lax.ppermute(array, 'mesh', [(4 * x + y, 4 * ((x + by) % 4) + y) for x in...  18.6 us
  transfers between devices with their start and end apart: 56, of which 40 were waited for; matrix products, arithmetic and copies ran while one was open for 2% of the time, Pallas kernels for 4%

profile of v2, /device:TPU:1, one launch (start us, length us, event | category | flops | bytes accessed | tf_op | source)
XLA Modules:
  0.0 346.7 jit_solution(9764582544747796831)
XLA Ops:
  8.7 8.7 %shard_map.185 = (bf16[8,32,64,128]{3,2,1,0:T(8,128)(2,1)}, bf16[16,128,128]{2,1,0:T(8,128)(2,1)}) custom-call(s32[32]{0:T(128)} %source.3, bf16[3072,512]{1,0:T(8,128)(2,1)} %latent.1, bf16[512,512]{1,0:T(8,128)(2,1)} %w_send.3, s32[32,128,128]{2,1,0:T(8,128)} %mask.3, s32[16,128,128]{2,1,0:T(8,128)} %other.1), custom_call_target="tpu_custom_call" | custom-call | tf_op jit(solution)/shard_map/pallas_call | solution.py:127
  17.4 7.0 %all-to-all-start = ((bf16[8,32,64,128]{3,2,1,0:T(8,128)(2,1)}), bf16[8,32,64,128]{3,2,1,0:T(8,128)(2,1)}, u32[]{:S(2)}, u32[]{:S(2)}) async-start(bf16[8,32,64,128]{3,2,1,0:T(8,128)(2,1)} %get-tuple-element.78), calls=%async_computation | async-start | bytes 8388608 | tf_op jit(solution)/shard_map/all_to_all | solution.py:485
  24.5 1.1 constant_dynamic-slice_fusion
  28.5 46.4 %all-reduce.meta = s32[512]{0:T(512)S(1)} all-reduce(s32[512]{0:T(512)S(1)} %dynamic-update-slice), channel_id=1, replica_groups=mesh['grid'=8,'mesh'=16] {'grid'}, use_global_device_ids=true, to_apply=%add | all-reduce | flops 512 | bytes 4096 | tf_op jit(solution)/shard_map/optimization_barrier | solution.py:533
  75.1 4.7 %shard_map.186 = (bf16[4,16,32,128]{3,2,1,0:T(8,128)(2,1)S(1)}, bf16[4,16,32,128]{3,2,1,0:T(8,128)(2,1)S(1)}, bf16[4,16,32,128]{3,2,1,0:T(8,128)(2,1)S(1)}, bf16...) custom-call(s32[4]{0:T(128)S(1)} %pad_add_fusion.ids, ...), custom_call_target="tpu_custom_call" | custom-call | tf_op jit(solution)/shard_map/pallas_call | solution.py:41
  79.8 1.4 collective-permute-start
  81.2 2.6 collective-permute-start.1
  84.9 1.2 collective-permute-start.3
  86.1 2.5 collective-permute-start.4
  88.5 4.2 %collective-permute-done.refs_1_ = bf16[4,16,32,128]{3,2,1,0:T(8,128)(2,1)S(1)} collective-permute-done((bf16[4,16,32,128]{3,2,1,0:T(8,128)(2,1)S(1)}, bf16[4,16,32,128]{3,2,1,0:T(8,128)(2,1)S(1)}, u32[]{:S(2)}, u32[]{:S(2)}) %collective-permute-start) | collective-permute-done | bytes 524320 | tf_op jit(solution)/shard_map/ppermute | solution.py:33
  92.7 2.5 collective-permute-start.5
  95.2 9.7 %collective-permute-done.1.refs_2_ = bf16[4,16,32,128]{3,2,1,0:T(8,128)(2,1)S(1)} collective-permute-done((bf16[4,16,32,128]{3,2,1,0:T(8,128)(2,1)S(1)}, bf16[4,16,32,128]{3,2,1,0:T(8,128)(2,1)S(1)}, u32[]{:S(2)}, u32[]{:S(2)}) %collective-permute-start.1) | collective-permute-done | bytes 524320 | tf_op jit(solution)/shard_map/ppermute | solution.py:33
  105.9 3.0 collective-permute-done.4.refs_6_
  109.9 2.4 collective-permute-start.11
  112.3 3.5 %collective-permute-start.6 = (bf16[16,32,128]{2,1,0:T(8,128)(2,1)S(1)}, bf16[16,32,128]{2,1,0:T(8,128)(2,1)S(1)}, u32[]{:S(2)}, u32[]{:S(2)}) collective-permute-start(bf16[16,32,128]{2,1,0:T(8,128)(2,1)S(1)} %get-tuple-element.98), channel_id=1, source_target_pairs={{0,4},{1,5},{2,6},{3,7},{4,8},{5,9},{6,10},{7,11},{8,12},{9,13},{1... | collective-permute-start | bytes 393224 | tf_op jit(solution)/shard_map/ppermute | solution.py:29
  116.1 2.0 collective-permute-start.8
  118.2 3.2 collective-permute-done.7.rest_2_
  121.4 2.7 collective-permute-done.9.rest_5_
  124.1 1.4 shard_map.188
  125.9 1.3 collective-permute-start.13
  127.2 1.4 collective-permute-start.14
  128.6 1.8 collective-permute-done.12.p1
  131.5 1.7 shard_map.189
  134.0 2.8 collective-permute-start.16
  136.8 1.5 collective-permute-done.15.p1
  138.3 1.6 collective-permute-done.16.p2
  140.9 4.8 %collective-permute-start.21 = (bf16[16,64,128]{2,1,0:T(8,128)(2,1)S(1)}, bf16[16,64,128]{2,1,0:T(8,128)(2,1)S(1)}, u32[]{:S(2)}, u32[]{:S(2)}) collective-permute-start(bf16[16,64,128]{2,1,0:T(8,128)(2,1)S(1)} %shard_map.190.rest_2_), channel_id=1, source_target_pairs={{0,15},{1,0},{2,1},{3,2},{4,3},{5,4},{6,5},{7,6},{8,7},{9,8},{10,9... | collective-permute-start | bytes 786440 | tf_op jit(solution)/shard_map/ppermute | solution.py:37
  145.7 11.6 %collective-permute-start.20 = (bf16[16,64,128]{2,1,0:T(8,128)(2,1)S(1)}, bf16[16,64,128]{2,1,0:T(8,128)(2,1)S(1)}, u32[]{:S(2)}, u32[]{:S(2)}) collective-permute-start(bf16[16,64,128]{2,1,0:T(8,128)(2,1)S(1)} %shard_map.190.rest_2_), channel_id=1, source_target_pairs={{0,16},{16,0},{32,48},{48,32},{64,80},{80,64},{96,112},{112,96},{1... | collective-permute-start | bytes 786440 | tf_op jit(solution)/shard_map/ppermute | solution.py:23
  157.3 4.3 %collective-permute-start.19 = (bf16[16,64,128]{2,1,0:T(8,128)(2,1)S(1)}, bf16[16,64,128]{2,1,0:T(8,128)(2,1)S(1)}, u32[]{:S(2)}, u32[]{:S(2)}) collective-permute-start(bf16[16,64,128]{2,1,0:T(8,128)(2,1)S(1)} %collective-permute-done.18.rest_0_), channel_id=1, source_target_pairs={{0,16},{16,0},{32,48},{48,32},{64,80},{80,64},{96,112},{112,96},{1... | collective-permute-start | bytes 786440 | tf_op jit(solution)/shard_map/ppermute | solution.py:23
  161.6 1.1 collective-permute-done.19.rest_1_
  163.1 4.3 %shard_map.191 = (f32[16,64,128]{2,1,0:T(8,128)S(1)}, bf16[16,64,128]{2,1,0:T(8,128)(2,1)S(1)}) custom-call(s32[4]{0:T(128)S(1)} %pad_add_fusion.ids, s32[512]{0:T(512)S(1)} %all-reduce.meta, bf16[64,128,128]{2,1,0:T(8,128)(2,1)S(1)} %copy-done.2, bf16[16,64,128]{2,1,0:T(8,128)(2,1)S(1)} %collective-permute-done.18.rest_0_, ...), custom_call_target="tpu_custom_call" | custom-call | tf_op jit(solution)/shard_map/pallas_call | solution.py:41
  167.9 1.2 collective-permute-done.23.other
  169.8 2.1 collective-permute-start.25
  171.9 1.2 collective-permute-start.26
  173.4 1.6 collective-permute-done.24.p1
  176.0 2.1 shard_map.193
  179.1 2.5 collective-permute-start.28
  182.4 1.6 collective-permute-done.28.p2
  184.1 1.3 collective-permute-done.29.p3
  186.0 2.7 collective-permute-start.30
  188.7 1.2 collective-permute-done.30.theirs
  189.8 4.0 %shard_map.195 = (f32[48,64,128]{2,1,0:T(8,128)S(1)}, bf16[48,64,128]{2,1,0:T(8,128)(2,1)S(1)}) custom-call(s32[4]{0:T(128)S(1)} %pad_add_fusion.ids, s32[512]{0:T(512)S(1)} %all-reduce.meta, bf16[64,128,128]{2,1,0:T(8,128)(2,1)S(1)} %copy-done.2, bf16[16,64,128]{2,1,0:T(8,128)(2,1)S(1)} %shard_map.194.mine, ...), custom_call_target="tpu_custom_call" | custom-call | tf_op jit(solution)/shard_map/pallas_call | solution.py:41
  194.3 1.9 collective-permute-done.31.other
  196.3 4.8 %collective-permute-start.32 = (bf16[16,64,128]{2,1,0:T(8,128)(2,1)S(1)}, bf16[16,64,128]{2,1,0:T(8,128)(2,1)S(1)}, u32[]{:S(2)}, u32[]{:S(2)}) collective-permute-start(bf16[16,64,128]{2,1,0:T(8,128)(2,1)S(1)} %get-tuple-element.129), channel_id=1, source_target_pairs={{0,15},{1,0},{2,1},{3,2},{4,3},{5,4},{6,5},{7,6},{8,7},{9,8},{10,9... | collective-permute-start | bytes 786440 | tf_op jit(solution)/shard_map/ppermute | solution.py:37
  201.1 5.3 %collective-permute-done.32.a = bf16[16,64,128]{2,1,0:T(8,128)(2,1)S(1)} collective-permute-done((bf16[16,64,128]{2,1,0:T(8,128)(2,1)S(1)}, bf16[16,64,128]{2,1,0:T(8,128)(2,1)S(1)}, u32[]{:S(2)}, u32[]{:S(2)}) %collective-permute-start.32) | collective-permute-done | bytes 262176 | tf_op jit(solution)/shard_map/ppermute | solution.py:37
  206.4 5.2 %collective-permute-done.33.c = bf16[16,64,128]{2,1,0:T(8,128)(2,1)S(1)} collective-permute-done((bf16[16,64,128]{2,1,0:T(8,128)(2,1)S(1)}, bf16[16,64,128]{2,1,0:T(8,128)(2,1)S(1)}, u32[]{:S(2)}, u32[]{:S(2)}) %collective-permute-start.33) | collective-permute-done | bytes 262176 | tf_op jit(solution)/shard_map/ppermute | solution.py:37
  212.3 2.4 collective-permute-start.35
  216.0 1.4 collective-permute-done.34.p1
  217.9 1.4 shard_map.198
  220.1 2.8 collective-permute-start.38
  223.7 1.6 collective-permute-done.38.p2
  226.8 2.6 collective-permute-start.42
  229.7 3.5 collective-permute-done.40.refs_1_
  233.8 2.4 collective-permute-done.43.refs_5_
  236.1 1.1 collective-permute-done.45.refs_7_
  237.4 2.7 collective-permute-start.47
  240.4 1.8 collective-permute-start.50
  242.2 10.5 %collective-permute-done.46.rest_1_ = bf16[4,16,32,128]{3,2,1,0:T(8,128)(2,1)S(1)} collective-permute-done((bf16[4,16,32,128]{3,2,1,0:T(8,128)(2,1)S(1)}, bf16[4,16,32,128]{3,2,1,0:T(8,128)(2,1)S(1)}, u32[]{:S(2)}, u32[]{:S(2)}) %collective-permute-start.46) | collective-permute-done | bytes 524320 | tf_op jit(solution)/shard_map/ppermute | solution.py:33
  255.3 7.6 %collective-permute-done.51.rest_7_ = bf16[4,16,32,128]{3,2,1,0:T(8,128)(2,1)} collective-permute-done((bf16[4,16,32,128]{3,2,1,0:T(8,128)(2,1)S(1)}, bf16[4,16,32,128]{3,2,1,0:T(8,128)(2,1)}, u32[]{:S(2)}, u32[]{:S(2)}) %collective-permute-start.51) | collective-permute-done | bytes 524320 | tf_op jit(solution)/shard_map/ppermute | solution.py:29
  262.9 5.7 %shard_map.201 = bf16[8,32,64,128]{3,2,1,0:T(8,128)(2,1)} custom-call(s32[4]{0:T(128)S(1)} %pad_add_fusion.ids, s32[512]{0:T(512)S(1)} %all-reduce.meta, bf16[4,16,32,128]{3,2,1,0:T(8,128)(2,1)S(1)} %get-tuple-element.147.rest_0_, bf16[4,16,32,128]{3,2,1,0:T(8,128)(2,1)S(1)} %collective-permute-done.46.rest_1_, ...), custom_call_target="tpu_custom_call" | custom-call | tf_op jit(solution)/shard_map/pallas_call | solution.py:404
  268.6 14.4 %all-to-all-start.1 = ((bf16[8,32,64,128]{3,2,1,0:T(8,128)(2,1)}), bf16[8,32,64,128]{3,2,1,0:T(8,128)(2,1)}, u32[]{:S(2)}, u32[]{:S(2)}) async-start(bf16[8,32,64,128]{3,2,1,0:T(8,128)(2,1)} %shard_map.201), calls=%async_computation.1 | async-start | bytes 8388608 | tf_op jit(solution)/shard_map/all_to_all | solution.py:485
  283.8 3.1 copy.25
  286.9 45.0 %all-to-all-done.1.pieces = bf16[8,32,64,128]{3,2,1,0:T(8,128)(2,1)} async-done(((bf16[8,32,64,128]{3,2,1,0:T(8,128)(2,1)}), bf16[8,32,64,128]{3,2,1,0:T(8,128)(2,1)}, u32[]{:S(2)}, u32[]{:S(2)}) %all-to-all-start.1) | async-done | bytes 4194336 | tf_op jit(solution)/shard_map/all_to_all | solution.py:485
  331.9 8.0 %shard_map.202 = bf16[3072,512]{1,0:T(8,128)(2,1)} custom-call(s32[32]{0:T(128)} %source.3, bf16[512,512]{1,0:T(8,128)(2,1)} %w_send.3, s32[32,128,128]{2,1,0:T(8,128)} %mask.3, bf16[8,32,64,128]{3,2,1,0:T(8,128)(2,1)} %all-to-all-done.1.pieces), custom_call_target="tpu_custom_call" | custom-call | tf_op jit(solution)/shard_map/pallas_call | solution.py:463
  (107 shorter events, 26.5 us)
Async XLA Ops:
  7.2 165.9 %copy-start = (bf16[512,512]{1,0:T(8,128)(2,1)S(1)}, bf16[512,512]{1,0:T(8,128)(2,1)}, u32[]{:S(2)}) copy-start(bf16[512,512]{1,0:T(8,128)(2,1)} %param.26) | copy-start | bytes 1572868
  17.4 57.5 %all-to-all-start = ((bf16[8,32,64,128]{3,2,1,0:T(8,128)(2,1)}), bf16[8,32,64,128]{3,2,1,0:T(8,128)(2,1)}, u32[]{:S(2)}, u32[]{:S(2)}) async-start(bf16[8,32,64,128]{3,2,1,0:T(8,128)(2,1)} %get-tuple-element.78), calls=%async_computation | async-start | bytes 8388608 | tf_op jit(solution)/shard_map/all_to_all | solution.py:485
  24.4 104.2 %all-gather.3.cloned.1.call-start = ((), (), s32[]{:S(2)}) async-start(), calls=%async_computation.2 | async-start | bytes 2621440 | tf_op jit(solution)/shard_map/all_gather | solution.py:534
  74.9 208.8 %all-gather.5.cloned.1.call-start = ((), (), s32[]{:S(2)}) async-start(), calls=%async_computation.3 | async-start | bytes 2359296 | tf_op jit(solution)/shard_map/all_gather | solution.py:592
  79.8 12.9 %collective-permute-start = (bf16[4,16,32,128]{3,2,1,0:T(8,128)(2,1)S(1)}, bf16[4,16,32,128]{3,2,1,0:T(8,128)(2,1)S(1)}, u32[]{:S(2)}, u32[]{:S(2)}) collective-permute-start(bf16[4,16,32,128]{3,2,1,0:T(8,128)(2,1)S(1)} %get-tuple-element.90), channel_id=1, source_target_pairs={{0,1},{1,2},{2,3},{3,0},{4,5},{5,6},{6,7},{7,4},{8,9},{9,10},{10,1... | collective-permute-start | bytes 1572872 | tf_op jit(solution)/shard_map/ppermute | solution.py:33
  81.2 23.8 %collective-permute-start.1 = (bf16[4,16,32,128]{3,2,1,0:T(8,128)(2,1)S(1)}, bf16[4,16,32,128]{3,2,1,0:T(8,128)(2,1)S(1)}, u32[]{:S(2)}, u32[]{:S(2)}) collective-permute-start(bf16[4,16,32,128]{3,2,1,0:T(8,128)(2,1)S(1)} %get-tuple-element.91), channel_id=1, source_target_pairs={{0,2},{1,3},{2,0},{3,1},{4,6},{5,7},{6,4},{7,5},{8,10},{9,11},{10,... | collective-permute-start | bytes 1572872 | tf_op jit(solution)/shard_map/ppermute | solution.py:33
  83.8 22.1 %collective-permute-start.2 = (bf16[4,16,32,128]{3,2,1,0:T(8,128)(2,1)S(1)}, bf16[4,16,32,128]{3,2,1,0:T(8,128)(2,1)S(1)}, u32[]{:S(2)}, u32[]{:S(2)}) collective-permute-start(bf16[4,16,32,128]{3,2,1,0:T(8,128)(2,1)S(1)} %get-tuple-element.92), channel_id=1, source_target_pairs={{0,3},{1,0},{2,1},{3,2},{4,7},{5,4},{6,5},{7,6},{8,11},{9,8},{10,9... | collective-permute-start | bytes 1572872 | tf_op jit(solution)/shard_map/ppermute | solution.py:33
  84.9 21.0 %collective-permute-start.3 = (bf16[4,16,32,128]{3,2,1,0:T(8,128)(2,1)S(1)}, bf16[4,16,32,128]{3,2,1,0:T(8,128)(2,1)S(1)}, u32[]{:S(2)}, u32[]{:S(2)}) collective-permute-start(bf16[4,16,32,128]{3,2,1,0:T(8,128)(2,1)S(1)} %get-tuple-element.94), channel_id=1, source_target_pairs={{0,4},{1,5},{2,6},{3,7},{4,8},{5,9},{6,10},{7,11},{8,12},{9,13},{1... | collective-permute-start | bytes 1572872 | tf_op jit(solution)/shard_map/ppermute | solution.py:29
  86.1 22.8 %collective-permute-start.4 = (bf16[4,16,32,128]{3,2,1,0:T(8,128)(2,1)S(1)}, bf16[4,16,32,128]{3,2,1,0:T(8,128)(2,1)S(1)}, u32[]{:S(2)}, u32[]{:S(2)}) collective-permute-start(bf16[4,16,32,128]{3,2,1,0:T(8,128)(2,1)S(1)} %get-tuple-element.95), channel_id=1, source_target_pairs={{0,8},{1,9},{2,10},{3,11},{4,12},{5,13},{6,14},{7,15},{8,0},{9,1},... | collective-permute-start | bytes 1572872 | tf_op jit(solution)/shard_map/ppermute | solution.py:29
  92.7 16.1 %collective-permute-start.5 = (bf16[4,16,32,128]{3,2,1,0:T(8,128)(2,1)S(1)}, bf16[4,16,32,128]{3,2,1,0:T(8,128)(2,1)S(1)}, u32[]{:S(2)}, u32[]{:S(2)}) collective-permute-start(bf16[4,16,32,128]{3,2,1,0:T(8,128)(2,1)S(1)} %get-tuple-element.96), channel_id=1, source_target_pairs={{0,12},{1,13},{2,14},{3,15},{4,0},{5,1},{6,2},{7,3},{8,4},{9,5},{1... | collective-permute-start | bytes 1572872 | tf_op jit(solution)/shard_map/ppermute | solution.py:29
  108.9 22.6 %copy-start.4 = (bf16[512,512]{1,0:T(8,128)(2,1)S(1)}, bf16[512,512]{1,0:T(8,128)(2,1)}, u32[]{:S(2)}) copy-start(bf16[512,512]{1,0:T(8,128)(2,1)} %w_agg.5) | copy-start | bytes 1572868
  108.9 22.6 %copy-start.5 = (bf16[512,512]{1,0:T(8,128)(2,1)S(1)}, bf16[512,512]{1,0:T(8,128)(2,1)}, u32[]{:S(2)}) copy-start(bf16[512,512]{1,0:T(8,128)(2,1)} %w_out.5) | copy-start | bytes 1572868
  108.9 22.6 %copy-start.6 = (bf16[512,512]{1,0:T(8,128)(2,1)S(1)}, bf16[512,512]{1,0:T(8,128)(2,1)}, u32[]{:S(2)}) copy-start(bf16[512,512]{1,0:T(8,128)(2,1)} %w_pass.3) | copy-start | bytes 1572868
  109.4 8.8 %collective-permute-start.10 = (bf16[16,32,128]{2,1,0:T(8,128)(2,1)S(1)}, bf16[16,32,128]{2,1,0:T(8,128)(2,1)S(1)}, u32[]{:S(2)}, u32[]{:S(2)}) collective-permute-start(bf16[16,32,128]{2,1,0:T(8,128)(2,1)S(1)} %get-tuple-element.103), channel_id=1, source_target_pairs={{0,2},{1,3},{2,0},{3,1},{4,6},{5,7},{6,4},{7,5},{8,10},{9,11},{10,... | collective-permute-start | bytes 393224 | tf_op jit(solution)/shard_map/ppermute | solution.py:33
  109.9 8.3 %collective-permute-start.11 = (bf16[16,32,128]{2,1,0:T(8,128)(2,1)S(1)}, bf16[16,32,128]{2,1,0:T(8,128)(2,1)S(1)}, u32[]{:S(2)}, u32[]{:S(2)}) collective-permute-start(bf16[16,32,128]{2,1,0:T(8,128)(2,1)S(1)} %get-tuple-element.104), channel_id=1, source_target_pairs={{0,3},{1,0},{2,1},{3,2},{4,7},{5,4},{6,5},{7,6},{8,11},{9,8},{10,9... | collective-permute-start | bytes 393224 | tf_op jit(solution)/shard_map/ppermute | solution.py:33
  112.3 5.9 %collective-permute-start.6 = (bf16[16,32,128]{2,1,0:T(8,128)(2,1)S(1)}, bf16[16,32,128]{2,1,0:T(8,128)(2,1)S(1)}, u32[]{:S(2)}, u32[]{:S(2)}) collective-permute-start(bf16[16,32,128]{2,1,0:T(8,128)(2,1)S(1)} %get-tuple-element.98), channel_id=1, source_target_pairs={{0,4},{1,5},{2,6},{3,7},{4,8},{5,9},{6,10},{7,11},{8,12},{9,13},{1... | collective-permute-start | bytes 393224 | tf_op jit(solution)/shard_map/ppermute | solution.py:29
  115.8 5.6 %collective-permute-start.7 = (bf16[16,32,128]{2,1,0:T(8,128)(2,1)S(1)}, bf16[16,32,128]{2,1,0:T(8,128)(2,1)S(1)}, u32[]{:S(2)}, u32[]{:S(2)}) collective-permute-start(bf16[16,32,128]{2,1,0:T(8,128)(2,1)S(1)} %get-tuple-element.99), channel_id=1, source_target_pairs={{0,8},{1,9},{2,10},{3,11},{4,12},{5,13},{6,14},{7,15},{8,0},{9,1},... | collective-permute-start | bytes 393224 | tf_op jit(solution)/shard_map/ppermute | solution.py:29
  116.1 5.3 %collective-permute-start.8 = (bf16[16,32,128]{2,1,0:T(8,128)(2,1)S(1)}, bf16[16,32,128]{2,1,0:T(8,128)(2,1)S(1)}, u32[]{:S(2)}, u32[]{:S(2)}) collective-permute-start(bf16[16,32,128]{2,1,0:T(8,128)(2,1)S(1)} %get-tuple-element.100), channel_id=1, source_target_pairs={{0,12},{1,13},{2,14},{3,15},{4,0},{5,1},{6,2},{7,3},{8,4},{9,5},{1... | collective-permute-start | bytes 393224 | tf_op jit(solution)/shard_map/ppermute | solution.py:29
  118.2 5.9 %collective-permute-start.9 = (bf16[16,32,128]{2,1,0:T(8,128)(2,1)S(1)}, bf16[16,32,128]{2,1,0:T(8,128)(2,1)S(1)}, u32[]{:S(2)}, u32[]{:S(2)}) collective-permute-start(bf16[16,32,128]{2,1,0:T(8,128)(2,1)S(1)} %get-tuple-element.102), channel_id=1, source_target_pairs={{0,1},{1,2},{2,3},{3,0},{4,5},{5,6},{6,7},{7,4},{8,9},{9,10},{10,1... | collective-permute-start | bytes 393224 | tf_op jit(solution)/shard_map/ppermute | solution.py:33
  125.5 4.8 %collective-permute-start.12 = (bf16[4,64,128]{2,1,0:T(8,128)(2,1)}, bf16[4,64,128]{2,1,0:T(8,128)(2,1)S(1)}, u32[]{:S(2)}, u32[]{:S(2)}) collective-permute-start(bf16[4,64,128]{2,1,0:T(8,128)(2,1)} %get-tuple-element.106), channel_id=1, source_target_pairs={{0,32},{16,48},{32,64},{48,80},{64,96},{80,112},{96,0},{112,16},{1... | collective-permute-start | bytes 196616 | tf_op jit(solution)/shard_map/ppermute | solution.py:19
  125.9 5.0 %collective-permute-start.13 = (bf16[4,64,128]{2,1,0:T(8,128)(2,1)}, bf16[4,64,128]{2,1,0:T(8,128)(2,1)}, u32[]{:S(2)}, u32[]{:S(2)}) collective-permute-start(bf16[4,64,128]{2,1,0:T(8,128)(2,1)} %get-tuple-element.107), channel_id=1, source_target_pairs={{0,64},{16,80},{32,96},{48,112},{64,0},{80,16},{96,32},{112,48},{1... | collective-permute-start | bytes 196616 | tf_op jit(solution)/shard_map/ppermute | solution.py:19
  127.2 4.2 %collective-permute-start.14 = (bf16[4,64,128]{2,1,0:T(8,128)(2,1)}, bf16[4,64,128]{2,1,0:T(8,128)(2,1)}, u32[]{:S(2)}, u32[]{:S(2)}) collective-permute-start(bf16[4,64,128]{2,1,0:T(8,128)(2,1)} %get-tuple-element.108), channel_id=1, source_target_pairs={{0,96},{16,112},{32,0},{48,16},{64,32},{80,48},{96,64},{112,80},{1... | collective-permute-start | bytes 196616 | tf_op jit(solution)/shard_map/ppermute | solution.py:19
  128.6 34.6 %copy-start.2 = (bf16[64,128,128]{2,1,0:T(8,128)(2,1)S(1)}, bf16[64,128,128]{2,1,0:T(8,128)(2,1)}, u32[]{:S(2)}) copy-start(bf16[64,128,128]{2,1,0:T(8,128)(2,1)} %all-gather.3.cloned.1.call-done.masks) | copy-start | bytes 6291460
  133.2 5.1 %collective-permute-start.15 = (bf16[4,64,128]{2,1,0:T(8,128)(2,1)S(1)}, bf16[4,64,128]{2,1,0:T(8,128)(2,1)S(1)}, u32[]{:S(2)}, u32[]{:S(2)}) collective-permute-start(bf16[4,64,128]{2,1,0:T(8,128)(2,1)S(1)} %get-tuple-element.112), channel_id=1, source_target_pairs={{0,32},{16,48},{32,64},{48,80},{64,96},{80,112},{96,0},{112,16},{1... | collective-permute-start | bytes 196616 | tf_op jit(solution)/shard_map/ppermute | solution.py:19
  134.0 5.9 %collective-permute-start.16 = (bf16[4,64,128]{2,1,0:T(8,128)(2,1)S(1)}, bf16[4,64,128]{2,1,0:T(8,128)(2,1)S(1)}, u32[]{:S(2)}, u32[]{:S(2)}) collective-permute-start(bf16[4,64,128]{2,1,0:T(8,128)(2,1)S(1)} %get-tuple-element.113), channel_id=1, source_target_pairs={{0,64},{16,80},{32,96},{48,112},{64,0},{80,16},{96,32},{112,48},{1... | collective-permute-start | bytes 196616 | tf_op jit(solution)/shard_map/ppermute | solution.py:19
  136.8 3.4 collective-permute-start.17
  140.8 35.2 %copy-start.7 = (bf16[256,512]{1,0:T(8,128)(2,1)S(1)}, bf16[256,512]{1,0:T(8,128)(2,1)}, u32[]{:S(2)}) copy-start(bf16[256,512]{1,0:T(8,128)(2,1)} %convolution_convert_fusion.g_hidden) | copy-start | bytes 786436
  140.8 35.1 %copy-start.8 = (bf16[512,512]{1,0:T(8,128)(2,1)S(1)}, bf16[512,512]{1,0:T(8,128)(2,1)}, u32[]{:S(2)}) copy-start(bf16[512,512]{1,0:T(8,128)(2,1)} %w_agg.4) | copy-start | bytes 1572868
  140.8 16.4 %collective-permute-start.18 = (bf16[16,64,128]{2,1,0:T(8,128)(2,1)S(1)}, bf16[16,64,128]{2,1,0:T(8,128)(2,1)S(1)}, u32[]{:S(2)}, u32[]{:S(2)}) collective-permute-start(bf16[16,64,128]{2,1,0:T(8,128)(2,1)S(1)} %shard_map.190.rest_2_), channel_id=1, source_target_pairs={{0,1},{1,2},{2,3},{3,4},{4,5},{5,6},{6,7},{7,8},{8,9},{9,10},{10,1... | collective-permute-start | bytes 786440 | tf_op jit(solution)/shard_map/ppermute | solution.py:37
  140.9 20.7 %collective-permute-start.21 = (bf16[16,64,128]{2,1,0:T(8,128)(2,1)S(1)}, bf16[16,64,128]{2,1,0:T(8,128)(2,1)S(1)}, u32[]{:S(2)}, u32[]{:S(2)}) collective-permute-start(bf16[16,64,128]{2,1,0:T(8,128)(2,1)S(1)} %shard_map.190.rest_2_), channel_id=1, source_target_pairs={{0,15},{1,0},{2,1},{3,2},{4,3},{5,4},{6,5},{7,6},{8,7},{9,8},{10,9... | collective-permute-start | bytes 786440 | tf_op jit(solution)/shard_map/ppermute | solution.py:37
  145.7 15.9 %collective-permute-start.20 = (bf16[16,64,128]{2,1,0:T(8,128)(2,1)S(1)}, bf16[16,64,128]{2,1,0:T(8,128)(2,1)S(1)}, u32[]{:S(2)}, u32[]{:S(2)}) collective-permute-start(bf16[16,64,128]{2,1,0:T(8,128)(2,1)S(1)} %shard_map.190.rest_2_), channel_id=1, source_target_pairs={{0,16},{16,0},{32,48},{48,32},{64,80},{80,64},{96,112},{112,96},{1... | collective-permute-start | bytes 786440 | tf_op jit(solution)/shard_map/ppermute | solution.py:23
  157.3 5.5 %collective-permute-start.19 = (bf16[16,64,128]{2,1,0:T(8,128)(2,1)S(1)}, bf16[16,64,128]{2,1,0:T(8,128)(2,1)S(1)}, u32[]{:S(2)}, u32[]{:S(2)}) collective-permute-start(bf16[16,64,128]{2,1,0:T(8,128)(2,1)S(1)} %collective-permute-done.18.rest_0_), channel_id=1, source_target_pairs={{0,16},{16,0},{32,48},{48,32},{64,80},{80,64},{96,112},{112,96},{1... | collective-permute-start | bytes 786440 | tf_op jit(solution)/shard_map/ppermute | solution.py:23
  161.6 1.5 collective-permute-start.22
  167.5 1.6 collective-permute-start.23
  169.7 5.2 %collective-permute-start.24 = (bf16[4,64,128]{2,1,0:T(8,128)(2,1)S(1)}, bf16[4,64,128]{2,1,0:T(8,128)(2,1)S(1)}, u32[]{:S(2)}, u32[]{:S(2)}) collective-permute-start(bf16[4,64,128]{2,1,0:T(8,128)(2,1)S(1)} %get-tuple-element.118), channel_id=1, source_target_pairs={{0,32},{16,48},{32,64},{48,80},{64,96},{80,112},{96,0},{112,16},{1... | collective-permute-start | bytes 196616 | tf_op jit(solution)/shard_map/ppermute | solution.py:19
  169.8 5.7 %collective-permute-start.25 = (bf16[4,64,128]{2,1,0:T(8,128)(2,1)S(1)}, bf16[4,64,128]{2,1,0:T(8,128)(2,1)S(1)}, u32[]{:S(2)}, u32[]{:S(2)}) collective-permute-start(bf16[4,64,128]{2,1,0:T(8,128)(2,1)S(1)} %get-tuple-element.119), channel_id=1, source_target_pairs={{0,64},{16,80},{32,96},{48,112},{64,0},{80,16},{96,32},{112,48},{1... | collective-permute-start | bytes 196616 | tf_op jit(solution)/shard_map/ppermute | solution.py:19
  171.9 4.1 %collective-permute-start.26 = (bf16[4,64,128]{2,1,0:T(8,128)(2,1)S(1)}, bf16[4,64,128]{2,1,0:T(8,128)(2,1)S(1)}, u32[]{:S(2)}, u32[]{:S(2)}) collective-permute-start(bf16[4,64,128]{2,1,0:T(8,128)(2,1)S(1)} %get-tuple-element.120), channel_id=1, source_target_pairs={{0,96},{16,112},{32,0},{48,16},{64,32},{80,48},{96,64},{112,80},{1... | collective-permute-start | bytes 196616 | tf_op jit(solution)/shard_map/ppermute | solution.py:19
  178.1 4.3 %collective-permute-start.27 = (bf16[4,64,128]{2,1,0:T(8,128)(2,1)S(1)}, bf16[4,64,128]{2,1,0:T(8,128)(2,1)S(1)}, u32[]{:S(2)}, u32[]{:S(2)}) collective-permute-start(bf16[4,64,128]{2,1,0:T(8,128)(2,1)S(1)} %get-tuple-element.124), channel_id=1, source_target_pairs={{0,32},{16,48},{32,64},{48,80},{64,96},{80,112},{96,0},{112,16},{1... | collective-permute-start | bytes 196616 | tf_op jit(solution)/shard_map/ppermute | solution.py:19
  179.1 4.9 %collective-permute-start.28 = (bf16[4,64,128]{2,1,0:T(8,128)(2,1)S(1)}, bf16[4,64,128]{2,1,0:T(8,128)(2,1)S(1)}, u32[]{:S(2)}, u32[]{:S(2)}) collective-permute-start(bf16[4,64,128]{2,1,0:T(8,128)(2,1)S(1)} %get-tuple-element.125), channel_id=1, source_target_pairs={{0,64},{16,80},{32,96},{48,112},{64,0},{80,16},{96,32},{112,48},{1... | collective-permute-start | bytes 196616 | tf_op jit(solution)/shard_map/ppermute | solution.py:19
  181.7 3.7 %collective-permute-start.29 = (bf16[4,64,128]{2,1,0:T(8,128)(2,1)S(1)}, bf16[4,64,128]{2,1,0:T(8,128)(2,1)S(1)}, u32[]{:S(2)}, u32[]{:S(2)}) collective-permute-start(bf16[4,64,128]{2,1,0:T(8,128)(2,1)S(1)} %get-tuple-element.126), channel_id=1, source_target_pairs={{0,96},{16,112},{32,0},{48,16},{64,32},{80,48},{96,64},{112,80},{1... | collective-permute-start | bytes 196616 | tf_op jit(solution)/shard_map/ppermute | solution.py:19
  186.0 3.9 %collective-permute-start.30 = (bf16[16,64,128]{2,1,0:T(8,128)(2,1)S(1)}, bf16[16,64,128]{2,1,0:T(8,128)(2,1)S(1)}, u32[]{:S(2)}, u32[]{:S(2)}) collective-permute-start(bf16[16,64,128]{2,1,0:T(8,128)(2,1)S(1)} %shard_map.194.mine), channel_id=1, source_target_pairs={{0,16},{16,0},{32,48},{48,32},{64,80},{80,64},{96,112},{112,96},{1... | collective-permute-start | bytes 786440 | tf_op jit(solution)/shard_map/ppermute | solution.py:23
  193.8 21.8 %copy-start.10 = (bf16[1,4,1,64,512]{4,3,2,1,0:T(8,128)(2,1)S(1)}, bf16[1,4,1,64,512]{4,3,2,1,0:T(8,128)(2,1)}, u32[]{:S(2)}) copy-start(bf16[1,4,1,64,512]{4,3,2,1,0:T(8,128)(2,1)} %copy-done.9) | copy-start | bytes 786436
  193.8 2.4 collective-permute-start.31
  196.3 10.1 %collective-permute-start.32 = (bf16[16,64,128]{2,1,0:T(8,128)(2,1)S(1)}, bf16[16,64,128]{2,1,0:T(8,128)(2,1)S(1)}, u32[]{:S(2)}, u32[]{:S(2)}) collective-permute-start(bf16[16,64,128]{2,1,0:T(8,128)(2,1)S(1)} %get-tuple-element.129), channel_id=1, source_target_pairs={{0,15},{1,0},{2,1},{3,2},{4,3},{5,4},{6,5},{7,6},{8,7},{9,8},{10,9... | collective-permute-start | bytes 786440 | tf_op jit(solution)/shard_map/ppermute | solution.py:37
  201.1 10.5 %collective-permute-start.33 = (bf16[16,64,128]{2,1,0:T(8,128)(2,1)S(1)}, bf16[16,64,128]{2,1,0:T(8,128)(2,1)S(1)}, u32[]{:S(2)}, u32[]{:S(2)}) collective-permute-start(bf16[16,64,128]{2,1,0:T(8,128)(2,1)S(1)} %get-tuple-element.131), channel_id=1, source_target_pairs={{0,1},{1,2},{2,3},{3,4},{4,5},{5,6},{6,7},{7,8},{8,9},{9,10},{10,1... | collective-permute-start | bytes 786440 | tf_op jit(solution)/shard_map/ppermute | solution.py:37
  212.2 5.1 %collective-permute-start.34 = (bf16[4,64,128]{2,1,0:T(8,128)(2,1)S(1)}, bf16[4,64,128]{2,1,0:T(8,128)(2,1)S(1)}, u32[]{:S(2)}, u32[]{:S(2)}) collective-permute-start(bf16[4,64,128]{2,1,0:T(8,128)(2,1)S(1)} %get-tuple-element.133), channel_id=1, source_target_pairs={{0,32},{16,48},{32,64},{48,80},{64,96},{80,112},{96,0},{112,16},{1... | collective-permute-start | bytes 196616 | tf_op jit(solution)/shard_map/ppermute | solution.py:19
  212.3 5.0 %collective-permute-start.35 = (bf16[4,64,128]{2,1,0:T(8,128)(2,1)S(1)}, bf16[4,64,128]{2,1,0:T(8,128)(2,1)S(1)}, u32[]{:S(2)}, u32[]{:S(2)}) collective-permute-start(bf16[4,64,128]{2,1,0:T(8,128)(2,1)S(1)} %get-tuple-element.134), channel_id=1, source_target_pairs={{0,64},{16,80},{32,96},{48,112},{64,0},{80,16},{96,32},{112,48},{1... | collective-permute-start | bytes 196616 | tf_op jit(solution)/shard_map/ppermute | solution.py:19
  214.7 3.2 collective-permute-start.36
  219.3 4.4 %collective-permute-start.37 = (bf16[4,64,128]{2,1,0:T(8,128)(2,1)S(1)}, bf16[4,64,128]{2,1,0:T(8,128)(2,1)S(1)}, u32[]{:S(2)}, u32[]{:S(2)}) collective-permute-start(bf16[4,64,128]{2,1,0:T(8,128)(2,1)S(1)} %get-tuple-element.140), channel_id=1, source_target_pairs={{0,32},{16,48},{32,64},{48,80},{64,96},{80,112},{96,0},{112,16},{1... | collective-permute-start | bytes 196616 | tf_op jit(solution)/shard_map/ppermute | solution.py:19
  220.1 5.2 %collective-permute-start.38 = (bf16[4,64,128]{2,1,0:T(8,128)(2,1)S(1)}, bf16[4,64,128]{2,1,0:T(8,128)(2,1)S(1)}, u32[]{:S(2)}, u32[]{:S(2)}) collective-permute-start(bf16[4,64,128]{2,1,0:T(8,128)(2,1)S(1)} %get-tuple-element.141), channel_id=1, source_target_pairs={{0,64},{16,80},{32,96},{48,112},{64,0},{80,16},{96,32},{112,48},{1... | collective-permute-start | bytes 196616 | tf_op jit(solution)/shard_map/ppermute | solution.py:19
  223.0 3.1 collective-permute-start.39
  226.6 6.5 %collective-permute-start.40 = (bf16[16,32,128]{2,1,0:T(8,128)(2,1)S(1)}, bf16[16,32,128]{2,1,0:T(8,128)(2,1)S(1)}, u32[]{:S(2)}, u32[]{:S(2)}) collective-permute-start(bf16[16,32,128]{2,1,0:T(8,128)(2,1)S(1)} %get-tuple-element.145.refs_0_), channel_id=1, source_target_pairs={{0,4},{1,5},{2,6},{3,7},{4,8},{5,9},{6,10},{7,11},{8,12},{9,13},{1... | collective-permute-start | bytes 393224 | tf_op jit(solution)/shard_map/ppermute | solution.py:29
  226.7 6.4 %collective-permute-start.41 = (bf16[16,32,128]{2,1,0:T(8,128)(2,1)S(1)}, bf16[16,32,128]{2,1,0:T(8,128)(2,1)S(1)}, u32[]{:S(2)}, u32[]{:S(2)}) collective-permute-start(bf16[16,32,128]{2,1,0:T(8,128)(2,1)S(1)} %get-tuple-element.145.refs_0_), channel_id=1, source_target_pairs={{0,8},{1,9},{2,10},{3,11},{4,12},{5,13},{6,14},{7,15},{8,0},{9,1},... | collective-permute-start | bytes 393224 | tf_op jit(solution)/shard_map/ppermute | solution.py:29
  226.8 6.9 %collective-permute-start.42 = (bf16[16,32,128]{2,1,0:T(8,128)(2,1)S(1)}, bf16[16,32,128]{2,1,0:T(8,128)(2,1)S(1)}, u32[]{:S(2)}, u32[]{:S(2)}) collective-permute-start(bf16[16,32,128]{2,1,0:T(8,128)(2,1)S(1)} %get-tuple-element.145.refs_0_), channel_id=1, source_target_pairs={{0,12},{1,13},{2,14},{3,15},{4,0},{5,1},{6,2},{7,3},{8,4},{9,5},{1... | collective-permute-start | bytes 393224 | tf_op jit(solution)/shard_map/ppermute | solution.py:29
  229.4 6.7 %collective-permute-start.43 = (bf16[16,32,128]{2,1,0:T(8,128)(2,1)S(1)}, bf16[16,32,128]{2,1,0:T(8,128)(2,1)S(1)}, u32[]{:S(2)}, u32[]{:S(2)}) collective-permute-start(bf16[16,32,128]{2,1,0:T(8,128)(2,1)S(1)} %get-tuple-element.146.refs_4_), channel_id=1, source_target_pairs={{0,1},{1,2},{2,3},{3,0},{4,5},{5,6},{6,7},{7,4},{8,9},{9,10},{10,1... | collective-permute-start | bytes 393224 | tf_op jit(solution)/shard_map/ppermute | solution.py:33
  229.4 6.7 %collective-permute-start.44 = (bf16[16,32,128]{2,1,0:T(8,128)(2,1)S(1)}, bf16[16,32,128]{2,1,0:T(8,128)(2,1)S(1)}, u32[]{:S(2)}, u32[]{:S(2)}) collective-permute-start(bf16[16,32,128]{2,1,0:T(8,128)(2,1)S(1)} %get-tuple-element.146.refs_4_), channel_id=1, source_target_pairs={{0,2},{1,3},{2,0},{3,1},{4,6},{5,7},{6,4},{7,5},{8,10},{9,11},{10,... | collective-permute-start | bytes 393224 | tf_op jit(solution)/shard_map/ppermute | solution.py:33
  233.1 4.1 %collective-permute-start.45 = (bf16[16,32,128]{2,1,0:T(8,128)(2,1)S(1)}, bf16[16,32,128]{2,1,0:T(8,128)(2,1)S(1)}, u32[]{:S(2)}, u32[]{:S(2)}) collective-permute-start(bf16[16,32,128]{2,1,0:T(8,128)(2,1)S(1)} %get-tuple-element.146.refs_4_), channel_id=1, source_target_pairs={{0,3},{1,0},{2,1},{3,2},{4,7},{5,4},{6,5},{7,6},{8,11},{9,8},{10,9... | collective-permute-start | bytes 393224 | tf_op jit(solution)/shard_map/ppermute | solution.py:33
  237.3 15.4 %collective-permute-start.46 = (bf16[4,16,32,128]{3,2,1,0:T(8,128)(2,1)S(1)}, bf16[4,16,32,128]{3,2,1,0:T(8,128)(2,1)S(1)}, u32[]{:S(2)}, u32[]{:S(2)}) collective-permute-start(bf16[4,16,32,128]{3,2,1,0:T(8,128)(2,1)S(1)} %get-tuple-element.147.rest_0_), channel_id=1, source_target_pairs={{0,1},{1,2},{2,3},{3,0},{4,5},{5,6},{6,7},{7,4},{8,9},{9,10},{10,1... | collective-permute-start | bytes 1572872 | tf_op jit(solution)/shard_map/ppermute | solution.py:33
  237.4 16.0 %collective-permute-start.47 = (bf16[4,16,32,128]{3,2,1,0:T(8,128)(2,1)S(1)}, bf16[4,16,32,128]{3,2,1,0:T(8,128)(2,1)S(1)}, u32[]{:S(2)}, u32[]{:S(2)}) collective-permute-start(bf16[4,16,32,128]{3,2,1,0:T(8,128)(2,1)S(1)} %get-tuple-element.147.rest_0_), channel_id=1, source_target_pairs={{0,2},{1,3},{2,0},{3,1},{4,6},{5,7},{6,4},{7,5},{8,10},{9,11},{10,... | collective-permute-start | bytes 1572872 | tf_op jit(solution)/shard_map/ppermute | solution.py:33
  240.1 14.4 %collective-permute-start.48 = (bf16[4,16,32,128]{3,2,1,0:T(8,128)(2,1)S(1)}, bf16[4,16,32,128]{3,2,1,0:T(8,128)(2,1)S(1)}, u32[]{:S(2)}, u32[]{:S(2)}) collective-permute-start(bf16[4,16,32,128]{3,2,1,0:T(8,128)(2,1)S(1)} %get-tuple-element.147.rest_0_), channel_id=1, source_target_pairs={{0,3},{1,0},{2,1},{3,2},{4,7},{5,4},{6,5},{7,6},{8,11},{9,8},{10,9... | collective-permute-start | bytes 1572872 | tf_op jit(solution)/shard_map/ppermute | solution.py:33
  240.1 15.2 %collective-permute-start.49 = (bf16[4,16,32,128]{3,2,1,0:T(8,128)(2,1)S(1)}, bf16[4,16,32,128]{3,2,1,0:T(8,128)(2,1)S(1)}, u32[]{:S(2)}, u32[]{:S(2)}) collective-permute-start(bf16[4,16,32,128]{3,2,1,0:T(8,128)(2,1)S(1)} %get-tuple-element.148.rest_4_), channel_id=1, source_target_pairs={{0,4},{1,5},{2,6},{3,7},{4,8},{5,9},{6,10},{7,11},{8,12},{9,13},{1... | collective-permute-start | bytes 1572872 | tf_op jit(solution)/shard_map/ppermute | solution.py:29
  240.4 14.9 %collective-permute-start.50 = (bf16[4,16,32,128]{3,2,1,0:T(8,128)(2,1)S(1)}, bf16[4,16,32,128]{3,2,1,0:T(8,128)(2,1)}, u32[]{:S(2)}, u32[]{:S(2)}) collective-permute-start(bf16[4,16,32,128]{3,2,1,0:T(8,128)(2,1)S(1)} %get-tuple-element.148.rest_4_), channel_id=1, source_target_pairs={{0,8},{1,9},{2,10},{3,11},{4,12},{5,13},{6,14},{7,15},{8,0},{9,1},... | collective-permute-start | bytes 1572872 | tf_op jit(solution)/shard_map/ppermute | solution.py:29
  252.7 10.1 %collective-permute-start.51 = (bf16[4,16,32,128]{3,2,1,0:T(8,128)(2,1)S(1)}, bf16[4,16,32,128]{3,2,1,0:T(8,128)(2,1)}, u32[]{:S(2)}, u32[]{:S(2)}) collective-permute-start(bf16[4,16,32,128]{3,2,1,0:T(8,128)(2,1)S(1)} %get-tuple-element.148.rest_4_), channel_id=1, source_target_pairs={{0,12},{1,13},{2,14},{3,15},{4,0},{5,1},{6,2},{7,3},{8,4},{9,5},{1... | collective-permute-start | bytes 1572872 | tf_op jit(solution)/shard_map/ppermute | solution.py:29
  268.6 63.3 %all-to-all-start.1 = ((bf16[8,32,64,128]{3,2,1,0:T(8,128)(2,1)}), bf16[8,32,64,128]{3,2,1,0:T(8,128)(2,1)}, u32[]{:S(2)}, u32[]{:S(2)}) async-start(bf16[8,32,64,128]{3,2,1,0:T(8,128)(2,1)} %shard_map.201), calls=%async_computation.1 | async-start | bytes 8388608 | tf_op jit(solution)/shard_map/all_to_all | solution.py:485
  (5 other events, 22.1 us)
Sparse Core Ops, SparseCore 0:
  75.1 31.5 all-gather.2
  253.6 30.1 all-gather.4

commit v3 on v2

--- a/solution.py
+++ b/solution.py
@@ -108,8 +108,7 @@
                 m[e].astype(F32).astype(BF16), block, (((0,), (0,)), ((), ())), preferred_element_type=F32
             ).astype(BF16)
             for n in range(8):
-                z, c = n // 2, n % 2
-                msg[n, e] = message[64 * c : 64 * c + 64, 128 * z : 128 * z + 128]
+                msg[n, e] = message[16 * n : 16 * n + 16, :]
         out_to(i).start()
         return 0
 
@@ -127,7 +126,7 @@
     return pl.pallas_call(
         messages_body,
         out_shape=[
-            jax.ShapeDtypeStruct((8, 32, 64, 128), BF16),
+            jax.ShapeDtypeStruct((8, 32, 16, 512), BF16),
             jax.ShapeDtypeStruct((16, 128, 128), BF16),
         ],
         in_specs=[SMEM, HBM, HBM, HBM, HBM],
@@ -138,7 +137,7 @@
             pltpu.VMEM((32, 128, 128), jnp.int32),
             pltpu.VMEM((16, 128, 128), jnp.int32),
             pltpu.VMEM((3072, 512), BF16),
-            pltpu.VMEM((8, 32, 64, 128), BF16),
+            pltpu.VMEM((8, 32, 16, 512), BF16),
             pltpu.VMEM((16, 128, 128), BF16),
             sems(6),
             sems(1),
@@ -163,17 +162,17 @@
     for kx in range(4):
         for ky in range(4):
             at = pl.ds((4 * ((x + kx) & 3) + ((y + ky) & 3)) * 16, 16)
-            outs[ky][kx] = acc[at, :32, :].astype(BF16)
-            outs[4 + kx][ky] = acc[at, 32:, :].astype(BF16)
+            outs[ky][kx] = acc[at, :, :256].astype(BF16)
+            outs[4 + kx][ky] = acc[at, :, 256:].astype(BF16)
 
 
 def combine(ids, meta, arrived):
     outs = local(
         combine_body,
-        [((4, 16, 32, 128), BF16)] * 8,
-        [ids, meta, arrived.reshape(256, 64, 128)],
+        [((4, 16, 16, 256), BF16)] * 8,
+        [ids, meta, arrived.reshape(256, 16, 512)],
         smem=2,
-        scratch=[pltpu.VMEM((256, 64, 128), F32)],
+        scratch=[pltpu.VMEM((256, 16, 512), F32)],
         limit=20,
     )
     return outs[:4], outs[4:]
@@ -191,50 +190,34 @@
 def reduce_halves(by_y, by_x):
     by_y = [by_y[0]] + [over_y(by_y[k], k) for k in (1, 2, 3)]
     by_x = [by_x[0]] + [over_x(by_x[k], k) for k in (1, 2, 3)]
-    sums = local(add_rows_body, [((16, 32, 128), BF16)] * 8, [*by_y, *by_x], smem=0)
+    sums = local(add_rows_body, [((16, 16, 256), BF16)] * 8, [*by_y, *by_x], smem=0)
     left, right = sums[:4], sums[4:]
     left = [left[0]] + [over_x(left[k], k) for k in (1, 2, 3)]
     right = [right[0]] + [over_y(right[k], k) for k in (1, 2, 3)]
     return [*left, *right]
 
 
-def add_last_body(ids, *rest):
-    terms, outs, acc = rest[:8], rest[8:12], rest[12]
+def to_rows(z, pieces, wide):
+    for k in range(4):
+        wide[:, lanes(z - k)] = pieces[k][...].reshape(256, 128)
+    return wide[...]
+
+
+def from_rows(z, wide, outs):
+    for k in range(4):
+        outs[k][...] = wide[:, lanes(z + k)].reshape(16, 16, 128)
+
+
+def enc_mlp_body(ids, *rest):
+    terms, (pre_self, rows, w_agg, w_out, w_pass, pre_ref, first_ref) = rest[:8], rest[8:15]
+    outs, wide = rest[15:19], rest[19]
     z = ids[0]
+    pre = pre_self[...]
     for q in range(2):
         total = terms[4 * q][...].astype(F32)
         for more in terms[4 * q + 1 : 4 * q + 4]:
             total += more[...].astype(F32)
-        acc[:, 32 * q : 32 * q + 32, :] = total.astype(BF16)
-    for k in range(4):
-        outs[k][...] = acc[pl.ds(4 * ((z + k) & 3), 4)]
-
-
-def add_last(ids, terms):
-    return local(
-        add_last_body,
-        [((4, 64, 128), BF16)] * 4,
-        [ids, *terms],
-        scratch=[pltpu.VMEM((16, 64, 128), BF16)],
-    )
-
-
-def to_rows(z, pieces, wide):
-    for k in range(4):
-        wide[:, lanes(z - k)] = pieces[k][...].reshape(256, 128)
-    return wide[...]
-
-
-def from_rows(z, wide, outs):
-    for k in range(4):
-        outs[k][...] = wide[:, lanes(z + k)].reshape(4, 64, 128)
-
-
-def enc_mlp_body(ids, p0, p1, p2, p3, pre_self, rows, w_agg, w_out, w_pass, pre_ref, first_ref, *rest):
-    outs, wide = rest[:4], rest[4]
-    z = ids[0]
-    summed = to_rows(z, (p0, p1, p2, p3), wide)
-    pre = pre_self[...] + dot(summed, w_agg[...])
+        pre += dot(total.astype(BF16).reshape(256, 256), w_agg[256 * q : 256 * q + 256, :])
     pre_ref[...] = pre
     hidden = jax.nn.silu(pre).astype(BF16)
     first = (rows[...].astype(F32) + dot(hidden, w_out[...])).astype(BF16)
@@ -256,41 +239,34 @@
     out_ref[...] = (rows[...].astype(F32) + dot(hidden, w_out[...])).astype(BF16)
 
 
-def enc_back_body(ids, p0, p1, p2, p3, g_part, pre, w_pass, w_out, w_agg, *rest):
-    outs, wide = rest[:4], rest[4]
+def enc_back_body(ids, p0, p1, p2, p3, g_part, pre, w_pass, w_out, w_agg, left, right, wide):
     z = ids[0]
     g_pass = to_rows(z, (p0, p1, p2, p3), wide)
     g_first = (g_part[...] + dot_t(g_pass, w_pass[...])).astype(BF16)
     g_hidden = dot_t(g_first, w_out[...]).astype(BF16)
     g_pre = (g_hidden.astype(F32) * silu_slope(pre[...])).astype(BF16)
-    wide[...] = dot_t(g_pre, w_agg[...]).astype(BF16)
-    from_rows(z, wide, outs)
+    g_agg = dot_t(g_pre, w_agg[...]).astype(BF16)
+    left[...] = g_agg[:, :256].reshape(16, 16, 256)
+    right[...] = g_agg[:, 256:].reshape(16, 16, 256)
 
 
 ROWS = ((256, 512), BF16)
 ROWS32 = ((256, 512), F32)
-PIECE = ((4, 64, 128), BF16)
+PIECE = ((16, 16, 128), BF16)
 WIDE = pltpu.VMEM((256, 512), BF16)
+
+
+def band(z):
+    return pl.ds(pl.multiple_of((z & 3) * 16, 16), 16)
 
 
 def table_body(ids, p0, p1, p2, p3, out):
     for k, piece in enumerate((p0, p1, p2, p3)):
-        out[pl.ds(4 * ((ids[0] - k) & 3), 4)] = piece[...]
+        out[:, band(ids[0] - k), :] = piece[...]
 
 
 def table(ids, pieces):
     return local(table_body, [((16, 64, 128), BF16)], [ids, *pieces])[0]
-
-
-def halves_body(ids, p0, p1, p2, p3, left, right):
-    for k, piece in enumerate((p0, p1, p2, p3)):
-        at = pl.ds(4 * ((ids[0] - k) & 3), 4)
-        left[at] = piece[:, :32, :]
-        right[at] = piece[:, 32:, :]
-
-
-def halves(ids, pieces):
-    return local(halves_body, [((16, 32, 128), BF16)] * 2, [ids, *pieces])
 
 
 def stack_body(*refs):
@@ -302,7 +278,7 @@
 def gather_halves(left, right):
     left = [left] + [over_x(left, k) for k in (1, 2, 3)]
     right = [right] + [over_y(right, k) for k in (1, 2, 3)]
-    left, right = local(stack_body, [((4, 16, 32, 128), BF16)] * 2, [*left, *right], smem=0)
+    left, right = local(stack_body, [((4, 16, 16, 256), BF16)] * 2, [*left, *right], smem=0)
     return [left] + [over_y(left, k) for k in (1, 2, 3)] + [right] + [over_x(right, k) for k in (1, 2, 3)]
 
 
@@ -311,22 +287,38 @@
 
 
 def edge_loop(c, meta, one):
-    def band(n, _):
+    def four(n, _):
         row = (2 * (n >> 2) + c) * 64 + (n & 3) * 4
         one(n * 4, [(meta[row + 32 + e], meta[row + 48 + e]) for e in range(4)])
         return 0
 
-    lax.fori_loop(0, 16, band, 0)
+    lax.fori_loop(0, 16, four, 0)
+
+
+def core_rows(z, c):
+    return pl.ds(pl.multiple_of(32 * z + 16 * c, 16), 16)
+
+
+def join_rows(c, mine, theirs, whole, first):
+    blocks = mine.shape[0]
+    for z in range(4):
+        at = slice(16 * z, 16 * z + 16)
+        whole[first : first + blocks, core_rows(z, c), :] = mine[:, at, :]
+        whole[first : first + blocks, core_rows(z, 1 - c), :] = theirs[:, at, :]
+
+
+def part_rows(c, whole, own, other):
+    for z in range(4):
+        at = slice(16 * z, 16 * z + 16)
+        own[:, at, :] = whole[:, core_rows(z, c), :]
+        other[:, at, :] = whole[:, core_rows(z, 1 - c), :].astype(BF16)
 
 
 def proc_body(ids, meta, masks, *rest):
     tables, (own, other, ext, acc) = rest[:6], rest[6:]
     c = ids[1]
-    at_own = pl.ds(pl.multiple_of(64 * c, 64), 64)
-    at_other = pl.ds(pl.multiple_of(64 * (1 - c), 64), 64)
     for k in range(3):
-        ext[16 * k : 16 * k + 16, at_own, :] = tables[2 * k][...]
-        ext[16 * k : 16 * k + 16, at_other, :] = tables[2 * k + 1][...]
+        join_rows(c, tables[2 * k], tables[2 * k + 1], ext, 16 * k)
     acc[...] = jnp.zeros_like(acc)
 
     def one(base, edges):
@@ -338,16 +330,12 @@
             acc[target] += term
 
     edge_loop(c, meta, one)
-    own[...] = acc[:, at_own, :]
-    other[...] = acc[:, at_other, :].astype(BF16)
+    part_rows(c, acc, own, other)
 
 
 def proc_back_body(ids, meta, masks, mine, theirs, own, other, grads, acc):
     c = ids[1]
-    at_own = pl.ds(pl.multiple_of(64 * c, 64), 64)
-    at_other = pl.ds(pl.multiple_of(64 * (1 - c), 64), 64)
-    grads[:, at_own, :] = mine[...]
-    grads[:, at_other, :] = theirs[...]
+    join_rows(c, mine, theirs, grads, 0)
     acc[...] = jnp.zeros_like(acc)
 
     def one(base, edges):
@@ -356,14 +344,13 @@
             acc[source] += term
 
     edge_loop(c, meta, one)
-    own[...] = acc[:, at_own, :]
-    other[...] = acc[:, at_other, :].astype(BF16)
+    part_rows(c, acc, own, other)
 
 
 def pair_sum_body(ids, own, other, *outs):
     for k in range(4):
-        at = pl.ds(4 * ((ids[0] + k) & 3), 4)
-        outs[k][...] = (own[at] + other[at].astype(F32)).astype(BF16)
+        at = band(ids[0] + k)
+        outs[k][...] = (own[:, at, :] + other[:, at, :].astype(F32)).astype(BF16)
 
 
 def part_sum_body(own, other, *outs):
@@ -374,40 +361,48 @@
 
 def three_sum_body(ids, a, b, c, *outs):
     for k in range(4):
-        at = pl.ds(4 * ((ids[0] + k) & 3), 4)
-        outs[k][...] = (a[at].astype(F32) + b[at].astype(F32) + c[at].astype(F32)).astype(BF16)
+        at = band(ids[0] + k)
+        total = a[:, at, :].astype(F32) + b[:, at, :].astype(F32) + c[:, at, :].astype(F32)
+        outs[k][...] = total.astype(BF16)
 
 
 def fetch_body(ids, meta, *rest):
-    parts, out, tab = rest[:8], rest[8], rest[9]
-    x, y, owner = ids[2], ids[3], pl.program_id(0)
-
-    @pl.when(owner == 0)
-    def _():
-        for kx in range(4):
-            for ky in range(4):
-                at = (kx * 4 + ky) * 16
-                tab[at : at + 16, :32, :] = parts[ky][kx]
-                tab[at : at + 16, 32:, :] = parts[4 + kx][ky]
-
-    def take(e, _):
-        slot = meta[owner * 64 + e]
-        kx = (x - (slot >> 6)) & 3
-        ky = (y - ((slot >> 4) & 3)) & 3
-        out[0, e] = tab[(kx * 4 + ky) * 16 + (slot & 15)]
+    parts, (out, tab, picked, sems) = rest[:8], rest[8:]
+    x, y = ids[2], ids[3]
+    for kx in range(4):
+        for ky in range(4):
+            at = (kx * 4 + ky) * 16
+            tab[at : at + 16, :, :256] = parts[ky][kx]
+            tab[at : at + 16, :, 256:] = parts[4 + kx][ky]
+
+    def out_to(i):
+        return move(picked.at[i], out.at[i], sems, i)
+
+    def owner(i, _):
+        for e in range(32):
+            slot = meta[i * 64 + e]
+            kx = (x - (slot >> 6)) & 3
+            ky = (y - ((slot >> 4) & 3)) & 3
+            picked[i, e] = tab[(kx * 4 + ky) * 16 + (slot & 15)]
+        out_to(i).start()
         return 0
 
-    lax.fori_loop(0, 32, take, 0, unroll=4)
+    lax.fori_loop(0, 8, owner, 0)
+    for i in range(8):
+        out_to(i).wait()
 
 
 def fetch(ids, meta, parts):
     return pl.pallas_call(
         fetch_body,
-        grid=(8,),
-        out_shape=jax.ShapeDtypeStruct((8, 32, 64, 128), BF16),
+        out_shape=jax.ShapeDtypeStruct((8, 32, 16, 512), BF16),
         in_specs=[SMEM, SMEM] + [VMEM] * 8,
-        out_specs=pl.BlockSpec((1, 32, 64, 128), lambda i: (i, 0, 0, 0)),
-        scratch_shapes=[pltpu.VMEM((256, 64, 128), BF16)],
+        out_specs=HBM,
+        scratch_shapes=[
+            pltpu.VMEM((256, 16, 512), BF16),
+            pltpu.VMEM((8, 32, 16, 512), BF16),
+            pltpu.SemaphoreType.DMA((8,)),
+        ],
         compiler_params=pltpu.CompilerParams(vmem_limit_bytes=48 * MIB),
     )(ids, meta, *parts)
 
@@ -436,8 +431,7 @@
         for k in range(8):
             e = i * 8 + k
             for n in range(8):
-                z, c = n // 2, n % 2
-                wide[k, 64 * c : 64 * c + 64, 128 * z : 128 * z + 128] = p[n, e]
+                wide[k, 16 * n : 16 * n + 16, :] = p[n, e]
         for k in range(8):
             e = i * 8 + k
             at = pl.ds(pl.multiple_of(source[e] * 128, 128), 128)
@@ -468,7 +462,7 @@
         scratch_shapes=[
             pltpu.VMEM((512, 512), BF16),
             pltpu.VMEM((32, 128, 128), jnp.int32),
-            pltpu.VMEM((8, 32, 64, 128), BF16),
+            pltpu.VMEM((8, 32, 16, 512), BF16),
             pltpu.VMEM((3072, 512), F32),
             pltpu.VMEM((8, 128, 512), BF16),
             pltpu.VMEM((3072, 512), BF16),
@@ -485,9 +479,8 @@
     return lax.all_to_all(pieces, "grid", 0, 0, tiled=True)
 
 
-def own_rows(array, z, c):
-    cut = lax.dynamic_slice(array.reshape(4, 4, 2, 64, 512), (z, 0, c, 0, 0), (1, 4, 1, 64, 512))
-    return cut.reshape(256, 512)
+def own_rows(array, g):
+    return lax.dynamic_index_in_dim(array.reshape(16, 8, 16, 512), g, 1, False).reshape(256, 512)
 
 
 def per_device(
@@ -522,8 +515,8 @@
         (messages, labels, mesh_latent, mesh_cotangent)
     )
     arrived = column_exchange(messages)
-    rows = own_rows(mesh_latent, z, c)
-    cotangent = own_rows(mesh_cotangent, z, c)
+    rows = own_rows(mesh_latent, g)
+    cotangent = own_rows(mesh_cotangent, g)
     pre_self = dot(rows, w_self_enc)
     g_hid_proc = dot_t(cotangent, w_out_proc).astype(BF16)
     labels, pre_self, g_hid_proc, rows, cotangent = lax.optimization_barrier(
@@ -538,8 +531,7 @@
         tiled=True,
         axis_index_groups=[[2 * i + j for i in range(4)] for j in range(2)],
     )
-    summed = spread_z(add_last(ids, reduce_halves(*combine(ids, meta, arrived))))
-    masks, pre_self = lax.optimization_barrier((masks, pre_self))
+    summed = reduce_halves(*combine(ids, meta, arrived))
     pre_enc, first, *passed = local(
         enc_mlp_body,
         [ROWS32, ROWS] + [PIECE] * 4,
@@ -547,7 +539,8 @@
         scratch=[WIDE],
     )
 
-    own = table(ids, spread_z(passed))
+    masks, kept = lax.optimization_barrier((masks, passed[0]))
+    own = table(ids, spread_z([kept, *passed[1:]]))
     tables = [over_mesh(own, 1), own, over_mesh(own, -1)]
     both = []
     for one in tables:
@@ -580,17 +573,16 @@
     g_pass = local(
         three_sum_body, [PIECE] * 4, [ids, over_mesh(parts[0], -1), parts[1], over_mesh(parts[2], 1)]
     )
-    g_agg = local(
+    left, right = local(
         enc_back_body,
-        [PIECE] * 4,
+        [((16, 16, 256), BF16)] * 2,
         [ids, *spread_z(g_pass), g_first_part, pre_enc, w_pass, w_out_enc, w_agg_enc],
         scratch=[WIDE],
     )
 
-    left, right = halves(ids, spread_z(g_agg))
     left, out_rows = lax.optimization_barrier((left, out_rows))
-    mesh_out = lax.all_gather(out_rows.reshape(1, 4, 64, 512), "grid", axis=0, tiled=True)
-    mesh_out = jnp.swapaxes(mesh_out.reshape(4, 2, 4, 64, 512), 1, 2).reshape(2048, 512)
+    mesh_out = lax.all_gather(out_rows.reshape(1, 16, 16, 512), "grid", axis=0, tiled=True)
+    mesh_out = jnp.swapaxes(mesh_out, 0, 1).reshape(2048, 512)
     returned = column_exchange(fetch(ids, meta, gather_halves(left, right)))
     returned, mesh_out = lax.optimization_barrier((returned, mesh_out))
     grid_grad = grid_gradient(enc_source, w_send, enc_mask, returned)

time: 347 us -> 326 us (0.939)
  starting transfers between devices: 99.8 us -> 85.5 us
  waiting for transfers between devices: 131 us -> 125 us
  Pallas kernels: 45.7 us -> 41.3 us
    ppermute x12, waiting for transfers between devices: 18.6 us -> 9.91 us  [over_x(): lax.ppermute(array, 'mesh', [(4 * x + y, 4 * ((x + by) % 4) + y) for x in...]
    ppermute x12, waiting for transfers between devices: 32.7 us -> 41 us  [over_y(): lax.ppermute(array, 'mesh', [(4 * x + y, 4 * x + (y + by) % 4) for x in r...]
    ppermute x18 -> x12, starting transfers between devices: 20.7 us -> 13.7 us  [over_z(): lax.ppermute(array, 'grid', [(2 * z + c, 2 * ((z + by) % 4) + c) for z in...]
    ppermute x18 -> x12, waiting for transfers between devices: 17.7 us -> 12.3 us  [over_z(): lax.ppermute(array, 'grid', [(2 * z + c, 2 * ((z + by) % 4) + c) for z in...]
    all_to_all x2, starting transfers between devices: 21.4 us -> 16.3 us  [column_exchange(): return lax.all_to_all(pieces, 'grid', 0, 0, tiled=True)]
    all_to_all x2, waiting for transfers between devices: 45 us -> 40.2 us  [column_exchange(): return lax.all_to_all(pieces, 'grid', 0, 0, tiled=True)]
    all_gather x1, waiting for transfers between devices: 0.79 us -> 5.54 us  [per_device(): lax.all_gather(out_rows.reshape(1, 16, 16, 512), 'grid', axis=0, tiled=True)]
    pallas_call x15 -> x13, Pallas kernels: 23.3 us -> 21.1 us  [local(): pl.pallas_call(body, out_shape=[jax.ShapeDtypeStruct(shape, dtype) for sh...]
  transfers between devices with their start and end apart: 56 -> 50, of which waited for: 40 -> 34; matrix products, arithmetic and copies ran while one was open for 2% -> 2% of each run, Pallas kernels for 4% -> 3%
where the time goes in v3:
time: 326 us; the launch traced here: 325 us
  waiting for transfers between devices  125 us (38%)
  starting transfers between devices  85.5 us (26%)
  blocking collectives  46.5 us (14%)
  Pallas kernels  41.3 us (13%)
  between operations  15.1 us (5%)
  local copies, waits for them, and re-layouts  8.24 us (3%)
    optimization_barrier x1, blocking collectives, per_device(): lax.optimization_barrier((arrived, meta, proc_mask))  46.5 us
    ppermute x12, waiting for transfers between devices, over_y(): lax.ppermute(array, 'mesh', [(4 * x + y, 4 * x + (y + by) % 4) for x in r...  41 us
    all_to_all x2, waiting for transfers between devices, column_exchange(): return lax.all_to_all(pieces, 'grid', 0, 0, tiled=True)  40.2 us
    pallas_call x13, Pallas kernels, local(): pl.pallas_call(body, out_shape=[jax.ShapeDtypeStruct(shape, dtype) for sh...  21.1 us
    ppermute x12, starting transfers between devices, over_x(): lax.ppermute(array, 'mesh', [(4 * x + y, 4 * ((x + by) % 4) + y) for x in...  17.4 us
    ppermute x6, starting transfers between devices, over_column(): lax.ppermute(array, 'grid', [(2 * z + c, 2 * ((z + dz) % 4) + (c ^ dc)) f...  16.9 us
    all_to_all x2, starting transfers between devices, column_exchange(): return lax.all_to_all(pieces, 'grid', 0, 0, tiled=True)  16.3 us
    ppermute x12, starting transfers between devices, over_z(): lax.ppermute(array, 'grid', [(2 * z + c, 2 * ((z + by) % 4) + c) for z in...  13.7 us
  transfers between devices with their start and end apart: 50, of which 34 were waited for; matrix products, arithmetic and copies ran while one was open for 2% of the time, Pallas kernels for 3%

profile of v3, /device:TPU:1, one launch (start us, length us, event | category | flops | bytes accessed | tf_op | source)
XLA Modules:
  0.0 325.5 jit_solution(182239580379214525)
XLA Ops:
  8.7 8.7 %shard_map.185 = (bf16[8,32,16,512]{3,2,1,0:T(8,128)(2,1)}, bf16[16,128,128]{2,1,0:T(8,128)(2,1)}) custom-call(s32[32]{0:T(128)} %source.3, bf16[3072,512]{1,0:T(8,128)(2,1)} %latent.1, bf16[512,512]{1,0:T(8,128)(2,1)} %w_send.3, s32[32,128,128]{2,1,0:T(8,128)} %mask.3, s32[16,128,128]{2,1,0:T(8,128)} %other.1), custom_call_target="tpu_custom_call" | custom-call | tf_op jit(solution)/shard_map/pallas_call | solution.py:126
  17.4 7.0 %all-to-all-start = ((bf16[8,32,16,512]{3,2,1,0:T(8,128)(2,1)}), bf16[8,32,16,512]{3,2,1,0:T(8,128)(2,1)}, u32[]{:S(2)}, u32[]{:S(2)}) async-start(bf16[8,32,16,512]{3,2,1,0:T(8,128)(2,1)} %get-tuple-element.70), calls=%async_computation | async-start | bytes 8388608 | tf_op jit(solution)/shard_map/all_to_all | solution.py:479
  24.4 1.1 constant_dynamic-slice_fusion
  25.6 1.0 convolution_convert_fusion.g_hidden
  28.4 46.5 %all-reduce.meta = s32[512]{0:T(512)S(1)} all-reduce(s32[512]{0:T(512)S(1)} %dynamic-update-slice), channel_id=1, replica_groups=mesh['grid'=8,'mesh'=16] {'grid'}, use_global_device_ids=true, to_apply=%add | all-reduce | flops 512 | bytes 4096 | tf_op jit(solution)/shard_map/optimization_barrier | solution.py:526
  75.1 4.7 %shard_map.186 = (bf16[4,16,16,256]{3,2,1,0:T(8,128)(2,1)S(1)}, bf16[4,16,16,256]{3,2,1,0:T(8,128)(2,1)S(1)}, bf16[4,16,16,256]{3,2,1,0:T(8,128)(2,1)S(1)}, bf16...) custom-call(s32[4]{0:T(128)S(1)} %pad_add_fusion.ids, ...), custom_call_target="tpu_custom_call" | custom-call | tf_op jit(solution)/shard_map/pallas_call | solution.py:41
  79.8 1.4 collective-permute-start
  81.2 2.6 collective-permute-start.1
  83.8 1.1 collective-permute-start.2
  84.9 1.2 collective-permute-start.3
  86.1 2.5 collective-permute-start.4
  88.6 4.2 %collective-permute-done.refs_1_ = bf16[4,16,16,256]{3,2,1,0:T(8,128)(2,1)S(1)} collective-permute-done((bf16[4,16,16,256]{3,2,1,0:T(8,128)(2,1)S(1)}, bf16[4,16,16,256]{3,2,1,0:T(8,128)(2,1)S(1)}, u32[]{:S(2)}, u32[]{:S(2)}) %collective-permute-start) | collective-permute-done | bytes 524320 | tf_op jit(solution)/shard_map/ppermute | solution.py:33
  92.8 2.6 collective-permute-start.5
  95.3 9.7 %collective-permute-done.1.refs_2_ = bf16[4,16,16,256]{3,2,1,0:T(8,128)(2,1)S(1)} collective-permute-done((bf16[4,16,16,256]{3,2,1,0:T(8,128)(2,1)S(1)}, bf16[4,16,16,256]{3,2,1,0:T(8,128)(2,1)S(1)}, u32[]{:S(2)}, u32[]{:S(2)}) %collective-permute-start.1) | collective-permute-done | bytes 524320 | tf_op jit(solution)/shard_map/ppermute | solution.py:33
  105.9 3.0 collective-permute-done.4.refs_6_
  109.9 2.4 collective-permute-start.11
  112.3 3.5 %collective-permute-start.6 = (bf16[16,16,256]{2,1,0:T(8,128)(2,1)S(1)}, bf16[16,16,256]{2,1,0:T(8,128)(2,1)S(1)}, u32[]{:S(2)}, u32[]{:S(2)}) collective-permute-start(bf16[16,16,256]{2,1,0:T(8,128)(2,1)S(1)} %get-tuple-element.88), channel_id=1, source_target_pairs={{0,4},{1,5},{2,6},{3,7},{4,8},{5,9},{6,10},{7,11},{8,12},{9,13},{1... | collective-permute-start | bytes 393224 | tf_op jit(solution)/shard_map/ppermute | solution.py:29
  116.2 2.0 collective-permute-start.8
  118.2 3.2 collective-permute-done.7.rest_2_
  121.4 2.7 collective-permute-done.9.rest_5_
  124.2 2.0 shard_map.188
  128.1 1.3 collective-permute-start.13
  129.3 1.4 collective-permute-start.14
  130.7 1.5 collective-permute-done.12.p1
  134.2 4.8 %collective-permute-start.18 = (bf16[16,64,128]{2,1,0:T(8,128)(2,1)S(1)}, bf16[16,64,128]{2,1,0:T(8,128)(2,1)S(1)}, u32[]{:S(2)}, u32[]{:S(2)}) collective-permute-start(bf16[16,64,128]{2,1,0:T(8,128)(2,1)S(1)} %shard_map.189.rest_2_), channel_id=1, source_target_pairs={{0,15},{1,0},{2,1},{3,2},{4,3},{5,4},{6,5},{7,6},{8,7},{9,8},{10,9... | collective-permute-start | bytes 786440 | tf_op jit(solution)/shard_map/ppermute | solution.py:37
  138.9 9.3 %collective-permute-start.17 = (bf16[16,64,128]{2,1,0:T(8,128)(2,1)S(1)}, bf16[16,64,128]{2,1,0:T(8,128)(2,1)S(1)}, u32[]{:S(2)}, u32[]{:S(2)}) collective-permute-start(bf16[16,64,128]{2,1,0:T(8,128)(2,1)S(1)} %shard_map.189.rest_2_), channel_id=1, source_target_pairs={{0,16},{16,0},{32,48},{48,32},{64,80},{80,64},{96,112},{112,96},{1... | collective-permute-start | bytes 786440 | tf_op jit(solution)/shard_map/ppermute | solution.py:23
  148.3 4.3 %collective-permute-start.16 = (bf16[16,64,128]{2,1,0:T(8,128)(2,1)S(1)}, bf16[16,64,128]{2,1,0:T(8,128)(2,1)S(1)}, u32[]{:S(2)}, u32[]{:S(2)}) collective-permute-start(bf16[16,64,128]{2,1,0:T(8,128)(2,1)S(1)} %collective-permute-done.15.rest_0_), channel_id=1, source_target_pairs={{0,16},{16,0},{32,48},{48,32},{64,80},{80,64},{96,112},{112,96},{1... | collective-permute-start | bytes 786440 | tf_op jit(solution)/shard_map/ppermute | solution.py:23
  152.6 1.1 collective-permute-done.16.rest_1_
  154.1 1.6 copy-done.2
  155.7 4.4 %shard_map.190 = (f32[16,64,128]{2,1,0:T(8,128)S(1)}, bf16[16,64,128]{2,1,0:T(8,128)(2,1)S(1)}) custom-call(s32[4]{0:T(128)S(1)} %pad_add_fusion.ids, s32[512]{0:T(512)S(1)} %all-reduce.meta, bf16[64,128,128]{2,1,0:T(8,128)(2,1)S(1)} %copy-done.2, bf16[16,64,128]{2,1,0:T(8,128)(2,1)S(1)} %collective-permute-done.15.rest_0_, ...), custom_call_target="tpu_custom_call" | custom-call | tf_op jit(solution)/shard_map/pallas_call | solution.py:41
  160.6 1.2 collective-permute-done.20.other
  162.4 1.1 collective-permute-start.21
  163.5 2.7 collective-permute-start.22
  167.0 2.2 collective-permute-done.22.p2
  169.7 1.4 shard_map.192
  171.5 3.1 collective-permute-start.25
  175.5 1.5 collective-permute-done.25.p2
  177.0 1.0 collective-permute-done.26.p3
  178.6 2.4 collective-permute-start.27
  180.9 1.2 collective-permute-done.27.theirs
  182.1 4.1 %shard_map.194 = (f32[48,64,128]{2,1,0:T(8,128)S(1)}, bf16[48,64,128]{2,1,0:T(8,128)(2,1)S(1)}) custom-call(s32[4]{0:T(128)S(1)} %pad_add_fusion.ids, s32[512]{0:T(512)S(1)} %all-reduce.meta, bf16[64,128,128]{2,1,0:T(8,128)(2,1)S(1)} %copy-done.3, bf16[16,64,128]{2,1,0:T(8,128)(2,1)S(1)} %shard_map.193.mine, ...), custom_call_target="tpu_custom_call" | custom-call | tf_op jit(solution)/shard_map/pallas_call | solution.py:41
  186.6 1.9 collective-permute-done.28.other
  188.7 4.8 %collective-permute-start.29 = (bf16[16,64,128]{2,1,0:T(8,128)(2,1)S(1)}, bf16[16,64,128]{2,1,0:T(8,128)(2,1)S(1)}, u32[]{:S(2)}, u32[]{:S(2)}) collective-permute-start(bf16[16,64,128]{2,1,0:T(8,128)(2,1)S(1)} %get-tuple-element.117), channel_id=1, source_target_pairs={{0,15},{1,0},{2,1},{3,2},{4,3},{5,4},{6,5},{7,6},{8,7},{9,8},{10,9... | collective-permute-start | bytes 786440 | tf_op jit(solution)/shard_map/ppermute | solution.py:37
  193.5 5.3 %collective-permute-done.29.a = bf16[16,64,128]{2,1,0:T(8,128)(2,1)S(1)} collective-permute-done((bf16[16,64,128]{2,1,0:T(8,128)(2,1)S(1)}, bf16[16,64,128]{2,1,0:T(8,128)(2,1)S(1)}, u32[]{:S(2)}, u32[]{:S(2)}) %collective-permute-start.29) | collective-permute-done | bytes 262176 | tf_op jit(solution)/shard_map/ppermute | solution.py:37
  198.8 5.2 %collective-permute-done.30.c = bf16[16,64,128]{2,1,0:T(8,128)(2,1)S(1)} collective-permute-done((bf16[16,64,128]{2,1,0:T(8,128)(2,1)S(1)}, bf16[16,64,128]{2,1,0:T(8,128)(2,1)S(1)}, u32[]{:S(2)}, u32[]{:S(2)}) %collective-permute-start.30) | collective-permute-done | bytes 262176 | tf_op jit(solution)/shard_map/ppermute | solution.py:37
  205.5 2.5 collective-permute-start.32
  209.0 1.3 collective-permute-done.32.p2
  210.3 1.0 collective-permute-done.33.p3
  211.3 1.3 shard_map.197
  212.9 2.6 collective-permute-start.36
  216.1 3.1 collective-permute-done.34.refs_1_
  219.8 2.4 collective-permute-done.37.refs_5_
  222.2 1.1 collective-permute-done.39.refs_7_
  223.5 2.7 collective-permute-start.41
  226.5 1.8 collective-permute-start.44
  228.3 4.8 %collective-permute-done.40.rest_1_ = bf16[4,16,16,256]{3,2,1,0:T(8,128)(2,1)S(1)} collective-permute-done((bf16[4,16,16,256]{3,2,1,0:T(8,128)(2,1)S(1)}, bf16[4,16,16,256]{3,2,1,0:T(8,128)(2,1)S(1)}, u32[]{:S(2)}, u32[]{:S(2)}) %collective-permute-start.40) | collective-permute-done | bytes 524320 | tf_op jit(solution)/shard_map/ppermute | solution.py:33
  233.6 10.8 %collective-permute-done.41.rest_2_ = bf16[4,16,16,256]{3,2,1,0:T(8,128)(2,1)S(1)} collective-permute-done((bf16[4,16,16,256]{3,2,1,0:T(8,128)(2,1)S(1)}, bf16[4,16,16,256]{3,2,1,0:T(8,128)(2,1)S(1)}, u32[]{:S(2)}, u32[]{:S(2)}) %collective-permute-start.41) | collective-permute-done | bytes 524320 | tf_op jit(solution)/shard_map/ppermute | solution.py:33
  244.4 4.4 %collective-permute-done.42.rest_3_ = bf16[4,16,16,256]{3,2,1,0:T(8,128)(2,1)S(1)} collective-permute-done((bf16[4,16,16,256]{3,2,1,0:T(8,128)(2,1)S(1)}, bf16[4,16,16,256]{3,2,1,0:T(8,128)(2,1)S(1)}, u32[]{:S(2)}, u32[]{:S(2)}) %collective-permute-start.42) | collective-permute-done | bytes 524320 | tf_op jit(solution)/shard_map/ppermute | solution.py:33
  248.8 3.7 %shard_map.199 = bf16[8,32,16,512]{3,2,1,0:T(8,128)(2,1)} custom-call(s32[4]{0:T(128)S(1)} %pad_add_fusion.ids, s32[512]{0:T(512)S(1)} %all-reduce.meta, bf16[4,16,16,256]{3,2,1,0:T(8,128)(2,1)S(1)} %get-tuple-element.131.rest_0_, bf16[4,16,16,256]{3,2,1,0:T(8,128)(2,1)S(1)} %collective-permute-done.40.rest_1_, ...), custom_call_target="tpu_custom_call" | custom-call | tf_op jit(solution)/shard_map/pallas_call | solution.py:396
  252.5 9.4 %all-to-all-start.1 = ((bf16[8,32,16,512]{3,2,1,0:T(8,128)(2,1)}), bf16[8,32,16,512]{3,2,1,0:T(8,128)(2,1)}, u32[]{:S(2)}, u32[]{:S(2)}) async-start(bf16[8,32,16,512]{3,2,1,0:T(8,128)(2,1)} %shard_map.199), calls=%async_computation.1 | async-start | bytes 8388608 | tf_op jit(solution)/shard_map/all_to_all | solution.py:479
  261.9 5.5 %all-gather.5.cloned.1.call-done = bf16[8,16,16,512]{3,2,1,0:T(8,128)(2,1)} async-done(((bf16[1,16,16,512]{3,2,1,0:T(8,128)(2,1)}), bf16[8,16,16,512]{3,2,1,0:T(8,128)(2,1)}) %all-gather.5.cloned.1.call-update) | async-done | bytes 2097168 | tf_op jit(solution)/shard_map/all_gather | solution.py:584
  267.5 3.1 copy.27
  270.6 40.2 %all-to-all-done.1.pieces = bf16[8,32,16,512]{3,2,1,0:T(8,128)(2,1)} async-done(((bf16[8,32,16,512]{3,2,1,0:T(8,128)(2,1)}), bf16[8,32,16,512]{3,2,1,0:T(8,128)(2,1)}, u32[]{:S(2)}, u32[]{:S(2)}) %all-to-all-start.1) | async-done | bytes 4194336 | tf_op jit(solution)/shard_map/all_to_all | solution.py:479
  310.9 7.8 %shard_map.200 = bf16[3072,512]{1,0:T(8,128)(2,1)} custom-call(s32[32]{0:T(128)} %source.3, bf16[512,512]{1,0:T(8,128)(2,1)} %w_send.3, s32[32,128,128]{2,1,0:T(8,128)} %mask.3, bf16[8,32,16,512]{3,2,1,0:T(8,128)(2,1)} %all-to-all-done.1.pieces), custom_call_target="tpu_custom_call" | custom-call | tf_op jit(solution)/shard_map/pallas_call | solution.py:457
  (105 shorter events, 18.9 us)
Async XLA Ops:
  7.2 159.1 %copy-start = (bf16[512,512]{1,0:T(8,128)(2,1)S(1)}, bf16[512,512]{1,0:T(8,128)(2,1)}, u32[]{:S(2)}) copy-start(bf16[512,512]{1,0:T(8,128)(2,1)} %param.26) | copy-start | bytes 1572868
  17.4 8.2 %copy-start.4 = (bf16[512,512]{1,0:T(8,128)(2,1)S(1)}, bf16[512,512]{1,0:T(8,128)(2,1)}, u32[]{:S(2)}) copy-start(bf16[512,512]{1,0:T(8,128)(2,1)} %w_out.2) | copy-start | bytes 1572868
  17.4 57.5 %all-to-all-start = ((bf16[8,32,16,512]{3,2,1,0:T(8,128)(2,1)}), bf16[8,32,16,512]{3,2,1,0:T(8,128)(2,1)}, u32[]{:S(2)}, u32[]{:S(2)}) async-start(bf16[8,32,16,512]{3,2,1,0:T(8,128)(2,1)} %get-tuple-element.70), calls=%async_computation | async-start | bytes 8388608 | tf_op jit(solution)/shard_map/all_to_all | solution.py:479
  24.4 2.5 copy-start.18
  24.4 106.4 %all-gather.3.cloned.1.call-start = ((), (), s32[]{:S(2)}) async-start(), calls=%async_computation.2 | async-start | bytes 2621440 | tf_op jit(solution)/shard_map/all_gather | solution.py:527
  74.9 192.5 %all-gather.5.cloned.1.call-start = ((), (), s32[]{:S(2)}) async-start(), calls=%async_computation.3 | async-start | bytes 2359296 | tf_op jit(solution)/shard_map/all_gather | solution.py:584
  79.8 12.9 %collective-permute-start = (bf16[4,16,16,256]{3,2,1,0:T(8,128)(2,1)S(1)}, bf16[4,16,16,256]{3,2,1,0:T(8,128)(2,1)S(1)}, u32[]{:S(2)}, u32[]{:S(2)}) collective-permute-start(bf16[4,16,16,256]{3,2,1,0:T(8,128)(2,1)S(1)} %get-tuple-element.80), channel_id=1, source_target_pairs={{0,1},{1,2},{2,3},{3,0},{4,5},{5,6},{6,7},{7,4},{8,9},{9,10},{10,1... | collective-permute-start | bytes 1572872 | tf_op jit(solution)/shard_map/ppermute | solution.py:33
  81.2 23.8 %collective-permute-start.1 = (bf16[4,16,16,256]{3,2,1,0:T(8,128)(2,1)S(1)}, bf16[4,16,16,256]{3,2,1,0:T(8,128)(2,1)S(1)}, u32[]{:S(2)}, u32[]{:S(2)}) collective-permute-start(bf16[4,16,16,256]{3,2,1,0:T(8,128)(2,1)S(1)} %get-tuple-element.81), channel_id=1, source_target_pairs={{0,2},{1,3},{2,0},{3,1},{4,6},{5,7},{6,4},{7,5},{8,10},{9,11},{10,... | collective-permute-start | bytes 1572872 | tf_op jit(solution)/shard_map/ppermute | solution.py:33
  83.8 22.1 %collective-permute-start.2 = (bf16[4,16,16,256]{3,2,1,0:T(8,128)(2,1)S(1)}, bf16[4,16,16,256]{3,2,1,0:T(8,128)(2,1)S(1)}, u32[]{:S(2)}, u32[]{:S(2)}) collective-permute-start(bf16[4,16,16,256]{3,2,1,0:T(8,128)(2,1)S(1)} %get-tuple-element.82), channel_id=1, source_target_pairs={{0,3},{1,0},{2,1},{3,2},{4,7},{5,4},{6,5},{7,6},{8,11},{9,8},{10,9... | collective-permute-start | bytes 1572872 | tf_op jit(solution)/shard_map/ppermute | solution.py:33
  84.9 21.0 %collective-permute-start.3 = (bf16[4,16,16,256]{3,2,1,0:T(8,128)(2,1)S(1)}, bf16[4,16,16,256]{3,2,1,0:T(8,128)(2,1)S(1)}, u32[]{:S(2)}, u32[]{:S(2)}) collective-permute-start(bf16[4,16,16,256]{3,2,1,0:T(8,128)(2,1)S(1)} %get-tuple-element.84), channel_id=1, source_target_pairs={{0,4},{1,5},{2,6},{3,7},{4,8},{5,9},{6,10},{7,11},{8,12},{9,13},{1... | collective-permute-start | bytes 1572872 | tf_op jit(solution)/shard_map/ppermute | solution.py:29
  86.1 22.8 %collective-permute-start.4 = (bf16[4,16,16,256]{3,2,1,0:T(8,128)(2,1)S(1)}, bf16[4,16,16,256]{3,2,1,0:T(8,128)(2,1)S(1)}, u32[]{:S(2)}, u32[]{:S(2)}) collective-permute-start(bf16[4,16,16,256]{3,2,1,0:T(8,128)(2,1)S(1)} %get-tuple-element.85), channel_id=1, source_target_pairs={{0,8},{1,9},{2,10},{3,11},{4,12},{5,13},{6,14},{7,15},{8,0},{9,1},... | collective-permute-start | bytes 1572872 | tf_op jit(solution)/shard_map/ppermute | solution.py:29
  92.8 16.2 %collective-permute-start.5 = (bf16[4,16,16,256]{3,2,1,0:T(8,128)(2,1)S(1)}, bf16[4,16,16,256]{3,2,1,0:T(8,128)(2,1)S(1)}, u32[]{:S(2)}, u32[]{:S(2)}) collective-permute-start(bf16[4,16,16,256]{3,2,1,0:T(8,128)(2,1)S(1)} %get-tuple-element.86), channel_id=1, source_target_pairs={{0,12},{1,13},{2,14},{3,15},{4,0},{5,1},{6,2},{7,3},{8,4},{9,5},{1... | collective-permute-start | bytes 1572872 | tf_op jit(solution)/shard_map/ppermute | solution.py:29
  108.9 15.2 %copy-start.5 = (bf16[512,512]{1,0:T(8,128)(2,1)S(1)}, bf16[512,512]{1,0:T(8,128)(2,1)}, u32[]{:S(2)}) copy-start(bf16[512,512]{1,0:T(8,128)(2,1)} %w_agg.3) | copy-start | bytes 1572868
  108.9 15.2 %copy-start.6 = (bf16[512,512]{1,0:T(8,128)(2,1)S(1)}, bf16[512,512]{1,0:T(8,128)(2,1)}, u32[]{:S(2)}) copy-start(bf16[512,512]{1,0:T(8,128)(2,1)} %w_out.3) | copy-start | bytes 1572868
  108.9 15.3 %copy-start.7 = (bf16[512,512]{1,0:T(8,128)(2,1)S(1)}, bf16[512,512]{1,0:T(8,128)(2,1)}, u32[]{:S(2)}) copy-start(bf16[512,512]{1,0:T(8,128)(2,1)} %w_pass.1) | copy-start | bytes 1572868
  109.5 8.8 %collective-permute-start.10 = (bf16[16,16,256]{2,1,0:T(8,128)(2,1)S(1)}, bf16[16,16,256]{2,1,0:T(8,128)(2,1)S(1)}, u32[]{:S(2)}, u32[]{:S(2)}) collective-permute-start(bf16[16,16,256]{2,1,0:T(8,128)(2,1)S(1)} %get-tuple-element.93), channel_id=1, source_target_pairs={{0,2},{1,3},{2,0},{3,1},{4,6},{5,7},{6,4},{7,5},{8,10},{9,11},{10,... | collective-permute-start | bytes 393224 | tf_op jit(solution)/shard_map/ppermute | solution.py:33
  109.9 8.3 %collective-permute-start.11 = (bf16[16,16,256]{2,1,0:T(8,128)(2,1)S(1)}, bf16[16,16,256]{2,1,0:T(8,128)(2,1)S(1)}, u32[]{:S(2)}, u32[]{:S(2)}) collective-permute-start(bf16[16,16,256]{2,1,0:T(8,128)(2,1)S(1)} %get-tuple-element.94), channel_id=1, source_target_pairs={{0,3},{1,0},{2,1},{3,2},{4,7},{5,4},{6,5},{7,6},{8,11},{9,8},{10,9... | collective-permute-start | bytes 393224 | tf_op jit(solution)/shard_map/ppermute | solution.py:33
  112.3 5.9 %collective-permute-start.6 = (bf16[16,16,256]{2,1,0:T(8,128)(2,1)S(1)}, bf16[16,16,256]{2,1,0:T(8,128)(2,1)S(1)}, u32[]{:S(2)}, u32[]{:S(2)}) collective-permute-start(bf16[16,16,256]{2,1,0:T(8,128)(2,1)S(1)} %get-tuple-element.88), channel_id=1, source_target_pairs={{0,4},{1,5},{2,6},{3,7},{4,8},{5,9},{6,10},{7,11},{8,12},{9,13},{1... | collective-permute-start | bytes 393224 | tf_op jit(solution)/shard_map/ppermute | solution.py:29
  115.8 5.6 %collective-permute-start.7 = (bf16[16,16,256]{2,1,0:T(8,128)(2,1)S(1)}, bf16[16,16,256]{2,1,0:T(8,128)(2,1)S(1)}, u32[]{:S(2)}, u32[]{:S(2)}) collective-permute-start(bf16[16,16,256]{2,1,0:T(8,128)(2,1)S(1)} %get-tuple-element.89), channel_id=1, source_target_pairs={{0,8},{1,9},{2,10},{3,11},{4,12},{5,13},{6,14},{7,15},{8,0},{9,1},... | collective-permute-start | bytes 393224 | tf_op jit(solution)/shard_map/ppermute | solution.py:29
  116.2 5.3 %collective-permute-start.8 = (bf16[16,16,256]{2,1,0:T(8,128)(2,1)S(1)}, bf16[16,16,256]{2,1,0:T(8,128)(2,1)S(1)}, u32[]{:S(2)}, u32[]{:S(2)}) collective-permute-start(bf16[16,16,256]{2,1,0:T(8,128)(2,1)S(1)} %get-tuple-element.90), channel_id=1, source_target_pairs={{0,12},{1,13},{2,14},{3,15},{4,0},{5,1},{6,2},{7,3},{8,4},{9,5},{1... | collective-permute-start | bytes 393224 | tf_op jit(solution)/shard_map/ppermute | solution.py:29
  118.2 6.0 %collective-permute-start.9 = (bf16[16,16,256]{2,1,0:T(8,128)(2,1)S(1)}, bf16[16,16,256]{2,1,0:T(8,128)(2,1)S(1)}, u32[]{:S(2)}, u32[]{:S(2)}) collective-permute-start(bf16[16,16,256]{2,1,0:T(8,128)(2,1)S(1)} %get-tuple-element.92), channel_id=1, source_target_pairs={{0,1},{1,2},{2,3},{3,0},{4,5},{5,6},{6,7},{7,4},{8,9},{9,10},{10,1... | collective-permute-start | bytes 393224 | tf_op jit(solution)/shard_map/ppermute | solution.py:33
  127.7 4.5 %collective-permute-start.12 = (bf16[16,16,128]{2,1,0:T(8,128)(2,1)}, bf16[16,16,128]{2,1,0:T(8,128)(2,1)S(1)}, u32[]{:S(2)}, u32[]{:S(2)}) collective-permute-start(bf16[16,16,128]{2,1,0:T(8,128)(2,1)} %get-tuple-element.100), channel_id=1, source_target_pairs={{0,32},{16,48},{32,64},{48,80},{64,96},{80,112},{96,0},{112,16},{1... | collective-permute-start | bytes 196616 | tf_op jit(solution)/shard_map/ppermute | solution.py:19
  128.1 4.9 %collective-permute-start.13 = (bf16[16,16,128]{2,1,0:T(8,128)(2,1)}, bf16[16,16,128]{2,1,0:T(8,128)(2,1)S(1)}, u32[]{:S(2)}, u32[]{:S(2)}) collective-permute-start(bf16[16,16,128]{2,1,0:T(8,128)(2,1)} %get-tuple-element.101), channel_id=1, source_target_pairs={{0,64},{16,80},{32,96},{48,112},{64,0},{80,16},{96,32},{112,48},{1... | collective-permute-start | bytes 196616 | tf_op jit(solution)/shard_map/ppermute | solution.py:19
  129.3 4.2 %collective-permute-start.14 = (bf16[16,16,128]{2,1,0:T(8,128)(2,1)S(1)}, bf16[16,16,128]{2,1,0:T(8,128)(2,1)S(1)}, u32[]{:S(2)}, u32[]{:S(2)}) collective-permute-start(bf16[16,16,128]{2,1,0:T(8,128)(2,1)S(1)} %get-tuple-element.102), channel_id=1, source_target_pairs={{0,96},{16,112},{32,0},{48,16},{64,32},{80,48},{96,64},{112,80},{1... | collective-permute-start | bytes 196616 | tf_op jit(solution)/shard_map/ppermute | solution.py:19
  133.5 32.8 %copy-start.9 = (bf16[256,512]{1,0:T(8,128)(2,1)S(1)}, bf16[256,512]{1,0:T(8,128)(2,1)}, u32[]{:S(2)}) copy-start(bf16[256,512]{1,0:T(8,128)(2,1)} %copy-done.8) | copy-start | bytes 786436
  133.5 36.2 %copy-start.10 = (bf16[256,512]{1,0:T(8,128)(2,1)S(1)}, bf16[256,512]{1,0:T(8,128)(2,1)}, u32[]{:S(2)}) copy-start(bf16[256,512]{1,0:T(8,128)(2,1)} %convolution_convert_fusion.g_hidden) | copy-start | bytes 786436
  134.1 14.2 %collective-permute-start.15 = (bf16[16,64,128]{2,1,0:T(8,128)(2,1)S(1)}, bf16[16,64,128]{2,1,0:T(8,128)(2,1)S(1)}, u32[]{:S(2)}, u32[]{:S(2)}) collective-permute-start(bf16[16,64,128]{2,1,0:T(8,128)(2,1)S(1)} %shard_map.189.rest_2_), channel_id=1, source_target_pairs={{0,1},{1,2},{2,3},{3,4},{4,5},{5,6},{6,7},{7,8},{8,9},{9,10},{10,1... | collective-permute-start | bytes 786440 | tf_op jit(solution)/shard_map/ppermute | solution.py:37
  134.2 18.5 %collective-permute-start.18 = (bf16[16,64,128]{2,1,0:T(8,128)(2,1)S(1)}, bf16[16,64,128]{2,1,0:T(8,128)(2,1)S(1)}, u32[]{:S(2)}, u32[]{:S(2)}) collective-permute-start(bf16[16,64,128]{2,1,0:T(8,128)(2,1)S(1)} %shard_map.189.rest_2_), channel_id=1, source_target_pairs={{0,15},{1,0},{2,1},{3,2},{4,3},{5,4},{6,5},{7,6},{8,7},{9,8},{10,9... | collective-permute-start | bytes 786440 | tf_op jit(solution)/shard_map/ppermute | solution.py:37
  138.9 13.7 %collective-permute-start.17 = (bf16[16,64,128]{2,1,0:T(8,128)(2,1)S(1)}, bf16[16,64,128]{2,1,0:T(8,128)(2,1)S(1)}, u32[]{:S(2)}, u32[]{:S(2)}) collective-permute-start(bf16[16,64,128]{2,1,0:T(8,128)(2,1)S(1)} %shard_map.189.rest_2_), channel_id=1, source_target_pairs={{0,16},{16,0},{32,48},{48,32},{64,80},{80,64},{96,112},{112,96},{1... | collective-permute-start | bytes 786440 | tf_op jit(solution)/shard_map/ppermute | solution.py:23
  148.3 5.5 %collective-permute-start.16 = (bf16[16,64,128]{2,1,0:T(8,128)(2,1)S(1)}, bf16[16,64,128]{2,1,0:T(8,128)(2,1)S(1)}, u32[]{:S(2)}, u32[]{:S(2)}) collective-permute-start(bf16[16,64,128]{2,1,0:T(8,128)(2,1)S(1)} %collective-permute-done.15.rest_0_), channel_id=1, source_target_pairs={{0,16},{16,0},{32,48},{48,32},{64,80},{80,64},{96,112},{112,96},{1... | collective-permute-start | bytes 786440 | tf_op jit(solution)/shard_map/ppermute | solution.py:23
  152.6 1.5 collective-permute-start.19
  155.7 14.0 %copy-start.11 = (bf16[512,512]{1,0:T(8,128)(2,1)S(1)}, bf16[512,512]{1,0:T(8,128)(2,1)}, u32[]{:S(2)}) copy-start(bf16[512,512]{1,0:T(8,128)(2,1)} %w_agg.2) | copy-start | bytes 1572868
  160.2 1.6 collective-permute-start.20
  162.4 4.6 %collective-permute-start.21 = (bf16[16,16,128]{2,1,0:T(8,128)(2,1)S(1)}, bf16[16,16,128]{2,1,0:T(8,128)(2,1)S(1)}, u32[]{:S(2)}, u32[]{:S(2)}) collective-permute-start(bf16[16,16,128]{2,1,0:T(8,128)(2,1)S(1)} %get-tuple-element.106), channel_id=1, source_target_pairs={{0,32},{16,48},{32,64},{48,80},{64,96},{80,112},{96,0},{112,16},{1... | collective-permute-start | bytes 196616 | tf_op jit(solution)/shard_map/ppermute | solution.py:19
  163.5 5.7 %collective-permute-start.22 = (bf16[16,16,128]{2,1,0:T(8,128)(2,1)S(1)}, bf16[16,16,128]{2,1,0:T(8,128)(2,1)S(1)}, u32[]{:S(2)}, u32[]{:S(2)}) collective-permute-start(bf16[16,16,128]{2,1,0:T(8,128)(2,1)S(1)} %get-tuple-element.107), channel_id=1, source_target_pairs={{0,64},{16,80},{32,96},{48,112},{64,0},{80,16},{96,32},{112,48},{1... | collective-permute-start | bytes 196616 | tf_op jit(solution)/shard_map/ppermute | solution.py:19
  166.2 3.4 %collective-permute-start.23 = (bf16[16,16,128]{2,1,0:T(8,128)(2,1)S(1)}, bf16[16,16,128]{2,1,0:T(8,128)(2,1)S(1)}, u32[]{:S(2)}, u32[]{:S(2)}) collective-permute-start(bf16[16,16,128]{2,1,0:T(8,128)(2,1)S(1)} %get-tuple-element.108), channel_id=1, source_target_pairs={{0,96},{16,112},{32,0},{48,16},{64,32},{80,48},{96,64},{112,80},{1... | collective-permute-start | bytes 196616 | tf_op jit(solution)/shard_map/ppermute | solution.py:19
  166.3 15.8 %copy-start.3 = (bf16[64,128,128]{2,1,0:T(8,128)(2,1)S(1)}, bf16[64,128,128]{2,1,0:T(8,128)(2,1)}, u32[]{:S(2)}) copy-start(bf16[64,128,128]{2,1,0:T(8,128)(2,1)} %all-gather.3.cloned.1.call-done.masks) | copy-start | bytes 6291460
  171.1 9.8 %copy-start.14 = (bf16[256,512]{1,0:T(8,128)(2,1)}, bf16[256,512]{1,0:T(8,128)(2,1)S(1)}, u32[]{:S(2)}) copy-start(bf16[256,512]{1,0:T(8,128)(2,1)S(1)} %get-tuple-element.133) | copy-start | bytes 786436
  171.1 4.4 %collective-permute-start.24 = (bf16[16,16,128]{2,1,0:T(8,128)(2,1)S(1)}, bf16[16,16,128]{2,1,0:T(8,128)(2,1)S(1)}, u32[]{:S(2)}, u32[]{:S(2)}) collective-permute-start(bf16[16,16,128]{2,1,0:T(8,128)(2,1)S(1)} %get-tuple-element.112), channel_id=1, source_target_pairs={{0,32},{16,48},{32,64},{48,80},{64,96},{80,112},{96,0},{112,16},{1... | collective-permute-start | bytes 196616 | tf_op jit(solution)/shard_map/ppermute | solution.py:19
  171.5 5.5 %collective-permute-start.25 = (bf16[16,16,128]{2,1,0:T(8,128)(2,1)S(1)}, bf16[16,16,128]{2,1,0:T(8,128)(2,1)S(1)}, u32[]{:S(2)}, u32[]{:S(2)}) collective-permute-start(bf16[16,16,128]{2,1,0:T(8,128)(2,1)S(1)} %get-tuple-element.113), channel_id=1, source_target_pairs={{0,64},{16,80},{32,96},{48,112},{64,0},{80,16},{96,32},{112,48},{1... | collective-permute-start | bytes 196616 | tf_op jit(solution)/shard_map/ppermute | solution.py:19
  174.6 3.4 %collective-permute-start.26 = (bf16[16,16,128]{2,1,0:T(8,128)(2,1)S(1)}, bf16[16,16,128]{2,1,0:T(8,128)(2,1)S(1)}, u32[]{:S(2)}, u32[]{:S(2)}) collective-permute-start(bf16[16,16,128]{2,1,0:T(8,128)(2,1)S(1)} %get-tuple-element.114), channel_id=1, source_target_pairs={{0,96},{16,112},{32,0},{48,16},{64,32},{80,48},{96,64},{112,80},{1... | collective-permute-start | bytes 196616 | tf_op jit(solution)/shard_map/ppermute | solution.py:19
  178.6 3.5 %collective-permute-start.27 = (bf16[16,64,128]{2,1,0:T(8,128)(2,1)S(1)}, bf16[16,64,128]{2,1,0:T(8,128)(2,1)S(1)}, u32[]{:S(2)}, u32[]{:S(2)}) collective-permute-start(bf16[16,64,128]{2,1,0:T(8,128)(2,1)S(1)} %shard_map.193.mine), channel_id=1, source_target_pairs={{0,16},{16,0},{32,48},{48,32},{64,80},{80,64},{96,112},{112,96},{1... | collective-permute-start | bytes 786440 | tf_op jit(solution)/shard_map/ppermute | solution.py:23
  186.2 21.8 %copy-start.16 = (bf16[16,1,16,512]{3,2,1,0:T(8,128)(2,1)S(1)}, bf16[16,1,16,512]{3,2,1,0:T(8,128)(2,1)}, u32[]{:S(2)}) copy-start(bf16[16,1,16,512]{3,2,1,0:T(8,128)(2,1)} %copy-done.15) | copy-start | bytes 786436
  186.2 2.4 collective-permute-start.28
  188.6 22.8 %copy-start.13 = (f32[256,512]{1,0:T(8,128)S(1)}, f32[256,512]{1,0:T(8,128)}, u32[]{:S(2)}) copy-start(f32[256,512]{1,0:T(8,128)} %copy-done.12) | copy-start | bytes 1572868
  188.7 10.1 %collective-permute-start.29 = (bf16[16,64,128]{2,1,0:T(8,128)(2,1)S(1)}, bf16[16,64,128]{2,1,0:T(8,128)(2,1)S(1)}, u32[]{:S(2)}, u32[]{:S(2)}) collective-permute-start(bf16[16,64,128]{2,1,0:T(8,128)(2,1)S(1)} %get-tuple-element.117), channel_id=1, source_target_pairs={{0,15},{1,0},{2,1},{3,2},{4,3},{5,4},{6,5},{7,6},{8,7},{9,8},{10,9... | collective-permute-start | bytes 786440 | tf_op jit(solution)/shard_map/ppermute | solution.py:37
  193.5 10.5 %collective-permute-start.30 = (bf16[16,64,128]{2,1,0:T(8,128)(2,1)S(1)}, bf16[16,64,128]{2,1,0:T(8,128)(2,1)S(1)}, u32[]{:S(2)}, u32[]{:S(2)}) collective-permute-start(bf16[16,64,128]{2,1,0:T(8,128)(2,1)S(1)} %get-tuple-element.119), channel_id=1, source_target_pairs={{0,1},{1,2},{2,3},{3,4},{4,5},{5,6},{6,7},{7,8},{8,9},{9,10},{10,1... | collective-permute-start | bytes 786440 | tf_op jit(solution)/shard_map/ppermute | solution.py:37
  204.6 4.4 %collective-permute-start.31 = (bf16[16,16,128]{2,1,0:T(8,128)(2,1)S(1)}, bf16[16,16,128]{2,1,0:T(8,128)(2,1)S(1)}, u32[]{:S(2)}, u32[]{:S(2)}) collective-permute-start(bf16[16,16,128]{2,1,0:T(8,128)(2,1)S(1)} %get-tuple-element.121), channel_id=1, source_target_pairs={{0,32},{16,48},{32,64},{48,80},{64,96},{80,112},{96,0},{112,16},{1... | collective-permute-start | bytes 196616 | tf_op jit(solution)/shard_map/ppermute | solution.py:19
  205.5 4.9 %collective-permute-start.32 = (bf16[16,16,128]{2,1,0:T(8,128)(2,1)S(1)}, bf16[16,16,128]{2,1,0:T(8,128)(2,1)S(1)}, u32[]{:S(2)}, u32[]{:S(2)}) collective-permute-start(bf16[16,16,128]{2,1,0:T(8,128)(2,1)S(1)} %get-tuple-element.122), channel_id=1, source_target_pairs={{0,64},{16,80},{32,96},{48,112},{64,0},{80,16},{96,32},{112,48},{1... | collective-permute-start | bytes 196616 | tf_op jit(solution)/shard_map/ppermute | solution.py:19
  208.0 3.3 %collective-permute-start.33 = (bf16[16,16,128]{2,1,0:T(8,128)(2,1)S(1)}, bf16[16,16,128]{2,1,0:T(8,128)(2,1)S(1)}, u32[]{:S(2)}, u32[]{:S(2)}) collective-permute-start(bf16[16,16,128]{2,1,0:T(8,128)(2,1)S(1)} %get-tuple-element.123), channel_id=1, source_target_pairs={{0,96},{16,112},{32,0},{48,16},{64,32},{80,48},{96,64},{112,80},{1... | collective-permute-start | bytes 196616 | tf_op jit(solution)/shard_map/ppermute | solution.py:19
  212.7 6.5 %collective-permute-start.34 = (bf16[16,16,256]{2,1,0:T(8,128)(2,1)S(1)}, bf16[16,16,256]{2,1,0:T(8,128)(2,1)S(1)}, u32[]{:S(2)}, u32[]{:S(2)}) collective-permute-start(bf16[16,16,256]{2,1,0:T(8,128)(2,1)S(1)} %get-tuple-element.129.refs_0_), channel_id=1, source_target_pairs={{0,4},{1,5},{2,6},{3,7},{4,8},{5,9},{6,10},{7,11},{8,12},{9,13},{1... | collective-permute-start | bytes 393224 | tf_op jit(solution)/shard_map/ppermute | solution.py:29
  212.8 6.4 %collective-permute-start.35 = (bf16[16,16,256]{2,1,0:T(8,128)(2,1)S(1)}, bf16[16,16,256]{2,1,0:T(8,128)(2,1)S(1)}, u32[]{:S(2)}, u32[]{:S(2)}) collective-permute-start(bf16[16,16,256]{2,1,0:T(8,128)(2,1)S(1)} %get-tuple-element.129.refs_0_), channel_id=1, source_target_pairs={{0,8},{1,9},{2,10},{3,11},{4,12},{5,13},{6,14},{7,15},{8,0},{9,1},... | collective-permute-start | bytes 393224 | tf_op jit(solution)/shard_map/ppermute | solution.py:29
  212.9 6.9 %collective-permute-start.36 = (bf16[16,16,256]{2,1,0:T(8,128)(2,1)S(1)}, bf16[16,16,256]{2,1,0:T(8,128)(2,1)S(1)}, u32[]{:S(2)}, u32[]{:S(2)}) collective-permute-start(bf16[16,16,256]{2,1,0:T(8,128)(2,1)S(1)} %get-tuple-element.129.refs_0_), channel_id=1, source_target_pairs={{0,12},{1,13},{2,14},{3,15},{4,0},{5,1},{6,2},{7,3},{8,4},{9,5},{1... | collective-permute-start | bytes 393224 | tf_op jit(solution)/shard_map/ppermute | solution.py:29
  215.4 6.7 %collective-permute-start.37 = (bf16[16,16,256]{2,1,0:T(8,128)(2,1)S(1)}, bf16[16,16,256]{2,1,0:T(8,128)(2,1)S(1)}, u32[]{:S(2)}, u32[]{:S(2)}) collective-permute-start(bf16[16,16,256]{2,1,0:T(8,128)(2,1)S(1)} %get-tuple-element.130.refs_4_), channel_id=1, source_target_pairs={{0,1},{1,2},{2,3},{3,0},{4,5},{5,6},{6,7},{7,4},{8,9},{9,10},{10,1... | collective-permute-start | bytes 393224 | tf_op jit(solution)/shard_map/ppermute | solution.py:33
  215.4 6.7 %collective-permute-start.38 = (bf16[16,16,256]{2,1,0:T(8,128)(2,1)S(1)}, bf16[16,16,256]{2,1,0:T(8,128)(2,1)S(1)}, u32[]{:S(2)}, u32[]{:S(2)}) collective-permute-start(bf16[16,16,256]{2,1,0:T(8,128)(2,1)S(1)} %get-tuple-element.130.refs_4_), channel_id=1, source_target_pairs={{0,2},{1,3},{2,0},{3,1},{4,6},{5,7},{6,4},{7,5},{8,10},{9,11},{10,... | collective-permute-start | bytes 393224 | tf_op jit(solution)/shard_map/ppermute | solution.py:33
  219.2 4.1 %collective-permute-start.39 = (bf16[16,16,256]{2,1,0:T(8,128)(2,1)S(1)}, bf16[16,16,256]{2,1,0:T(8,128)(2,1)S(1)}, u32[]{:S(2)}, u32[]{:S(2)}) collective-permute-start(bf16[16,16,256]{2,1,0:T(8,128)(2,1)S(1)} %get-tuple-element.130.refs_4_), channel_id=1, source_target_pairs={{0,3},{1,0},{2,1},{3,2},{4,7},{5,4},{6,5},{7,6},{8,11},{9,8},{10,9... | collective-permute-start | bytes 393224 | tf_op jit(solution)/shard_map/ppermute | solution.py:33
  223.4 9.7 %collective-permute-start.40 = (bf16[4,16,16,256]{3,2,1,0:T(8,128)(2,1)S(1)}, bf16[4,16,16,256]{3,2,1,0:T(8,128)(2,1)S(1)}, u32[]{:S(2)}, u32[]{:S(2)}) collective-permute-start(bf16[4,16,16,256]{3,2,1,0:T(8,128)(2,1)S(1)} %get-tuple-element.131.rest_0_), channel_id=1, source_target_pairs={{0,1},{1,2},{2,3},{3,0},{4,5},{5,6},{6,7},{7,4},{8,9},{9,10},{10,1... | collective-permute-start | bytes 1572872 | tf_op jit(solution)/shard_map/ppermute | solution.py:33
  223.5 20.9 %collective-permute-start.41 = (bf16[4,16,16,256]{3,2,1,0:T(8,128)(2,1)S(1)}, bf16[4,16,16,256]{3,2,1,0:T(8,128)(2,1)S(1)}, u32[]{:S(2)}, u32[]{:S(2)}) collective-permute-start(bf16[4,16,16,256]{3,2,1,0:T(8,128)(2,1)S(1)} %get-tuple-element.131.rest_0_), channel_id=1, source_target_pairs={{0,2},{1,3},{2,0},{3,1},{4,6},{5,7},{6,4},{7,5},{8,10},{9,11},{10,... | collective-permute-start | bytes 1572872 | tf_op jit(solution)/shard_map/ppermute | solution.py:33
  226.2 22.6 %collective-permute-start.42 = (bf16[4,16,16,256]{3,2,1,0:T(8,128)(2,1)S(1)}, bf16[4,16,16,256]{3,2,1,0:T(8,128)(2,1)S(1)}, u32[]{:S(2)}, u32[]{:S(2)}) collective-permute-start(bf16[4,16,16,256]{3,2,1,0:T(8,128)(2,1)S(1)} %get-tuple-element.131.rest_0_), channel_id=1, source_target_pairs={{0,3},{1,0},{2,1},{3,2},{4,7},{5,4},{6,5},{7,6},{8,11},{9,8},{10,9... | collective-permute-start | bytes 1572872 | tf_op jit(solution)/shard_map/ppermute | solution.py:33
  226.2 22.6 %collective-permute-start.43 = (bf16[4,16,16,256]{3,2,1,0:T(8,128)(2,1)S(1)}, bf16[4,16,16,256]{3,2,1,0:T(8,128)(2,1)S(1)}, u32[]{:S(2)}, u32[]{:S(2)}) collective-permute-start(bf16[4,16,16,256]{3,2,1,0:T(8,128)(2,1)S(1)} %get-tuple-element.132.rest_4_), channel_id=1, source_target_pairs={{0,4},{1,5},{2,6},{3,7},{4,8},{5,9},{6,10},{7,11},{8,12},{9,13},{1... | collective-permute-start | bytes 1572872 | tf_op jit(solution)/shard_map/ppermute | solution.py:29
  226.5 22.3 %collective-permute-start.44 = (bf16[4,16,16,256]{3,2,1,0:T(8,128)(2,1)S(1)}, bf16[4,16,16,256]{3,2,1,0:T(8,128)(2,1)}, u32[]{:S(2)}, u32[]{:S(2)}) collective-permute-start(bf16[4,16,16,256]{3,2,1,0:T(8,128)(2,1)S(1)} %get-tuple-element.132.rest_4_), channel_id=1, source_target_pairs={{0,8},{1,9},{2,10},{3,11},{4,12},{5,13},{6,14},{7,15},{8,0},{9,1},... | collective-permute-start | bytes 1572872 | tf_op jit(solution)/shard_map/ppermute | solution.py:29
  233.1 15.7 %collective-permute-start.45 = (bf16[4,16,16,256]{3,2,1,0:T(8,128)(2,1)S(1)}, bf16[4,16,16,256]{3,2,1,0:T(8,128)(2,1)}, u32[]{:S(2)}, u32[]{:S(2)}) collective-permute-start(bf16[4,16,16,256]{3,2,1,0:T(8,128)(2,1)S(1)} %get-tuple-element.132.rest_4_), channel_id=1, source_target_pairs={{0,12},{1,13},{2,14},{3,15},{4,0},{5,1},{6,2},{7,3},{8,4},{9,5},{1... | collective-permute-start | bytes 1572872 | tf_op jit(solution)/shard_map/ppermute | solution.py:29
  252.5 58.3 %all-to-all-start.1 = ((bf16[8,32,16,512]{3,2,1,0:T(8,128)(2,1)}), bf16[8,32,16,512]{3,2,1,0:T(8,128)(2,1)}, u32[]{:S(2)}, u32[]{:S(2)}) async-start(bf16[8,32,16,512]{3,2,1,0:T(8,128)(2,1)} %shard_map.199), calls=%async_computation.1 | async-start | bytes 8388608 | tf_op jit(solution)/shard_map/all_to_all | solution.py:479
  310.9 7.8 %copy-start.1 = (bf16[512,512]{1,0:T(8,128)(2,1)S(1)}, bf16[512,512]{1,0:T(8,128)(2,1)}, u32[]{:S(2)}) copy-start(bf16[512,512]{1,0:T(8,128)(2,1)} %param.26) | copy-start | bytes 1572868
  (5 other events, 6.4 us)
Sparse Core Ops, SparseCore 0:
  75.1 31.5 all-gather.2
  233.7 33.7 all-gather.4

commit v4 on v3

--- a/solution.py
+++ b/solution.py
@@ -12,7 +12,7 @@
 MIB = 1024 * 1024
 SMEM = pl.BlockSpec(memory_space=pltpu.SMEM)
 VMEM = pl.BlockSpec(memory_space=pltpu.VMEM)
-HBM = pl.BlockSpec(memory_space=pl.ANY)
+HBM = pl.BlockSpec(memory_space=pltpu.HBM)
 
 
 def over_z(array, by):
@@ -150,7 +150,7 @@
 
 
 def combine_body(ids, meta, arrived, *rest):
-    outs, acc = rest[:8], rest[8]
+    outs, acc = rest[:10], rest[10]
     x, y = ids[2], ids[3]
     acc[...] = jnp.zeros_like(acc)
 
@@ -162,38 +162,73 @@
     for kx in range(4):
         for ky in range(4):
             at = pl.ds((4 * ((x + kx) & 3) + ((y + ky) & 3)) * 16, 16)
-            outs[ky][kx] = acc[at, :, :256].astype(BF16)
-            outs[4 + kx][ky] = acc[at, :, 256:].astype(BF16)
+            place(outs[:5], ky, kx, acc[at, :, :256].astype(BF16))
+            place(outs[5:], kx, ky, acc[at, :, 256:].astype(BF16))
+
+
+def place(refs, step, other, value):
+    if step == 2:
+        refs[2 + other // 2][other % 2] = value
+    else:
+        refs[{0: 0, 1: 1, 3: 4}[step]][other] = value
+
+
+PARTS = [((4, 16, 16, 256), BF16)] * 2 + [((2, 16, 16, 256), BF16)] * 2 + [((4, 16, 16, 256), BF16)]
+SMALL = [((16, 16, 256), BF16)] * 2 + [((8, 16, 256), BF16)] * 2 + [((16, 16, 256), BF16)]
 
 
 def combine(ids, meta, arrived):
     outs = local(
         combine_body,
-        [((4, 16, 16, 256), BF16)] * 8,
+        PARTS * 2,
         [ids, meta, arrived.reshape(256, 16, 512)],
         smem=2,
         scratch=[pltpu.VMEM((256, 16, 512), F32)],
         limit=20,
     )
-    return outs[:4], outs[4:]
+    return outs[:5], outs[5:]
+
+
+def relay_body(*refs):
+    for q in range(2):
+        on, back, from_back, from_on = refs[4 * q : 4 * q + 4]
+        new_on, new_back = refs[8 + 2 * q : 10 + 2 * q]
+        half = on.shape[0] // 2
+        new_on[:half] = (on[:half].astype(F32) + from_back[...].astype(F32)).astype(BF16)
+        new_on[half:] = on[half:]
+        new_back[:half] = back[:half]
+        new_back[half:] = (back[half:].astype(F32) + from_on[...].astype(F32)).astype(BF16)
+
+
+def relay(first, first_over, second, second_over):
+    ins = []
+    for parts, over in ((first, first_over), (second, second_over)):
+        ins += [parts[1], parts[4], over(parts[2], 1), over(parts[3], 3)]
+    kind = (ins[0].shape, BF16)
+    on_1, back_1, on_2, back_2 = local(relay_body, [kind] * 4, ins, smem=0)
+    return (
+        [first[0], first_over(on_1, 1), first_over(back_1, 3)],
+        [second[0], second_over(on_2, 1), second_over(back_2, 3)],
+    )
 
 
 def add_rows_body(*refs):
     for q in range(2):
-        a, b, c, d = refs[4 * q : 4 * q + 4]
+        a, b, c = refs[3 * q : 3 * q + 3]
+        outs = refs[6 + 5 * q : 11 + 5 * q]
         for j in range(4):
-            refs[8 + 4 * q + j][...] = (
-                a[j].astype(F32) + b[j].astype(F32) + c[j].astype(F32) + d[j].astype(F32)
-            ).astype(BF16)
+            total = (a[j].astype(F32) + b[j].astype(F32) + c[j].astype(F32)).astype(BF16)
+            if j == 2:
+                outs[2][...] = total[:8]
+                outs[3][...] = total[8:]
+            else:
+                outs[{0: 0, 1: 1, 3: 4}[j]][...] = total
 
 
 def reduce_halves(by_y, by_x):
-    by_y = [by_y[0]] + [over_y(by_y[k], k) for k in (1, 2, 3)]
-    by_x = [by_x[0]] + [over_x(by_x[k], k) for k in (1, 2, 3)]
-    sums = local(add_rows_body, [((16, 16, 256), BF16)] * 8, [*by_y, *by_x], smem=0)
-    left, right = sums[:4], sums[4:]
-    left = [left[0]] + [over_x(left[k], k) for k in (1, 2, 3)]
-    right = [right[0]] + [over_y(right[k], k) for k in (1, 2, 3)]
+    by_y, by_x = relay(by_y, over_y, by_x, over_x)
+    sums = local(add_rows_body, SMALL * 2, [*by_y, *by_x], smem=0)
+    left, right = relay(sums[:5], over_x, sums[5:], over_y)
     return [*left, *right]
 
 
@@ -209,14 +244,13 @@
 
 
 def enc_mlp_body(ids, *rest):
-    terms, (pre_self, rows, w_agg, w_out, w_pass, pre_ref, first_ref) = rest[:8], rest[8:15]
-    outs, wide = rest[15:19], rest[19]
+    terms, (pre_self, rows, w_agg, w_out, w_pass, pre_ref, first_ref) = rest[:6], rest[6:13]
+    outs, wide = rest[13:17], rest[17]
     z = ids[0]
     pre = pre_self[...]
     for q in range(2):
-        total = terms[4 * q][...].astype(F32)
-        for more in terms[4 * q + 1 : 4 * q + 4]:
-            total += more[...].astype(F32)
+        a, b, c = terms[3 * q : 3 * q + 3]
+        total = a[...].astype(F32) + b[...].astype(F32) + c[...].astype(F32)
         pre += dot(total.astype(BF16).reshape(256, 256), w_agg[256 * q : 256 * q + 256, :])
     pre_ref[...] = pre
     hidden = jax.nn.silu(pre).astype(BF16)
@@ -286,13 +320,16 @@
     return [pieces[0]] + [over_z(pieces[k], k) for k in (1, 2, 3)]
 
 
-def edge_loop(c, meta, one):
-    def four(n, _):
-        row = (2 * (n >> 2) + c) * 64 + (n & 3) * 4
-        one(n * 4, [(meta[row + 32 + e], meta[row + 48 + e]) for e in range(4)])
-        return 0
-
-    lax.fori_loop(0, 16, four, 0)
+def edge_loop(z, c, meta, one):
+    for k in range(4):
+        row = (2 * ((z - k) & 3) + c) * 64
+
+        def four(n, _):
+            at = row + n * 4
+            one(k, n * 4, [(meta[at + 32 + e], meta[at + 48 + e]) for e in range(4)])
+            return 0
+
+        lax.fori_loop(0, 4, four, 0)
 
 
 def core_rows(z, c):
@@ -314,37 +351,64 @@
         other[:, at, :] = whole[:, core_rows(z, 1 - c), :].astype(BF16)
 
 
-def proc_body(ids, meta, masks, *rest):
-    tables, (own, other, ext, acc) = rest[:6], rest[6:]
-    c = ids[1]
+def proc_body(ids, meta, *rest):
+    masks, tables, (own, other, ext, acc) = rest[:4], rest[4:10], rest[10:]
+    z, c = ids[0], ids[1]
     for k in range(3):
         join_rows(c, tables[2 * k], tables[2 * k + 1], ext, 16 * k)
     acc[...] = jnp.zeros_like(acc)
 
-    def one(base, edges):
+    def one(k, base, edges):
         terms = [
-            lax.dot_general(masks[base + e], ext[source], (((0,), (0,)), ((), ())), preferred_element_type=F32)
+            lax.dot_general(masks[k][base + e], ext[source], (((0,), (0,)), ((), ())), preferred_element_type=F32)
             for e, (source, _) in enumerate(edges)
         ]
         for term, (_, target) in zip(terms, edges):
             acc[target] += term
 
-    edge_loop(c, meta, one)
+    edge_loop(z, c, meta, one)
     part_rows(c, acc, own, other)
 
 
-def proc_back_body(ids, meta, masks, mine, theirs, own, other, grads, acc):
-    c = ids[1]
+def proc_back_body(ids, meta, *rest):
+    masks, (mine, theirs, own, other, grads, acc) = rest[:4], rest[4:]
+    z, c = ids[0], ids[1]
     join_rows(c, mine, theirs, grads, 0)
     acc[...] = jnp.zeros_like(acc)
 
-    def one(base, edges):
-        terms = [dot(masks[base + e], grads[target]) for e, (_, target) in enumerate(edges)]
+    def one(k, base, edges):
+        terms = [dot(masks[k][base + e], grads[target]) for e, (_, target) in enumerate(edges)]
         for term, (source, _) in zip(terms, edges):
             acc[source] += term
 
-    edge_loop(c, meta, one)
+    edge_loop(z, c, meta, one)
     part_rows(c, acc, own, other)
+
+
+def pack_body(ids, p0, p1, p2, p3, out):
+    for k, piece in enumerate((p0, p1, p2, p3)):
+        out[(ids[0] - k) & 3] = piece[...].reshape(16, 16, 512)
+
+
+def unpack_body(ids, mine, theirs, out, whole, sem):
+    c = ids[1]
+    for z in range(4):
+        whole[:, core_rows(z, c), :] = mine[z]
+        whole[:, core_rows(z, 1 - c), :] = theirs[z]
+    to = move(whole, out, sem, 0)
+    to.start()
+    to.wait()
+
+
+def unpack(ids, mine, theirs):
+    return pl.pallas_call(
+        unpack_body,
+        out_shape=jax.ShapeDtypeStruct((16, 128, 512), BF16),
+        in_specs=[SMEM, VMEM, VMEM],
+        out_specs=HBM,
+        scratch_shapes=[pltpu.VMEM((16, 128, 512), BF16), pltpu.SemaphoreType.DMA((1,))],
+        compiler_params=pltpu.CompilerParams(vmem_limit_bytes=48 * MIB),
+    )(ids, mine, theirs).reshape(2048, 512)
 
 
 def pair_sum_body(ids, own, other, *outs):
@@ -503,17 +567,15 @@
     proc_target,
     proc_mask,
 ):
-    g, p = lax.axis_index("grid"), lax.axis_index("mesh")
+    messages, proc_mask = send_messages(enc_source, grid_latent, w_send, enc_mask, proc_mask)
+    places = (lax.axis_index("grid"), lax.axis_index("mesh"))
+    edges = (enc_part, enc_block, proc_source, proc_target)
+    messages, (g, p), edges, mesh_latent, mesh_cotangent = lax.optimization_barrier(
+        (messages, places, edges, mesh_latent, mesh_cotangent)
+    )
     z, c = g // 2, g % 2
     ids = jnp.stack([z, c, p // 4, p % 4]).astype(jnp.int32)
-    slots = enc_part[:, 0] * 16 + enc_block
-
-    labels = jnp.concatenate([slots, proc_source, proc_target])
-
-    messages, proc_mask = send_messages(enc_source, grid_latent, w_send, enc_mask, proc_mask)
-    messages, labels, mesh_latent, mesh_cotangent = lax.optimization_barrier(
-        (messages, labels, mesh_latent, mesh_cotangent)
-    )
+    labels = jnp.concatenate([edges[0][:, 0] * 16 + edges[1], edges[2], edges[3]])
     arrived = column_exchange(messages)
     rows = own_rows(mesh_latent, g)
     cotangent = own_rows(mesh_cotangent, g)
@@ -524,14 +586,11 @@
     )
     meta = lax.all_gather(labels, "grid", axis=0, tiled=True)
     arrived, meta, proc_mask = lax.optimization_barrier((arrived, meta, proc_mask))
-    masks = lax.all_gather(
-        proc_mask,
-        "grid",
-        axis=0,
-        tiled=True,
-        axis_index_groups=[[2 * i + j for i in range(4)] for j in range(2)],
-    )
-    summed = reduce_halves(*combine(ids, meta, arrived))
+    by_y, by_x = combine(ids, meta, arrived)
+    proc_mask, kept = lax.optimization_barrier((proc_mask, by_y[0]))
+    masks = spread_z([proc_mask] * 4)
+    summed = reduce_halves([kept, *by_y[1:]], by_x)
+    pre_self, masks = lax.optimization_barrier((pre_self, tuple(masks)))
     pre_enc, first, *passed = local(
         enc_mlp_body,
         [ROWS32, ROWS] + [PIECE] * 4,
@@ -539,8 +598,7 @@
         scratch=[WIDE],
     )
 
-    masks, kept = lax.optimization_barrier((masks, passed[0]))
-    own = table(ids, spread_z([kept, *passed[1:]]))
+    own = table(ids, spread_z(passed))
     tables = [over_mesh(own, 1), own, over_mesh(own, -1)]
     both = []
     for one in tables:
@@ -548,7 +606,7 @@
     mine, theirs = local(
         proc_body,
         [((16, 64, 128), F32), ((16, 64, 128), BF16)],
-        [ids, meta, masks, *both],
+        [ids, meta, *masks, *both],
         smem=2,
         scratch=[pltpu.VMEM((48, 128, 128), BF16), pltpu.VMEM((16, 128, 128), F32)],
     )
@@ -565,11 +623,15 @@
     mine, theirs = local(
         proc_back_body,
         [((48, 64, 128), F32), ((48, 64, 128), BF16)],
-        [ids, meta, masks, own, over_column(own, 0, 1)],
+        [ids, meta, *masks, own, over_column(own, 0, 1)],
         smem=2,
         scratch=[pltpu.VMEM((16, 128, 128), BF16), pltpu.VMEM((48, 128, 128), F32)],
     )
     parts = local(part_sum_body, [((16, 64, 128), BF16)] * 3, [mine, over_column(theirs, 0, 1)], smem=0)
+    out_rows, middle = lax.optimization_barrier((out_rows, parts[1]))
+    parts = [parts[0], middle, parts[2]]
+    out_parts = spread_z([out_rows] * 4)
+    g_first_part, out_parts = lax.optimization_barrier((g_first_part, tuple(out_parts)))
     g_pass = local(
         three_sum_body, [PIECE] * 4, [ids, over_mesh(parts[0], -1), parts[1], over_mesh(parts[2], 1)]
     )
@@ -580,10 +642,9 @@
         scratch=[WIDE],
     )
 
-    left, out_rows = lax.optimization_barrier((left, out_rows))
-    mesh_out = lax.all_gather(out_rows.reshape(1, 16, 16, 512), "grid", axis=0, tiled=True)
-    mesh_out = jnp.swapaxes(mesh_out, 0, 1).reshape(2048, 512)
+    packed = local(pack_body, [((4, 16, 16, 512), BF16)], [ids, *out_parts])[0]
     returned = column_exchange(fetch(ids, meta, gather_halves(left, right)))
+    mesh_out = unpack(ids, packed, over_column(packed, 0, 1))
     returned, mesh_out = lax.optimization_barrier((returned, mesh_out))
     grid_grad = grid_gradient(enc_source, w_send, enc_mask, returned)
     return (mesh_out, grid_grad)

time: 326 us -> 310 us (0.951)
  between operations: 15.1 us -> 1.96 us
  starting transfers between devices: 85.5 us -> 94 us
  local copies, waits for them, and re-layouts: 8.24 us -> 2.03 us
  waiting for transfers between devices: 125 us -> 120 us
    ppermute x12 -> x18, waiting for transfers between devices: 12.3 us -> 23.6 us  [over_z(): lax.ppermute(array, 'grid', [(2 * z + c, 2 * ((z + by) % 4) + c) for z in...]
    ppermute x12 -> x14, waiting for transfers between devices: 41 us -> 31.4 us  [over_y(): lax.ppermute(array, 'mesh', [(4 * x + y, 4 * x + (y + by) % 4) for x in r...]
    ppermute x12 -> x18, starting transfers between devices: 13.7 us -> 20.8 us  [over_z(): lax.ppermute(array, 'grid', [(2 * z + c, 2 * ((z + by) % 4) + c) for z in...]
    ppermute x4, starting transfers between devices: 9.6 us -> 3.49 us  [over_mesh(): return lax.ppermute(array, 'mesh', [(p, (p + by) % 16) for p in range(16)])]
    all_gather x2 -> x0, waiting for transfers between devices: 5.54 us -> none  [the longest x1 5.54 us: per_device(): lax.all_gather(out_rows.reshape(1, 16, 16, 512), 'grid', axis=0, tiled=True)]
    ppermute x12 -> x14, starting transfers between devices: 11.4 us -> 16.2 us  [over_y(): lax.ppermute(array, 'mesh', [(4 * x + y, 4 * x + (y + by) % 4) for x in r...]
    ppermute x4, waiting for transfers between devices: 10.5 us -> 6.38 us  [over_mesh(): return lax.ppermute(array, 'mesh', [(p, (p + by) % 16) for p in range(16)])]
    all_to_all x2, waiting for transfers between devices: 40.2 us -> 43.5 us  [column_exchange(): return lax.all_to_all(pieces, 'grid', 0, 0, tiled=True)]
  transfers between devices with their start and end apart: 50 -> 59, of which waited for: 34 -> 31; matrix products, arithmetic and copies ran while one was open for 2% -> 1% of each run, Pallas kernels for 3% -> 1%
where the time goes in v4:
time: 310 us
  waiting for transfers between devices  120 us (39%)
  starting transfers between devices  94 us (30%)
  blocking collectives  47.1 us (15%)
  Pallas kernels  43.2 us (14%)
    optimization_barrier x1, blocking collectives, per_device(): lax.optimization_barrier((arrived, meta, proc_mask))  47.1 us
    all_to_all x2, waiting for transfers between devices, column_exchange(): return lax.all_to_all(pieces, 'grid', 0, 0, tiled=True)  43.5 us
    ppermute x14, waiting for transfers between devices, over_y(): lax.ppermute(array, 'mesh', [(4 * x + y, 4 * x + (y + by) % 4) for x in r...  31.4 us
    ppermute x18, waiting for transfers between devices, over_z(): lax.ppermute(array, 'grid', [(2 * z + c, 2 * ((z + by) % 4) + c) for z in...  23.6 us
    pallas_call x16, Pallas kernels, local(): pl.pallas_call(body, out_shape=[jax.ShapeDtypeStruct(shape, dtype) for sh...  21.5 us
    ppermute x18, starting transfers between devices, over_z(): lax.ppermute(array, 'grid', [(2 * z + c, 2 * ((z + by) % 4) + c) for z in...  20.8 us
    ppermute x7, starting transfers between devices, over_column(): lax.ppermute(array, 'grid', [(2 * z + c, 2 * ((z + dz) % 4) + (c ^ dc)) f...  18.4 us
    ppermute x14, starting transfers between devices, over_x(): lax.ppermute(array, 'mesh', [(4 * x + y, 4 * ((x + by) % 4) + y) for x in...  17.8 us
  transfers between devices with their start and end apart: 59, of which 31 were waited for; matrix products, arithmetic and copies ran while one was open for 1% of the time, Pallas kernels for 1%

profile of v4, /device:TPU:1, one launch (start us, length us, event | category | flops | bytes accessed | tf_op | source)
XLA Modules:
  0.0 309.7 jit_solution(11698949495414655285)
XLA Ops:
  0.7 8.9 %shard_map.185 = (bf16[8,32,16,512]{3,2,1,0:T(8,128)(2,1)}, bf16[16,128,128]{2,1,0:T(8,128)(2,1)}) custom-call(s32[32]{0:T(128)} %source.3, bf16[3072,512]{1,0:T(8,128)(2,1)} %latent.1, bf16[512,512]{1,0:T(8,128)(2,1)} %w_send.3, s32[32,128,128]{2,1,0:T(8,128)} %mask.3, s32[16,128,128]{2,1,0:T(8,128)} %other.1), custom_call_target="tpu_custom_call" | custom-call | tf_op jit(solution)/shard_map/pallas_call | solution.py:126
  9.6 7.0 %all-to-all-start = ((bf16[8,32,16,512]{3,2,1,0:T(8,128)(2,1)}), bf16[8,32,16,512]{3,2,1,0:T(8,128)(2,1)}, u32[]{:S(2)}, u32[]{:S(2)}) async-start(bf16[8,32,16,512]{3,2,1,0:T(8,128)(2,1)} %get-tuple-element.99), calls=%async_computation | async-start | bytes 8388608 | tf_op jit(solution)/shard_map/all_to_all | solution.py:543
  20.0 47.1 %all-reduce.meta = s32[512]{0:T(512)S(1)} all-reduce(s32[512]{0:T(512)S(1)} %dynamic-update-slice), channel_id=1, replica_groups=mesh['grid'=8,'mesh'=16] {'grid'}, use_global_device_ids=true, to_apply=%add | all-reduce | flops 512 | bytes 4096 | tf_op jit(solution)/shard_map/optimization_barrier | solution.py:588
  67.2 4.8 %shard_map.186 = (bf16[4,16,16,256]{3,2,1,0:T(8,128)(2,1)S(1)}, bf16[4,16,16,256]{3,2,1,0:T(8,128)(2,1)S(1)}, bf16[2,16,16,256]{3,2,1,0:T(8,128)(2,1)S(1)}, bf16...) custom-call(s32[4]{0:T(128)S(1)} %pad_add_fusion.ids, ...), custom_call_target="tpu_custom_call" | custom-call | tf_op jit(solution)/shard_map/pallas_call | solution.py:41
  72.0 1.4 collective-permute-start.3
  73.4 1.5 collective-permute-start.4
  74.9 1.2 collective-permute-start.5
  76.1 1.5 collective-permute-start.6
  77.6 1.6 collective-permute-done.3.refs_2_
  79.2 2.4 collective-permute-done.5.refs_6_
  82.1 2.7 collective-permute-start.8
  84.7 1.2 collective-permute-start.9
  85.9 1.5 collective-permute-start.10
  87.4 1.3 collective-permute-start.2
  88.7 4.4 %collective-permute-done.7.refs_1_ = bf16[4,16,16,256]{3,2,1,0:T(8,128)(2,1)S(1)} collective-permute-done((bf16[4,16,16,256]{3,2,1,0:T(8,128)(2,1)S(1)}, bf16[4,16,16,256]{3,2,1,0:T(8,128)(2,1)S(1)}, u32[]{:S(2)}, u32[]{:S(2)}) %collective-permute-start.7) | collective-permute-done | bytes 524320 | tf_op jit(solution)/shard_map/ppermute | solution.py:33
  93.1 1.8 collective-permute-start.1
  97.0 2.1 collective-permute-start.12
  99.0 1.6 collective-permute-done.11.refs_2_
  100.7 2.7 collective-permute-start.14
  103.4 1.9 collective-permute-done.13.refs_6_
  105.5 2.7 collective-permute-start.16
  108.1 2.7 collective-permute-start.18
  110.9 8.8 %collective-permute-done.rest_1_ = bf16[16,128,128]{2,1,0:T(8,128)(2,1)S(1)} collective-permute-done((bf16[16,128,128]{2,1,0:T(8,128)(2,1)S(1)}, bf16[16,128,128]{2,1,0:T(8,128)(2,1)S(1)}, u32[]{:S(2)}, u32[]{:S(2)}) %collective-permute-start) | collective-permute-done | bytes 524320 | tf_op jit(solution)/shard_map/ppermute | solution.py:19
  119.8 1.4 shard_map.190
  121.2 1.6 collective-permute-start.20
  122.8 1.8 collective-permute-start.21
  124.6 1.6 collective-permute-done.19.p1
  127.4 2.0 collective-permute-start.25
  129.4 5.3 %collective-permute-start.24 = (bf16[16,64,128]{2,1,0:T(8,128)(2,1)S(1)}, bf16[16,64,128]{2,1,0:T(8,128)(2,1)S(1)}, u32[]{:S(2)}, u32[]{:S(2)}) collective-permute-start(bf16[16,64,128]{2,1,0:T(8,128)(2,1)S(1)} %shard_map.191.rest_6_), channel_id=1, source_target_pairs={{0,16},{16,0},{32,48},{48,32},{64,80},{80,64},{96,112},{112,96},{1... | collective-permute-start | bytes 786440 | tf_op jit(solution)/shard_map/ppermute | solution.py:23
  134.7 3.9 %collective-permute-start.26 = (bf16[16,64,128]{2,1,0:T(8,128)(2,1)S(1)}, bf16[16,64,128]{2,1,0:T(8,128)(2,1)S(1)}, u32[]{:S(2)}, u32[]{:S(2)}) collective-permute-start(bf16[16,64,128]{2,1,0:T(8,128)(2,1)S(1)} %collective-permute-done.25.rest_8_), channel_id=1, source_target_pairs={{0,16},{16,0},{32,48},{48,32},{64,80},{80,64},{96,112},{112,96},{1... | collective-permute-start | bytes 786440 | tf_op jit(solution)/shard_map/ppermute | solution.py:23
  138.5 5.8 %collective-permute-start.23 = (bf16[16,64,128]{2,1,0:T(8,128)(2,1)S(1)}, bf16[16,64,128]{2,1,0:T(8,128)(2,1)S(1)}, u32[]{:S(2)}, u32[]{:S(2)}) collective-permute-start(bf16[16,64,128]{2,1,0:T(8,128)(2,1)S(1)} %collective-permute-done.22.rest_4_), channel_id=1, source_target_pairs={{0,16},{16,0},{32,48},{48,32},{64,80},{80,64},{96,112},{112,96},{1... | collective-permute-start | bytes 786440 | tf_op jit(solution)/shard_map/ppermute | solution.py:23
  145.5 4.5 %shard_map.192 = (f32[16,64,128]{2,1,0:T(8,128)S(1)}, bf16[16,64,128]{2,1,0:T(8,128)(2,1)S(1)}) custom-call(s32[4]{0:T(128)S(1)} %pad_add_fusion.ids, s32[512]{0:T(512)S(1)} %all-reduce.meta, bf16[16,128,128]{2,1,0:T(8,128)(2,1)S(1)} %copy-done.2, bf16[16,128,128]{2,1,0:T(8,128)(2,1)S(1)} %collective-permute-done.rest_1_, ...), custom_call_target="tpu_custom_call" | custom-call | tf_op jit(solution)/shard_map/pallas_call | solution.py:41
  150.4 1.2 collective-permute-done.27.other
  153.2 2.9 collective-permute-start.29
  156.6 2.4 collective-permute-done.29.p2
  159.4 1.4 shard_map.194
  160.9 3.2 %collective-permute-start.32 = (bf16[16,16,128]{2,1,0:T(8,128)(2,1)S(1)}, bf16[16,16,128]{2,1,0:T(8,128)(2,1)S(1)}, u32[]{:S(2)}, u32[]{:S(2)}) collective-permute-start(bf16[16,16,128]{2,1,0:T(8,128)(2,1)S(1)} %get-tuple-element.162), channel_id=1, source_target_pairs={{0,64},{16,80},{32,96},{48,112},{64,0},{80,16},{96,32},{112,48},{1... | collective-permute-start | bytes 196616 | tf_op jit(solution)/shard_map/ppermute | solution.py:19
  165.2 1.3 collective-permute-done.32.p2
  168.1 2.4 collective-permute-start.34
  171.7 4.1 %shard_map.196 = (f32[48,64,128]{2,1,0:T(8,128)S(1)}, bf16[48,64,128]{2,1,0:T(8,128)(2,1)S(1)}) custom-call(s32[4]{0:T(128)S(1)} %pad_add_fusion.ids, s32[512]{0:T(512)S(1)} %all-reduce.meta, bf16[16,128,128]{2,1,0:T(8,128)(2,1)S(1)} %copy-done.2, bf16[16,128,128]{2,1,0:T(8,128)(2,1)S(1)} %collective-permute-done.rest_1_, ...), custom_call_target="tpu_custom_call" | custom-call | tf_op jit(solution)/shard_map/pallas_call | solution.py:41
  176.3 1.9 collective-permute-done.35.other
  178.5 1.4 collective-permute-start.37
  179.9 2.2 collective-permute-start.43
  182.7 3.3 %collective-permute-done.36.a = bf16[16,64,128]{2,1,0:T(8,128)(2,1)S(1)} collective-permute-done((bf16[16,64,128]{2,1,0:T(8,128)(2,1)S(1)}, bf16[16,64,128]{2,1,0:T(8,128)(2,1)S(1)}, u32[]{:S(2)}, u32[]{:S(2)}) %collective-permute-start.36) | collective-permute-done | bytes 262176 | tf_op jit(solution)/shard_map/ppermute | solution.py:37
  185.9 3.1 %collective-permute-done.37.c = bf16[16,64,128]{2,1,0:T(8,128)(2,1)S(1)} collective-permute-done((bf16[16,64,128]{2,1,0:T(8,128)(2,1)S(1)}, bf16[16,64,128]{2,1,0:T(8,128)(2,1)S(1)}, u32[]{:S(2)}, u32[]{:S(2)}) %collective-permute-start.37) | collective-permute-done | bytes 262176 | tf_op jit(solution)/shard_map/ppermute | solution.py:37
  190.6 2.5 collective-permute-start.39
  193.5 4.1 %collective-permute-done.41.p1 = bf16[256,512]{1,0:T(8,128)(2,1)S(1)} collective-permute-done((bf16[256,512]{1,0:T(8,128)(2,1)S(1)}, bf16[256,512]{1,0:T(8,128)(2,1)S(1)}, u32[]{:S(2)}, u32[]{:S(2)}) %collective-permute-start.41) | collective-permute-done | bytes 262176 | tf_op jit(solution)/shard_map/ppermute | solution.py:19
  197.6 1.9 collective-permute-done.38.p1
  199.5 1.3 shard_map.199
  201.0 1.4 collective-permute-start.45
  202.4 2.9 collective-permute-start.49
  206.4 2.5 collective-permute-done.44.refs_1_
  208.9 1.8 collective-permute-done.48.refs_6_
  213.5 2.5 collective-permute-start.55
  216.0 1.2 collective-permute-start.54
  217.2 3.8 %collective-permute-done.52.rest_3_ = bf16[4,16,16,256]{3,2,1,0:T(8,128)(2,1)S(1)} collective-permute-done((bf16[4,16,16,256]{3,2,1,0:T(8,128)(2,1)S(1)}, bf16[4,16,16,256]{3,2,1,0:T(8,128)(2,1)S(1)}, u32[]{:S(2)}, u32[]{:S(2)}) %collective-permute-start.52) | collective-permute-done | bytes 524320 | tf_op jit(solution)/shard_map/ppermute | solution.py:33
  220.9 1.7 collective-permute-start.53
  223.5 15.9 %collective-permute-done.50.rest_1_ = bf16[4,16,16,256]{3,2,1,0:T(8,128)(2,1)S(1)} collective-permute-done((bf16[4,16,16,256]{3,2,1,0:T(8,128)(2,1)S(1)}, bf16[4,16,16,256]{3,2,1,0:T(8,128)(2,1)S(1)}, u32[]{:S(2)}, u32[]{:S(2)}) %collective-permute-start.50) | collective-permute-done | bytes 524320 | tf_op jit(solution)/shard_map/ppermute | solution.py:33
  239.4 3.1 shard_map.201
  242.4 10.4 %all-to-all-start.1 = ((bf16[8,32,16,512]{3,2,1,0:T(8,128)(2,1)}), bf16[8,32,16,512]{3,2,1,0:T(8,128)(2,1)}, u32[]{:S(2)}, u32[]{:S(2)}) async-start(bf16[8,32,16,512]{3,2,1,0:T(8,128)(2,1)} %shard_map.201), calls=%async_computation.1 | async-start | bytes 8388608 | tf_op jit(solution)/shard_map/all_to_all | solution.py:543
  253.6 2.6 collective-permute-done.56.theirs
  256.2 2.0 shard_map.203
  258.3 43.5 %all-to-all-done.1.pieces = bf16[8,32,16,512]{3,2,1,0:T(8,128)(2,1)} async-done(((bf16[8,32,16,512]{3,2,1,0:T(8,128)(2,1)}), bf16[8,32,16,512]{3,2,1,0:T(8,128)(2,1)}, u32[]{:S(2)}, u32[]{:S(2)}) %all-to-all-start.1) | async-done | bytes 4194336 | tf_op jit(solution)/shard_map/all_to_all | solution.py:543
  301.8 7.8 %shard_map.204 = bf16[3072,512]{1,0:T(8,128)(2,1)} custom-call(s32[32]{0:T(128)} %source.3, bf16[512,512]{1,0:T(8,128)(2,1)} %w_send.3, s32[32,128,128]{2,1,0:T(8,128)} %mask.3, bf16[8,32,16,512]{3,2,1,0:T(8,128)(2,1)} %all-to-all-done.1.pieces), custom_call_target="tpu_custom_call" | custom-call | tf_op jit(solution)/shard_map/pallas_call | solution.py:521
  (114 shorter events, 23.5 us)
Async XLA Ops:
  0.6 155.4 %copy-start = (bf16[512,512]{1,0:T(8,128)(2,1)S(1)}, bf16[512,512]{1,0:T(8,128)(2,1)}, u32[]{:S(2)}) copy-start(bf16[512,512]{1,0:T(8,128)(2,1)} %param.26) | copy-start | bytes 1572868
  9.6 57.6 %all-to-all-start = ((bf16[8,32,16,512]{3,2,1,0:T(8,128)(2,1)}), bf16[8,32,16,512]{3,2,1,0:T(8,128)(2,1)}, u32[]{:S(2)}, u32[]{:S(2)}) async-start(bf16[8,32,16,512]{3,2,1,0:T(8,128)(2,1)} %get-tuple-element.99), calls=%async_computation | async-start | bytes 8388608 | tf_op jit(solution)/shard_map/all_to_all | solution.py:543
  72.0 7.2 %collective-permute-start.3 = (bf16[2,16,16,256]{3,2,1,0:T(8,128)(2,1)S(1)}, bf16[2,16,16,256]{3,2,1,0:T(8,128)(2,1)S(1)}, u32[]{:S(2)}, u32[]{:S(2)}) collective-permute-start(bf16[2,16,16,256]{3,2,1,0:T(8,128)(2,1)S(1)} %get-tuple-element.121), channel_id=1, source_target_pairs={{0,1},{1,2},{2,3},{3,0},{4,5},{5,6},{6,7},{7,4},{8,9},{9,10},{10,1... | collective-permute-start | bytes 786440 | tf_op jit(solution)/shard_map/ppermute | solution.py:33
  73.4 5.9 %collective-permute-start.4 = (bf16[2,16,16,256]{3,2,1,0:T(8,128)(2,1)S(1)}, bf16[2,16,16,256]{3,2,1,0:T(8,128)(2,1)S(1)}, u32[]{:S(2)}, u32[]{:S(2)}) collective-permute-start(bf16[2,16,16,256]{3,2,1,0:T(8,128)(2,1)S(1)} %get-tuple-element.122), channel_id=1, source_target_pairs={{0,3},{1,0},{2,1},{3,2},{4,7},{5,4},{6,5},{7,6},{8,11},{9,8},{10,9... | collective-permute-start | bytes 786440 | tf_op jit(solution)/shard_map/ppermute | solution.py:33
  74.9 6.7 %collective-permute-start.5 = (bf16[2,16,16,256]{3,2,1,0:T(8,128)(2,1)S(1)}, bf16[2,16,16,256]{3,2,1,0:T(8,128)(2,1)S(1)}, u32[]{:S(2)}, u32[]{:S(2)}) collective-permute-start(bf16[2,16,16,256]{3,2,1,0:T(8,128)(2,1)S(1)} %get-tuple-element.125), channel_id=1, source_target_pairs={{0,4},{1,5},{2,6},{3,7},{4,8},{5,9},{6,10},{7,11},{8,12},{9,13},{1... | collective-permute-start | bytes 786440 | tf_op jit(solution)/shard_map/ppermute | solution.py:29
  76.1 5.5 %collective-permute-start.6 = (bf16[2,16,16,256]{3,2,1,0:T(8,128)(2,1)S(1)}, bf16[2,16,16,256]{3,2,1,0:T(8,128)(2,1)S(1)}, u32[]{:S(2)}, u32[]{:S(2)}) collective-permute-start(bf16[2,16,16,256]{3,2,1,0:T(8,128)(2,1)S(1)} %get-tuple-element.126), channel_id=1, source_target_pairs={{0,12},{1,13},{2,14},{3,15},{4,0},{5,1},{6,2},{7,3},{8,4},{9,5},{1... | collective-permute-start | bytes 786440 | tf_op jit(solution)/shard_map/ppermute | solution.py:29
  82.0 37.8 %copy-start.4 = (bf16[512,512]{1,0:T(8,128)(2,1)S(1)}, bf16[512,512]{1,0:T(8,128)(2,1)}, u32[]{:S(2)}) copy-start(bf16[512,512]{1,0:T(8,128)(2,1)} %w_agg.3) | copy-start | bytes 1572868
  82.0 37.8 %copy-start.5 = (bf16[512,512]{1,0:T(8,128)(2,1)S(1)}, bf16[512,512]{1,0:T(8,128)(2,1)}, u32[]{:S(2)}) copy-start(bf16[512,512]{1,0:T(8,128)(2,1)} %w_out.3) | copy-start | bytes 1572868
  82.0 37.8 %copy-start.6 = (bf16[512,512]{1,0:T(8,128)(2,1)S(1)}, bf16[512,512]{1,0:T(8,128)(2,1)}, u32[]{:S(2)}) copy-start(bf16[512,512]{1,0:T(8,128)(2,1)} %w_pass.1) | copy-start | bytes 1572868
  82.0 11.1 %collective-permute-start.7 = (bf16[4,16,16,256]{3,2,1,0:T(8,128)(2,1)S(1)}, bf16[4,16,16,256]{3,2,1,0:T(8,128)(2,1)S(1)}, u32[]{:S(2)}, u32[]{:S(2)}) collective-permute-start(bf16[4,16,16,256]{3,2,1,0:T(8,128)(2,1)S(1)} %get-tuple-element.127), channel_id=1, source_target_pairs={{0,1},{1,2},{2,3},{3,0},{4,5},{5,6},{6,7},{7,4},{8,9},{9,10},{10,1... | collective-permute-start | bytes 1572872 | tf_op jit(solution)/shard_map/ppermute | solution.py:33
  82.1 12.8 %collective-permute-start.8 = (bf16[4,16,16,256]{3,2,1,0:T(8,128)(2,1)S(1)}, bf16[4,16,16,256]{3,2,1,0:T(8,128)(2,1)S(1)}, u32[]{:S(2)}, u32[]{:S(2)}) collective-permute-start(bf16[4,16,16,256]{3,2,1,0:T(8,128)(2,1)S(1)} %get-tuple-element.128), channel_id=1, source_target_pairs={{0,3},{1,0},{2,1},{3,2},{4,7},{5,4},{6,5},{7,6},{8,11},{9,8},{10,9... | collective-permute-start | bytes 1572872 | tf_op jit(solution)/shard_map/ppermute | solution.py:33
  84.7 11.1 %collective-permute-start.9 = (bf16[4,16,16,256]{3,2,1,0:T(8,128)(2,1)S(1)}, bf16[4,16,16,256]{3,2,1,0:T(8,128)(2,1)S(1)}, u32[]{:S(2)}, u32[]{:S(2)}) collective-permute-start(bf16[4,16,16,256]{3,2,1,0:T(8,128)(2,1)S(1)} %get-tuple-element.130), channel_id=1, source_target_pairs={{0,4},{1,5},{2,6},{3,7},{4,8},{5,9},{6,10},{7,11},{8,12},{9,13},{1... | collective-permute-start | bytes 1572872 | tf_op jit(solution)/shard_map/ppermute | solution.py:29
  85.9 9.9 %collective-permute-start.10 = (bf16[4,16,16,256]{3,2,1,0:T(8,128)(2,1)S(1)}, bf16[4,16,16,256]{3,2,1,0:T(8,128)(2,1)S(1)}, u32[]{:S(2)}, u32[]{:S(2)}) collective-permute-start(bf16[4,16,16,256]{3,2,1,0:T(8,128)(2,1)S(1)} %get-tuple-element.131), channel_id=1, source_target_pairs={{0,12},{1,13},{2,14},{3,15},{4,0},{5,1},{6,2},{7,3},{8,4},{9,5},{1... | collective-permute-start | bytes 1572872 | tf_op jit(solution)/shard_map/ppermute | solution.py:29
  87.4 20.7 %collective-permute-start.2 = (bf16[16,128,128]{2,1,0:T(8,128)(2,1)S(1)}, bf16[16,128,128]{2,1,0:T(8,128)(2,1)S(1)}, u32[]{:S(2)}, u32[]{:S(2)}) collective-permute-start(bf16[16,128,128]{2,1,0:T(8,128)(2,1)S(1)} %copy-done.2), channel_id=1, source_target_pairs={{0,96},{16,112},{32,0},{48,16},{64,32},{80,48},{96,64},{112,80},{1... | collective-permute-start | bytes 1572872 | tf_op jit(solution)/shard_map/ppermute | solution.py:19
  93.1 15.0 %collective-permute-start.1 = (bf16[16,128,128]{2,1,0:T(8,128)(2,1)S(1)}, bf16[16,128,128]{2,1,0:T(8,128)(2,1)S(1)}, u32[]{:S(2)}, u32[]{:S(2)}) collective-permute-start(bf16[16,128,128]{2,1,0:T(8,128)(2,1)S(1)} %copy-done.2), channel_id=1, source_target_pairs={{0,64},{16,80},{32,96},{48,112},{64,0},{80,16},{96,32},{112,48},{1... | collective-permute-start | bytes 1572872 | tf_op jit(solution)/shard_map/ppermute | solution.py:19
  94.9 24.8 %collective-permute-start = (bf16[16,128,128]{2,1,0:T(8,128)(2,1)S(1)}, bf16[16,128,128]{2,1,0:T(8,128)(2,1)S(1)}, u32[]{:S(2)}, u32[]{:S(2)}) collective-permute-start(bf16[16,128,128]{2,1,0:T(8,128)(2,1)S(1)} %copy-done.2), channel_id=1, source_target_pairs={{0,32},{16,48},{32,64},{48,80},{64,96},{80,112},{96,0},{112,16},{1... | collective-permute-start | bytes 1572872 | tf_op jit(solution)/shard_map/ppermute | solution.py:19
  96.3 4.4 %collective-permute-start.11 = (bf16[8,16,256]{2,1,0:T(8,128)(2,1)S(1)}, bf16[8,16,256]{2,1,0:T(8,128)(2,1)S(1)}, u32[]{:S(2)}, u32[]{:S(2)}) collective-permute-start(bf16[8,16,256]{2,1,0:T(8,128)(2,1)S(1)} %get-tuple-element.135), channel_id=1, source_target_pairs={{0,4},{1,5},{2,6},{3,7},{4,8},{5,9},{6,10},{7,11},{8,12},{9,13},{1... | collective-permute-start | bytes 196616 | tf_op jit(solution)/shard_map/ppermute | solution.py:29
  97.0 3.7 %collective-permute-start.12 = (bf16[8,16,256]{2,1,0:T(8,128)(2,1)S(1)}, bf16[8,16,256]{2,1,0:T(8,128)(2,1)S(1)}, u32[]{:S(2)}, u32[]{:S(2)}) collective-permute-start(bf16[8,16,256]{2,1,0:T(8,128)(2,1)S(1)} %get-tuple-element.136), channel_id=1, source_target_pairs={{0,12},{1,13},{2,14},{3,15},{4,0},{5,1},{6,2},{7,3},{8,4},{9,5},{1... | collective-permute-start | bytes 196616 | tf_op jit(solution)/shard_map/ppermute | solution.py:29
  100.7 4.6 %collective-permute-start.13 = (bf16[8,16,256]{2,1,0:T(8,128)(2,1)S(1)}, bf16[8,16,256]{2,1,0:T(8,128)(2,1)S(1)}, u32[]{:S(2)}, u32[]{:S(2)}) collective-permute-start(bf16[8,16,256]{2,1,0:T(8,128)(2,1)S(1)} %get-tuple-element.139), channel_id=1, source_target_pairs={{0,1},{1,2},{2,3},{3,0},{4,5},{5,6},{6,7},{7,4},{8,9},{9,10},{10,1... | collective-permute-start | bytes 196616 | tf_op jit(solution)/shard_map/ppermute | solution.py:33
  100.7 4.6 %collective-permute-start.14 = (bf16[8,16,256]{2,1,0:T(8,128)(2,1)S(1)}, bf16[8,16,256]{2,1,0:T(8,128)(2,1)S(1)}, u32[]{:S(2)}, u32[]{:S(2)}) collective-permute-start(bf16[8,16,256]{2,1,0:T(8,128)(2,1)S(1)} %get-tuple-element.140), channel_id=1, source_target_pairs={{0,3},{1,0},{2,1},{3,2},{4,7},{5,4},{6,5},{7,6},{8,11},{9,8},{10,9... | collective-permute-start | bytes 196616 | tf_op jit(solution)/shard_map/ppermute | solution.py:33
  105.4 14.4 %collective-permute-start.15 = (bf16[16,16,256]{2,1,0:T(8,128)(2,1)S(1)}, bf16[16,16,256]{2,1,0:T(8,128)(2,1)S(1)}, u32[]{:S(2)}, u32[]{:S(2)}) collective-permute-start(bf16[16,16,256]{2,1,0:T(8,128)(2,1)S(1)} %get-tuple-element.141), channel_id=1, source_target_pairs={{0,4},{1,5},{2,6},{3,7},{4,8},{5,9},{6,10},{7,11},{8,12},{9,13},{1... | collective-permute-start | bytes 393224 | tf_op jit(solution)/shard_map/ppermute | solution.py:29
  105.5 14.3 %collective-permute-start.16 = (bf16[16,16,256]{2,1,0:T(8,128)(2,1)S(1)}, bf16[16,16,256]{2,1,0:T(8,128)(2,1)S(1)}, u32[]{:S(2)}, u32[]{:S(2)}) collective-permute-start(bf16[16,16,256]{2,1,0:T(8,128)(2,1)S(1)} %get-tuple-element.142), channel_id=1, source_target_pairs={{0,12},{1,13},{2,14},{3,15},{4,0},{5,1},{6,2},{7,3},{8,4},{9,5},{1... | collective-permute-start | bytes 393224 | tf_op jit(solution)/shard_map/ppermute | solution.py:29
  108.1 11.6 %collective-permute-start.17 = (bf16[16,16,256]{2,1,0:T(8,128)(2,1)S(1)}, bf16[16,16,256]{2,1,0:T(8,128)(2,1)S(1)}, u32[]{:S(2)}, u32[]{:S(2)}) collective-permute-start(bf16[16,16,256]{2,1,0:T(8,128)(2,1)S(1)} %get-tuple-element.144), channel_id=1, source_target_pairs={{0,1},{1,2},{2,3},{3,0},{4,5},{5,6},{6,7},{7,4},{8,9},{9,10},{10,1... | collective-permute-start | bytes 393224 | tf_op jit(solution)/shard_map/ppermute | solution.py:33
  108.1 11.6 %collective-permute-start.18 = (bf16[16,16,256]{2,1,0:T(8,128)(2,1)S(1)}, bf16[16,16,256]{2,1,0:T(8,128)(2,1)S(1)}, u32[]{:S(2)}, u32[]{:S(2)}) collective-permute-start(bf16[16,16,256]{2,1,0:T(8,128)(2,1)S(1)} %get-tuple-element.145), channel_id=1, source_target_pairs={{0,3},{1,0},{2,1},{3,2},{4,7},{5,4},{6,5},{7,6},{8,11},{9,8},{10,9... | collective-permute-start | bytes 393224 | tf_op jit(solution)/shard_map/ppermute | solution.py:33
  121.2 5.1 %collective-permute-start.19 = (bf16[16,16,128]{2,1,0:T(8,128)(2,1)S(1)}, bf16[16,16,128]{2,1,0:T(8,128)(2,1)S(1)}, u32[]{:S(2)}, u32[]{:S(2)}) collective-permute-start(bf16[16,16,128]{2,1,0:T(8,128)(2,1)S(1)} %get-tuple-element.149), channel_id=1, source_target_pairs={{0,32},{16,48},{32,64},{48,80},{64,96},{80,112},{96,0},{112,16},{1... | collective-permute-start | bytes 196616 | tf_op jit(solution)/shard_map/ppermute | solution.py:19
  121.2 5.0 %collective-permute-start.20 = (bf16[16,16,128]{2,1,0:T(8,128)(2,1)S(1)}, bf16[16,16,128]{2,1,0:T(8,128)(2,1)S(1)}, u32[]{:S(2)}, u32[]{:S(2)}) collective-permute-start(bf16[16,16,128]{2,1,0:T(8,128)(2,1)S(1)} %get-tuple-element.150), channel_id=1, source_target_pairs={{0,64},{16,80},{32,96},{48,112},{64,0},{80,16},{96,32},{112,48},{1... | collective-permute-start | bytes 196616 | tf_op jit(solution)/shard_map/ppermute | solution.py:19
  122.8 4.0 %collective-permute-start.21 = (bf16[16,16,128]{2,1,0:T(8,128)(2,1)S(1)}, bf16[16,16,128]{2,1,0:T(8,128)(2,1)S(1)}, u32[]{:S(2)}, u32[]{:S(2)}) collective-permute-start(bf16[16,16,128]{2,1,0:T(8,128)(2,1)S(1)} %get-tuple-element.151), channel_id=1, source_target_pairs={{0,96},{16,112},{32,0},{48,16},{64,32},{80,48},{96,64},{112,80},{1... | collective-permute-start | bytes 196616 | tf_op jit(solution)/shard_map/ppermute | solution.py:19
  127.4 32.0 %copy-start.7 = (bf16[512,512]{1,0:T(8,128)(2,1)S(1)}, bf16[512,512]{1,0:T(8,128)(2,1)}, u32[]{:S(2)}) copy-start(bf16[512,512]{1,0:T(8,128)(2,1)} %w_agg.2) | copy-start | bytes 1572868
  127.4 7.2 %collective-permute-start.25 = (bf16[16,64,128]{2,1,0:T(8,128)(2,1)S(1)}, bf16[16,64,128]{2,1,0:T(8,128)(2,1)S(1)}, u32[]{:S(2)}, u32[]{:S(2)}) collective-permute-start(bf16[16,64,128]{2,1,0:T(8,128)(2,1)S(1)} %shard_map.191.rest_6_), channel_id=1, source_target_pairs={{0,15},{1,0},{2,1},{3,2},{4,3},{5,4},{6,5},{7,6},{8,7},{9,8},{10,9... | collective-permute-start | bytes 786440 | tf_op jit(solution)/shard_map/ppermute | solution.py:37
  129.4 9.2 %collective-permute-start.22 = (bf16[16,64,128]{2,1,0:T(8,128)(2,1)S(1)}, bf16[16,64,128]{2,1,0:T(8,128)(2,1)S(1)}, u32[]{:S(2)}, u32[]{:S(2)}) collective-permute-start(bf16[16,64,128]{2,1,0:T(8,128)(2,1)S(1)} %shard_map.191.rest_6_), channel_id=1, source_target_pairs={{0,1},{1,2},{2,3},{3,4},{4,5},{5,6},{6,7},{7,8},{8,9},{9,10},{10,1... | collective-permute-start | bytes 786440 | tf_op jit(solution)/shard_map/ppermute | solution.py:37
  129.4 15.0 %collective-permute-start.24 = (bf16[16,64,128]{2,1,0:T(8,128)(2,1)S(1)}, bf16[16,64,128]{2,1,0:T(8,128)(2,1)S(1)}, u32[]{:S(2)}, u32[]{:S(2)}) collective-permute-start(bf16[16,64,128]{2,1,0:T(8,128)(2,1)S(1)} %shard_map.191.rest_6_), channel_id=1, source_target_pairs={{0,16},{16,0},{32,48},{48,32},{64,80},{80,64},{96,112},{112,96},{1... | collective-permute-start | bytes 786440 | tf_op jit(solution)/shard_map/ppermute | solution.py:23
  134.7 9.7 %collective-permute-start.26 = (bf16[16,64,128]{2,1,0:T(8,128)(2,1)S(1)}, bf16[16,64,128]{2,1,0:T(8,128)(2,1)S(1)}, u32[]{:S(2)}, u32[]{:S(2)}) collective-permute-start(bf16[16,64,128]{2,1,0:T(8,128)(2,1)S(1)} %collective-permute-done.25.rest_8_), channel_id=1, source_target_pairs={{0,16},{16,0},{32,48},{48,32},{64,80},{80,64},{96,112},{112,96},{1... | collective-permute-start | bytes 786440 | tf_op jit(solution)/shard_map/ppermute | solution.py:23
  138.5 7.0 %collective-permute-start.23 = (bf16[16,64,128]{2,1,0:T(8,128)(2,1)S(1)}, bf16[16,64,128]{2,1,0:T(8,128)(2,1)S(1)}, u32[]{:S(2)}, u32[]{:S(2)}) collective-permute-start(bf16[16,64,128]{2,1,0:T(8,128)(2,1)S(1)} %collective-permute-done.22.rest_4_), channel_id=1, source_target_pairs={{0,16},{16,0},{32,48},{48,32},{64,80},{80,64},{96,112},{112,96},{1... | collective-permute-start | bytes 786440 | tf_op jit(solution)/shard_map/ppermute | solution.py:23
  150.0 1.6 collective-permute-start.27
  152.2 4.4 %collective-permute-start.28 = (bf16[16,16,128]{2,1,0:T(8,128)(2,1)S(1)}, bf16[16,16,128]{2,1,0:T(8,128)(2,1)S(1)}, u32[]{:S(2)}, u32[]{:S(2)}) collective-permute-start(bf16[16,16,128]{2,1,0:T(8,128)(2,1)S(1)} %get-tuple-element.155), channel_id=1, source_target_pairs={{0,32},{16,48},{32,64},{48,80},{64,96},{80,112},{96,0},{112,16},{1... | collective-permute-start | bytes 196616 | tf_op jit(solution)/shard_map/ppermute | solution.py:19
  153.2 5.8 %collective-permute-start.29 = (bf16[16,16,128]{2,1,0:T(8,128)(2,1)S(1)}, bf16[16,16,128]{2,1,0:T(8,128)(2,1)S(1)}, u32[]{:S(2)}, u32[]{:S(2)}) collective-permute-start(bf16[16,16,128]{2,1,0:T(8,128)(2,1)S(1)} %get-tuple-element.156), channel_id=1, source_target_pairs={{0,64},{16,80},{32,96},{48,112},{64,0},{80,16},{96,32},{112,48},{1... | collective-permute-start | bytes 196616 | tf_op jit(solution)/shard_map/ppermute | solution.py:19
  156.0 3.4 %collective-permute-start.30 = (bf16[16,16,128]{2,1,0:T(8,128)(2,1)S(1)}, bf16[16,16,128]{2,1,0:T(8,128)(2,1)S(1)}, u32[]{:S(2)}, u32[]{:S(2)}) collective-permute-start(bf16[16,16,128]{2,1,0:T(8,128)(2,1)S(1)} %get-tuple-element.157), channel_id=1, source_target_pairs={{0,96},{16,112},{32,0},{48,16},{64,32},{80,48},{96,64},{112,80},{1... | collective-permute-start | bytes 196616 | tf_op jit(solution)/shard_map/ppermute | solution.py:19
  160.8 4.4 %collective-permute-start.31 = (bf16[16,16,128]{2,1,0:T(8,128)(2,1)S(1)}, bf16[16,16,128]{2,1,0:T(8,128)(2,1)S(1)}, u32[]{:S(2)}, u32[]{:S(2)}) collective-permute-start(bf16[16,16,128]{2,1,0:T(8,128)(2,1)S(1)} %get-tuple-element.161), channel_id=1, source_target_pairs={{0,32},{16,48},{32,64},{48,80},{64,96},{80,112},{96,0},{112,16},{1... | collective-permute-start | bytes 196616 | tf_op jit(solution)/shard_map/ppermute | solution.py:19
  160.9 5.6 %collective-permute-start.32 = (bf16[16,16,128]{2,1,0:T(8,128)(2,1)S(1)}, bf16[16,16,128]{2,1,0:T(8,128)(2,1)S(1)}, u32[]{:S(2)}, u32[]{:S(2)}) collective-permute-start(bf16[16,16,128]{2,1,0:T(8,128)(2,1)S(1)} %get-tuple-element.162), channel_id=1, source_target_pairs={{0,64},{16,80},{32,96},{48,112},{64,0},{80,16},{96,32},{112,48},{1... | collective-permute-start | bytes 196616 | tf_op jit(solution)/shard_map/ppermute | solution.py:19
  164.2 3.4 %collective-permute-start.33 = (bf16[16,16,128]{2,1,0:T(8,128)(2,1)S(1)}, bf16[16,16,128]{2,1,0:T(8,128)(2,1)S(1)}, u32[]{:S(2)}, u32[]{:S(2)}) collective-permute-start(bf16[16,16,128]{2,1,0:T(8,128)(2,1)S(1)} %get-tuple-element.163), channel_id=1, source_target_pairs={{0,96},{16,112},{32,0},{48,16},{64,32},{80,48},{96,64},{112,80},{1... | collective-permute-start | bytes 196616 | tf_op jit(solution)/shard_map/ppermute | solution.py:19
  168.1 3.6 %collective-permute-start.34 = (bf16[16,64,128]{2,1,0:T(8,128)(2,1)S(1)}, bf16[16,64,128]{2,1,0:T(8,128)(2,1)S(1)}, u32[]{:S(2)}, u32[]{:S(2)}) collective-permute-start(bf16[16,64,128]{2,1,0:T(8,128)(2,1)S(1)} %shard_map.195.rest_4_), channel_id=1, source_target_pairs={{0,16},{16,0},{32,48},{48,32},{64,80},{80,64},{96,112},{112,96},{1... | collective-permute-start | bytes 786440 | tf_op jit(solution)/shard_map/ppermute | solution.py:23
  175.8 2.4 collective-permute-start.35
  178.3 7.6 %collective-permute-start.36 = (bf16[16,64,128]{2,1,0:T(8,128)(2,1)S(1)}, bf16[16,64,128]{2,1,0:T(8,128)(2,1)S(1)}, u32[]{:S(2)}, u32[]{:S(2)}) collective-permute-start(bf16[16,64,128]{2,1,0:T(8,128)(2,1)S(1)} %get-tuple-element.166), channel_id=1, source_target_pairs={{0,15},{1,0},{2,1},{3,2},{4,3},{5,4},{6,5},{7,6},{8,7},{9,8},{10,9... | collective-permute-start | bytes 786440 | tf_op jit(solution)/shard_map/ppermute | solution.py:37
  178.5 10.5 %collective-permute-start.37 = (bf16[16,64,128]{2,1,0:T(8,128)(2,1)S(1)}, bf16[16,64,128]{2,1,0:T(8,128)(2,1)S(1)}, u32[]{:S(2)}, u32[]{:S(2)}) collective-permute-start(bf16[16,64,128]{2,1,0:T(8,128)(2,1)S(1)} %get-tuple-element.170), channel_id=1, source_target_pairs={{0,1},{1,2},{2,3},{3,4},{4,5},{5,6},{6,7},{7,8},{8,9},{9,10},{10,1... | collective-permute-start | bytes 786440 | tf_op jit(solution)/shard_map/ppermute | solution.py:37
  179.9 13.3 %collective-permute-start.43 = (bf16[256,512]{1,0:T(8,128)(2,1)S(1)}, bf16[256,512]{1,0:T(8,128)(2,1)S(1)}, u32[]{:S(2)}, u32[]{:S(2)}) collective-permute-start(bf16[256,512]{1,0:T(8,128)(2,1)S(1)} %get-tuple-element.184.p0), channel_id=1, source_target_pairs={{0,96},{16,112},{32,0},{48,16},{64,32},{80,48},{96,64},{112,80},{1... | collective-permute-start | bytes 786440 | tf_op jit(solution)/shard_map/ppermute | solution.py:19
  182.1 11.4 %collective-permute-start.42 = (bf16[256,512]{1,0:T(8,128)(2,1)S(1)}, bf16[256,512]{1,0:T(8,128)(2,1)S(1)}, u32[]{:S(2)}, u32[]{:S(2)}) collective-permute-start(bf16[256,512]{1,0:T(8,128)(2,1)S(1)} %get-tuple-element.184.p0), channel_id=1, source_target_pairs={{0,64},{16,80},{32,96},{48,112},{64,0},{80,16},{96,32},{112,48},{1... | collective-permute-start | bytes 786440 | tf_op jit(solution)/shard_map/ppermute | solution.py:19
  182.5 15.1 %collective-permute-start.41 = (bf16[256,512]{1,0:T(8,128)(2,1)S(1)}, bf16[256,512]{1,0:T(8,128)(2,1)S(1)}, u32[]{:S(2)}, u32[]{:S(2)}) collective-permute-start(bf16[256,512]{1,0:T(8,128)(2,1)S(1)} %get-tuple-element.184.p0), channel_id=1, source_target_pairs={{0,32},{16,48},{32,64},{48,80},{64,96},{80,112},{96,0},{112,16},{1... | collective-permute-start | bytes 786440 | tf_op jit(solution)/shard_map/ppermute | solution.py:19
  189.7 9.8 %collective-permute-start.38 = (bf16[16,16,128]{2,1,0:T(8,128)(2,1)S(1)}, bf16[16,16,128]{2,1,0:T(8,128)(2,1)S(1)}, u32[]{:S(2)}, u32[]{:S(2)}) collective-permute-start(bf16[16,16,128]{2,1,0:T(8,128)(2,1)S(1)} %get-tuple-element.172), channel_id=1, source_target_pairs={{0,32},{16,48},{32,64},{48,80},{64,96},{80,112},{96,0},{112,16},{1... | collective-permute-start | bytes 196616 | tf_op jit(solution)/shard_map/ppermute | solution.py:19
  190.6 8.9 %collective-permute-start.39 = (bf16[16,16,128]{2,1,0:T(8,128)(2,1)S(1)}, bf16[16,16,128]{2,1,0:T(8,128)(2,1)S(1)}, u32[]{:S(2)}, u32[]{:S(2)}) collective-permute-start(bf16[16,16,128]{2,1,0:T(8,128)(2,1)S(1)} %get-tuple-element.173), channel_id=1, source_target_pairs={{0,64},{16,80},{32,96},{48,112},{64,0},{80,16},{96,32},{112,48},{1... | collective-permute-start | bytes 196616 | tf_op jit(solution)/shard_map/ppermute | solution.py:19
  193.1 6.4 %collective-permute-start.40 = (bf16[16,16,128]{2,1,0:T(8,128)(2,1)S(1)}, bf16[16,16,128]{2,1,0:T(8,128)(2,1)S(1)}, u32[]{:S(2)}, u32[]{:S(2)}) collective-permute-start(bf16[16,16,128]{2,1,0:T(8,128)(2,1)S(1)} %get-tuple-element.174), channel_id=1, source_target_pairs={{0,96},{16,112},{32,0},{48,16},{64,32},{80,48},{96,64},{112,80},{1... | collective-permute-start | bytes 196616 | tf_op jit(solution)/shard_map/ppermute | solution.py:19
  200.9 4.4 %collective-permute-start.46 = (bf16[16,16,256]{2,1,0:T(8,128)(2,1)S(1)}, bf16[16,16,256]{2,1,0:T(8,128)(2,1)S(1)}, u32[]{:S(2)}, u32[]{:S(2)}) collective-permute-start(bf16[16,16,256]{2,1,0:T(8,128)(2,1)S(1)} %get-tuple-element.180.refs_0_), channel_id=1, source_target_pairs={{0,12},{1,13},{2,14},{3,15},{4,0},{5,1},{6,2},{7,3},{8,4},{9,5},{1... | collective-permute-start | bytes 393224 | tf_op jit(solution)/shard_map/ppermute | solution.py:29
  201.0 5.4 %collective-permute-start.45 = (bf16[16,16,256]{2,1,0:T(8,128)(2,1)S(1)}, bf16[16,16,256]{2,1,0:T(8,128)(2,1)S(1)}, u32[]{:S(2)}, u32[]{:S(2)}) collective-permute-start(bf16[16,16,256]{2,1,0:T(8,128)(2,1)S(1)} %get-tuple-element.180.refs_0_), channel_id=1, source_target_pairs={{0,8},{1,9},{2,10},{3,11},{4,12},{5,13},{6,14},{7,15},{8,0},{9,1},... | collective-permute-start | bytes 393224 | tf_op jit(solution)/shard_map/ppermute | solution.py:29
  202.4 6.5 %collective-permute-start.44 = (bf16[16,16,256]{2,1,0:T(8,128)(2,1)S(1)}, bf16[16,16,256]{2,1,0:T(8,128)(2,1)S(1)}, u32[]{:S(2)}, u32[]{:S(2)}) collective-permute-start(bf16[16,16,256]{2,1,0:T(8,128)(2,1)S(1)} %get-tuple-element.180.refs_0_), channel_id=1, source_target_pairs={{0,4},{1,5},{2,6},{3,7},{4,8},{5,9},{6,10},{7,11},{8,12},{9,13},{1... | collective-permute-start | bytes 393224 | tf_op jit(solution)/shard_map/ppermute | solution.py:29
  202.4 6.5 %collective-permute-start.49 = (bf16[16,16,256]{2,1,0:T(8,128)(2,1)S(1)}, bf16[16,16,256]{2,1,0:T(8,128)(2,1)S(1)}, u32[]{:S(2)}, u32[]{:S(2)}) collective-permute-start(bf16[16,16,256]{2,1,0:T(8,128)(2,1)S(1)} %get-tuple-element.181.refs_4_), channel_id=1, source_target_pairs={{0,3},{1,0},{2,1},{3,2},{4,7},{5,4},{6,5},{7,6},{8,11},{9,8},{10,9... | collective-permute-start | bytes 393224 | tf_op jit(solution)/shard_map/ppermute | solution.py:33
  205.3 5.4 %collective-permute-start.48 = (bf16[16,16,256]{2,1,0:T(8,128)(2,1)S(1)}, bf16[16,16,256]{2,1,0:T(8,128)(2,1)S(1)}, u32[]{:S(2)}, u32[]{:S(2)}) collective-permute-start(bf16[16,16,256]{2,1,0:T(8,128)(2,1)S(1)} %get-tuple-element.181.refs_4_), channel_id=1, source_target_pairs={{0,2},{1,3},{2,0},{3,1},{4,6},{5,7},{6,4},{7,5},{8,10},{9,11},{10,... | collective-permute-start | bytes 393224 | tf_op jit(solution)/shard_map/ppermute | solution.py:33
  205.3 6.4 %collective-permute-start.47 = (bf16[16,16,256]{2,1,0:T(8,128)(2,1)S(1)}, bf16[16,16,256]{2,1,0:T(8,128)(2,1)S(1)}, u32[]{:S(2)}, u32[]{:S(2)}) collective-permute-start(bf16[16,16,256]{2,1,0:T(8,128)(2,1)S(1)} %get-tuple-element.181.refs_4_), channel_id=1, source_target_pairs={{0,1},{1,2},{2,3},{3,0},{4,5},{5,6},{6,7},{7,4},{8,9},{9,10},{10,1... | collective-permute-start | bytes 393224 | tf_op jit(solution)/shard_map/ppermute | solution.py:33
  211.8 9.1 %collective-permute-start.52 = (bf16[4,16,16,256]{3,2,1,0:T(8,128)(2,1)S(1)}, bf16[4,16,16,256]{3,2,1,0:T(8,128)(2,1)S(1)}, u32[]{:S(2)}, u32[]{:S(2)}) collective-permute-start(bf16[4,16,16,256]{3,2,1,0:T(8,128)(2,1)S(1)} %get-tuple-element.182.rest_0_), channel_id=1, source_target_pairs={{0,3},{1,0},{2,1},{3,2},{4,7},{5,4},{6,5},{7,6},{8,11},{9,8},{10,9... | collective-permute-start | bytes 1572872 | tf_op jit(solution)/shard_map/ppermute | solution.py:33
  212.8 10.7 %collective-permute-start.51 = (bf16[4,16,16,256]{3,2,1,0:T(8,128)(2,1)S(1)}, bf16[4,16,16,256]{3,2,1,0:T(8,128)(2,1)S(1)}, u32[]{:S(2)}, u32[]{:S(2)}) collective-permute-start(bf16[4,16,16,256]{3,2,1,0:T(8,128)(2,1)S(1)} %get-tuple-element.182.rest_0_), channel_id=1, source_target_pairs={{0,2},{1,3},{2,0},{3,1},{4,6},{5,7},{6,4},{7,5},{8,10},{9,11},{10,... | collective-permute-start | bytes 1572872 | tf_op jit(solution)/shard_map/ppermute | solution.py:33
  212.8 26.5 %collective-permute-start.50 = (bf16[4,16,16,256]{3,2,1,0:T(8,128)(2,1)S(1)}, bf16[4,16,16,256]{3,2,1,0:T(8,128)(2,1)S(1)}, u32[]{:S(2)}, u32[]{:S(2)}) collective-permute-start(bf16[4,16,16,256]{3,2,1,0:T(8,128)(2,1)S(1)} %get-tuple-element.182.rest_0_), channel_id=1, source_target_pairs={{0,1},{1,2},{2,3},{3,0},{4,5},{5,6},{6,7},{7,4},{8,9},{9,10},{10,1... | collective-permute-start | bytes 1572872 | tf_op jit(solution)/shard_map/ppermute | solution.py:33
  213.5 25.9 %collective-permute-start.55 = (bf16[4,16,16,256]{3,2,1,0:T(8,128)(2,1)S(1)}, bf16[4,16,16,256]{3,2,1,0:T(8,128)(2,1)S(1)}, u32[]{:S(2)}, u32[]{:S(2)}) collective-permute-start(bf16[4,16,16,256]{3,2,1,0:T(8,128)(2,1)S(1)} %get-tuple-element.183.rest_4_), channel_id=1, source_target_pairs={{0,12},{1,13},{2,14},{3,15},{4,0},{5,1},{6,2},{7,3},{8,4},{9,5},{1... | collective-permute-start | bytes 1572872 | tf_op jit(solution)/shard_map/ppermute | solution.py:29
  216.0 23.4 %collective-permute-start.54 = (bf16[4,16,16,256]{3,2,1,0:T(8,128)(2,1)S(1)}, bf16[4,16,16,256]{3,2,1,0:T(8,128)(2,1)S(1)}, u32[]{:S(2)}, u32[]{:S(2)}) collective-permute-start(bf16[4,16,16,256]{3,2,1,0:T(8,128)(2,1)S(1)} %get-tuple-element.183.rest_4_), channel_id=1, source_target_pairs={{0,8},{1,9},{2,10},{3,11},{4,12},{5,13},{6,14},{7,15},{8,0},{9,1},... | collective-permute-start | bytes 1572872 | tf_op jit(solution)/shard_map/ppermute | solution.py:29
  220.9 18.4 %collective-permute-start.53 = (bf16[4,16,16,256]{3,2,1,0:T(8,128)(2,1)S(1)}, bf16[4,16,16,256]{3,2,1,0:T(8,128)(2,1)S(1)}, u32[]{:S(2)}, u32[]{:S(2)}) collective-permute-start(bf16[4,16,16,256]{3,2,1,0:T(8,128)(2,1)S(1)} %get-tuple-element.183.rest_4_), channel_id=1, source_target_pairs={{0,4},{1,5},{2,6},{3,7},{4,8},{5,9},{6,10},{7,11},{8,12},{9,13},{1... | collective-permute-start | bytes 1572872 | tf_op jit(solution)/shard_map/ppermute | solution.py:29
  242.4 59.3 %all-to-all-start.1 = ((bf16[8,32,16,512]{3,2,1,0:T(8,128)(2,1)}), bf16[8,32,16,512]{3,2,1,0:T(8,128)(2,1)}, u32[]{:S(2)}, u32[]{:S(2)}) async-start(bf16[8,32,16,512]{3,2,1,0:T(8,128)(2,1)} %shard_map.201), calls=%async_computation.1 | async-start | bytes 8388608 | tf_op jit(solution)/shard_map/all_to_all | solution.py:543
  253.5 2.7 collective-permute-start.56
  (9 other events, 63.0 us)

commit v5 on v4

--- a/solution.py
+++ b/solution.py
@@ -174,7 +174,7 @@
 
 
 PARTS = [((4, 16, 16, 256), BF16)] * 2 + [((2, 16, 16, 256), BF16)] * 2 + [((4, 16, 16, 256), BF16)]
-SMALL = [((16, 16, 256), BF16)] * 2 + [((8, 16, 256), BF16)] * 2 + [((16, 16, 256), BF16)]
+SMALL = [((16, 16, 256), BF16)] * 4
 
 
 def combine(ids, meta, arrived):
@@ -215,20 +215,16 @@
 def add_rows_body(*refs):
     for q in range(2):
         a, b, c = refs[3 * q : 3 * q + 3]
-        outs = refs[6 + 5 * q : 11 + 5 * q]
+        outs = refs[6 + 4 * q : 10 + 4 * q]
         for j in range(4):
-            total = (a[j].astype(F32) + b[j].astype(F32) + c[j].astype(F32)).astype(BF16)
-            if j == 2:
-                outs[2][...] = total[:8]
-                outs[3][...] = total[8:]
-            else:
-                outs[{0: 0, 1: 1, 3: 4}[j]][...] = total
+            outs[j][...] = (a[j].astype(F32) + b[j].astype(F32) + c[j].astype(F32)).astype(BF16)
 
 
 def reduce_halves(by_y, by_x):
     by_y, by_x = relay(by_y, over_y, by_x, over_x)
     sums = local(add_rows_body, SMALL * 2, [*by_y, *by_x], smem=0)
-    left, right = relay(sums[:5], over_x, sums[5:], over_y)
+    left = [sums[0]] + [over_x(sums[k], k) for k in (1, 2, 3)]
+    right = [sums[4]] + [over_y(sums[4 + k], k) for k in (1, 2, 3)]
     return [*left, *right]
 
 
@@ -244,13 +240,14 @@
 
 
 def enc_mlp_body(ids, *rest):
-    terms, (pre_self, rows, w_agg, w_out, w_pass, pre_ref, first_ref) = rest[:6], rest[6:13]
-    outs, wide = rest[13:17], rest[17]
+    terms, (pre_self, rows, w_agg, w_out, w_pass, pre_ref, first_ref) = rest[:8], rest[8:15]
+    outs, wide = rest[15:19], rest[19]
     z = ids[0]
     pre = pre_self[...]
     for q in range(2):
-        a, b, c = terms[3 * q : 3 * q + 3]
-        total = a[...].astype(F32) + b[...].astype(F32) + c[...].astype(F32)
+        total = terms[4 * q][...].astype(F32)
+        for more in terms[4 * q + 1 : 4 * q + 4]:
+            total += more[...].astype(F32)
         pre += dot(total.astype(BF16).reshape(256, 256), w_agg[256 * q : 256 * q + 256, :])
     pre_ref[...] = pre
     hidden = jax.nn.silu(pre).astype(BF16)

time: 310 us -> 318 us (1.026)
  waiting for transfers between devices: 120 us -> 136 us
  starting transfers between devices: 94 us -> 85.9 us
    ppermute x18, waiting for transfers between devices: 23.6 us -> 33.5 us  [over_z(): lax.ppermute(array, 'grid', [(2 * z + c, 2 * ((z + by) % 4) + c) for z in...]
    ppermute x7, starting transfers between devices: 18.4 us -> 10.9 us  [over_column(): lax.ppermute(array, 'grid', [(2 * z + c, 2 * ((z + dz) % 4) + (c ^ dc)) f...]
    ppermute x4, waiting for transfers between devices: 6.38 us -> 11.2 us  [over_mesh(): return lax.ppermute(array, 'mesh', [(p, (p + by) % 16) for p in range(16)])]
    ppermute x14 -> x13, starting transfers between devices: 16.2 us -> 12.2 us  [over_y(): lax.ppermute(array, 'mesh', [(4 * x + y, 4 * x + (y + by) % 4) for x in r...]
    ppermute x4, starting transfers between devices: 3.49 us -> 7.06 us  [over_mesh(): return lax.ppermute(array, 'mesh', [(p, (p + by) % 16) for p in range(16)])]
    ppermute x14 -> x13, waiting for transfers between devices: 31.4 us -> 33.7 us  [over_y(): lax.ppermute(array, 'mesh', [(4 * x + y, 4 * x + (y + by) % 4) for x in r...]
    ppermute x14 -> x13, starting transfers between devices: 17.8 us -> 16.4 us  [over_x(): lax.ppermute(array, 'mesh', [(4 * x + y, 4 * ((x + by) % 4) + y) for x in...]
    ppermute x14 -> x13, waiting for transfers between devices: 7.08 us -> 6.16 us  [over_x(): lax.ppermute(array, 'mesh', [(4 * x + y, 4 * ((x + by) % 4) + y) for x in...]
  transfers between devices with their start and end apart: 59 -> 57, of which waited for: 31 -> 34; matrix products, arithmetic and copies ran while one was open for 1% -> 1% of each run, Pallas kernels for 1% -> 1%
where the time goes in v5:
time: 318 us
  waiting for transfers between devices  136 us (43%)
  starting transfers between devices  85.9 us (27%)
  blocking collectives  47.1 us (15%)
  Pallas kernels  43.2 us (14%)
    optimization_barrier x1, blocking collectives, per_device(): lax.optimization_barrier((arrived, meta, proc_mask))  47.1 us
    all_to_all x2, waiting for transfers between devices, column_exchange(): return lax.all_to_all(pieces, 'grid', 0, 0, tiled=True)  43.5 us
    ppermute x13, waiting for transfers between devices, over_y(): lax.ppermute(array, 'mesh', [(4 * x + y, 4 * x + (y + by) % 4) for x in r...  33.7 us
    ppermute x18, waiting for transfers between devices, over_z(): lax.ppermute(array, 'grid', [(2 * z + c, 2 * ((z + by) % 4) + c) for z in...  33.5 us
    ppermute x18, starting transfers between devices, over_z(): lax.ppermute(array, 'grid', [(2 * z + c, 2 * ((z + by) % 4) + c) for z in...  22 us
    pallas_call x15, Pallas kernels, local(): pl.pallas_call(body, out_shape=[jax.ShapeDtypeStruct(shape, dtype) for sh...  21.4 us
    all_to_all x2, starting transfers between devices, column_exchange(): return lax.all_to_all(pieces, 'grid', 0, 0, tiled=True)  17.4 us
    ppermute x13, starting transfers between devices, over_x(): lax.ppermute(array, 'mesh', [(4 * x + y, 4 * ((x + by) % 4) + y) for x in...  16.4 us
  transfers between devices with their start and end apart: 57, of which 34 were waited for; matrix products, arithmetic and copies ran while one was open for 1% of the time, Pallas kernels for 1%

profile of v5, /device:TPU:1, one launch (start us, length us, event | category | flops | bytes accessed | tf_op | source)
XLA Modules:
  0.0 317.6 jit_solution(8475685798130478402)
XLA Ops:
  0.7 8.9 %shard_map.185 = (bf16[8,32,16,512]{3,2,1,0:T(8,128)(2,1)}, bf16[16,128,128]{2,1,0:T(8,128)(2,1)}) custom-call(s32[32]{0:T(128)} %source.3, bf16[3072,512]{1,0:T(8,128)(2,1)} %latent.1, bf16[512,512]{1,0:T(8,128)(2,1)} %w_send.3, s32[32,128,128]{2,1,0:T(8,128)} %mask.3, s32[16,128,128]{2,1,0:T(8,128)} %other.1), custom_call_target="tpu_custom_call" | custom-call | tf_op jit(solution)/shard_map/pallas_call | solution.py:126
  9.6 7.0 %all-to-all-start = ((bf16[8,32,16,512]{3,2,1,0:T(8,128)(2,1)}), bf16[8,32,16,512]{3,2,1,0:T(8,128)(2,1)}, u32[]{:S(2)}, u32[]{:S(2)}) async-start(bf16[8,32,16,512]{3,2,1,0:T(8,128)(2,1)} %get-tuple-element.93), calls=%async_computation | async-start | bytes 8388608 | tf_op jit(solution)/shard_map/all_to_all | solution.py:540
  16.7 1.1 constant_dynamic-slice_fusion
  20.0 47.1 %all-reduce.meta = s32[512]{0:T(512)S(1)} all-reduce(s32[512]{0:T(512)S(1)} %dynamic-update-slice), channel_id=1, replica_groups=mesh['grid'=8,'mesh'=16] {'grid'}, use_global_device_ids=true, to_apply=%add | all-reduce | flops 512 | bytes 4096 | tf_op jit(solution)/shard_map/optimization_barrier | solution.py:585
  67.2 4.8 %shard_map.186 = (bf16[4,16,16,256]{3,2,1,0:T(8,128)(2,1)S(1)}, bf16[4,16,16,256]{3,2,1,0:T(8,128)(2,1)S(1)}, bf16[2,16,16,256]{3,2,1,0:T(8,128)(2,1)S(1)}, bf16...) custom-call(s32[4]{0:T(128)S(1)} %pad_add_fusion.ids, ...), custom_call_target="tpu_custom_call" | custom-call | tf_op jit(solution)/shard_map/pallas_call | solution.py:41
  72.0 1.4 collective-permute-start.3
  73.4 1.5 collective-permute-start.4
  74.9 1.2 collective-permute-start.5
  76.1 1.5 collective-permute-start.6
  77.6 1.6 collective-permute-done.3.refs_2_
  79.2 2.4 collective-permute-done.5.refs_6_
  82.1 2.7 collective-permute-start.8
  84.7 1.2 collective-permute-start.9
  85.9 1.5 collective-permute-start.10
  87.4 1.3 collective-permute-start.2
  88.7 4.4 %collective-permute-done.7.refs_1_ = bf16[4,16,16,256]{3,2,1,0:T(8,128)(2,1)S(1)} collective-permute-done((bf16[4,16,16,256]{3,2,1,0:T(8,128)(2,1)S(1)}, bf16[4,16,16,256]{3,2,1,0:T(8,128)(2,1)S(1)}, u32[]{:S(2)}, u32[]{:S(2)}) %collective-permute-start.7) | collective-permute-done | bytes 524320 | tf_op jit(solution)/shard_map/ppermute | solution.py:33
  93.1 1.8 collective-permute-start.1
  97.0 2.7 collective-permute-start.12
  100.4 3.3 %collective-permute-done.1.rest_2_ = bf16[16,128,128]{2,1,0:T(8,128)(2,1)S(1)} collective-permute-done((bf16[16,128,128]{2,1,0:T(8,128)(2,1)S(1)}, bf16[16,128,128]{2,1,0:T(8,128)(2,1)S(1)}, u32[]{:S(2)}, u32[]{:S(2)}) %collective-permute-start.1) | collective-permute-done | bytes 524320 | tf_op jit(solution)/shard_map/ppermute | solution.py:19
  103.7 16.0 %collective-permute-done.rest_1_ = bf16[16,128,128]{2,1,0:T(8,128)(2,1)S(1)} collective-permute-done((bf16[16,128,128]{2,1,0:T(8,128)(2,1)S(1)}, bf16[16,128,128]{2,1,0:T(8,128)(2,1)S(1)}, u32[]{:S(2)}, u32[]{:S(2)}) %collective-permute-start) | collective-permute-done | bytes 524320 | tf_op jit(solution)/shard_map/ppermute | solution.py:19
  120.8 5.0 %collective-permute-done.15.rest_6_ = bf16[16,16,256]{2,1,0:T(8,128)(2,1)S(1)} collective-permute-done((bf16[16,16,256]{2,1,0:T(8,128)(2,1)S(1)}, bf16[16,16,256]{2,1,0:T(8,128)(2,1)S(1)}, u32[]{:S(2)}, u32[]{:S(2)}) %collective-permute-start.15) | collective-permute-done | bytes 131104 | tf_op jit(solution)/shard_map/ppermute | solution.py:33
  125.8 1.4 shard_map.189
  127.3 2.0 collective-permute-start.18
  129.3 2.0 collective-permute-start.19
  133.7 5.5 %collective-permute-start.23 = (bf16[16,64,128]{2,1,0:T(8,128)(2,1)S(1)}, bf16[16,64,128]{2,1,0:T(8,128)(2,1)S(1)}, u32[]{:S(2)}, u32[]{:S(2)}) collective-permute-start(bf16[16,64,128]{2,1,0:T(8,128)(2,1)S(1)} %shard_map.190.rest_6_), channel_id=1, source_target_pairs={{0,15},{1,0},{2,1},{3,2},{4,3},{5,4},{6,5},{7,6},{8,7},{9,8},{10,9... | collective-permute-start | bytes 786440 | tf_op jit(solution)/shard_map/ppermute | solution.py:37
  139.3 2.0 collective-permute-start.22
  141.3 1.9 collective-permute-done.23.rest_8_
  143.2 2.6 collective-permute-start.24
  145.8 2.6 collective-permute-done.20.rest_4_
  148.4 2.9 collective-permute-start.21
  151.3 1.2 collective-permute-done.21.rest_5_
  152.5 4.5 %shard_map.191 = (f32[16,64,128]{2,1,0:T(8,128)S(1)}, bf16[16,64,128]{2,1,0:T(8,128)(2,1)S(1)}) custom-call(s32[4]{0:T(128)S(1)} %pad_add_fusion.ids, s32[512]{0:T(512)S(1)} %all-reduce.meta, bf16[16,128,128]{2,1,0:T(8,128)(2,1)S(1)} %copy-done.2, bf16[16,128,128]{2,1,0:T(8,128)(2,1)S(1)} %collective-permute-done.rest_1_, ...), custom_call_target="tpu_custom_call" | custom-call | tf_op jit(solution)/shard_map/pallas_call | solution.py:41
  157.4 1.2 collective-permute-done.25.other
  160.3 3.3 %collective-permute-start.27 = (bf16[16,16,128]{2,1,0:T(8,128)(2,1)S(1)}, bf16[16,16,128]{2,1,0:T(8,128)(2,1)S(1)}, u32[]{:S(2)}, u32[]{:S(2)}) collective-permute-start(bf16[16,16,128]{2,1,0:T(8,128)(2,1)S(1)} %get-tuple-element.144), channel_id=1, source_target_pairs={{0,64},{16,80},{32,96},{48,112},{64,0},{80,16},{96,32},{112,48},{1... | collective-permute-start | bytes 196616 | tf_op jit(solution)/shard_map/ppermute | solution.py:19
  164.5 2.0 collective-permute-done.27.p2
  167.0 1.4 shard_map.193
  168.5 3.3 %collective-permute-start.30 = (bf16[16,16,128]{2,1,0:T(8,128)(2,1)S(1)}, bf16[16,16,128]{2,1,0:T(8,128)(2,1)S(1)}, u32[]{:S(2)}, u32[]{:S(2)}) collective-permute-start(bf16[16,16,128]{2,1,0:T(8,128)(2,1)S(1)} %get-tuple-element.150), channel_id=1, source_target_pairs={{0,64},{16,80},{32,96},{48,112},{64,0},{80,16},{96,32},{112,48},{1... | collective-permute-start | bytes 196616 | tf_op jit(solution)/shard_map/ppermute | solution.py:19
  172.8 1.4 collective-permute-done.30.p2
  175.8 2.4 collective-permute-start.32
  178.1 1.2 collective-permute-done.32.rest_5_
  179.3 4.1 %shard_map.195 = (f32[48,64,128]{2,1,0:T(8,128)S(1)}, bf16[48,64,128]{2,1,0:T(8,128)(2,1)S(1)}) custom-call(s32[4]{0:T(128)S(1)} %pad_add_fusion.ids, s32[512]{0:T(512)S(1)} %all-reduce.meta, bf16[16,128,128]{2,1,0:T(8,128)(2,1)S(1)} %copy-done.2, bf16[16,128,128]{2,1,0:T(8,128)(2,1)S(1)} %collective-permute-done.rest_1_, ...), custom_call_target="tpu_custom_call" | custom-call | tf_op jit(solution)/shard_map/pallas_call | solution.py:41
  183.8 1.9 collective-permute-done.33.other
  187.4 2.2 collective-permute-start.41
  190.2 3.3 %collective-permute-done.34.a = bf16[16,64,128]{2,1,0:T(8,128)(2,1)S(1)} collective-permute-done((bf16[16,64,128]{2,1,0:T(8,128)(2,1)S(1)}, bf16[16,64,128]{2,1,0:T(8,128)(2,1)S(1)}, u32[]{:S(2)}, u32[]{:S(2)}) %collective-permute-start.34) | collective-permute-done | bytes 262176 | tf_op jit(solution)/shard_map/ppermute | solution.py:37
  193.5 3.4 %collective-permute-done.35.c = bf16[16,64,128]{2,1,0:T(8,128)(2,1)S(1)} collective-permute-done((bf16[16,64,128]{2,1,0:T(8,128)(2,1)S(1)}, bf16[16,64,128]{2,1,0:T(8,128)(2,1)S(1)}, u32[]{:S(2)}, u32[]{:S(2)}) %collective-permute-start.35) | collective-permute-done | bytes 262176 | tf_op jit(solution)/shard_map/ppermute | solution.py:37
  198.4 2.5 collective-permute-start.37
  201.3 3.8 %collective-permute-done.39.p1 = bf16[256,512]{1,0:T(8,128)(2,1)S(1)} collective-permute-done((bf16[256,512]{1,0:T(8,128)(2,1)S(1)}, bf16[256,512]{1,0:T(8,128)(2,1)S(1)}, u32[]{:S(2)}, u32[]{:S(2)}) %collective-permute-start.39) | collective-permute-done | bytes 262176 | tf_op jit(solution)/shard_map/ppermute | solution.py:19
  205.1 1.9 collective-permute-done.36.p1
  207.1 1.3 shard_map.198
  208.6 1.4 collective-permute-start.42
  210.0 3.2 collective-permute-start.47
  214.0 3.5 %collective-permute-done.42.refs_1_ = bf16[16,16,256]{2,1,0:T(8,128)(2,1)S(1)} collective-permute-done((bf16[16,16,256]{2,1,0:T(8,128)(2,1)S(1)}, bf16[16,16,256]{2,1,0:T(8,128)(2,1)S(1)}, u32[]{:S(2)}, u32[]{:S(2)}) %collective-permute-start.42) | collective-permute-done | bytes 131104 | tf_op jit(solution)/shard_map/ppermute | solution.py:29
  217.4 1.1 collective-permute-done.46.refs_6_
  221.3 2.5 collective-permute-start.53
  223.8 1.2 collective-permute-start.52
  225.0 3.8 %collective-permute-done.50.rest_3_ = bf16[4,16,16,256]{3,2,1,0:T(8,128)(2,1)S(1)} collective-permute-done((bf16[4,16,16,256]{3,2,1,0:T(8,128)(2,1)S(1)}, bf16[4,16,16,256]{3,2,1,0:T(8,128)(2,1)S(1)}, u32[]{:S(2)}, u32[]{:S(2)}) %collective-permute-start.50) | collective-permute-done | bytes 524320 | tf_op jit(solution)/shard_map/ppermute | solution.py:33
  228.8 1.7 collective-permute-start.51
  231.3 15.9 %collective-permute-done.48.rest_1_ = bf16[4,16,16,256]{3,2,1,0:T(8,128)(2,1)S(1)} collective-permute-done((bf16[4,16,16,256]{3,2,1,0:T(8,128)(2,1)S(1)}, bf16[4,16,16,256]{3,2,1,0:T(8,128)(2,1)S(1)}, u32[]{:S(2)}, u32[]{:S(2)}) %collective-permute-start.48) | collective-permute-done | bytes 524320 | tf_op jit(solution)/shard_map/ppermute | solution.py:33
  247.2 3.1 shard_map.200
  250.3 10.4 %all-to-all-start.1 = ((bf16[8,32,16,512]{3,2,1,0:T(8,128)(2,1)}), bf16[8,32,16,512]{3,2,1,0:T(8,128)(2,1)}, u32[]{:S(2)}, u32[]{:S(2)}) async-start(bf16[8,32,16,512]{3,2,1,0:T(8,128)(2,1)} %shard_map.200), calls=%async_computation.1 | async-start | bytes 8388608 | tf_op jit(solution)/shard_map/all_to_all | solution.py:540
  261.4 2.6 collective-permute-done.54.theirs
  264.1 2.0 shard_map.202
  266.1 43.5 %all-to-all-done.1.pieces = bf16[8,32,16,512]{3,2,1,0:T(8,128)(2,1)} async-done(((bf16[8,32,16,512]{3,2,1,0:T(8,128)(2,1)}), bf16[8,32,16,512]{3,2,1,0:T(8,128)(2,1)}, u32[]{:S(2)}, u32[]{:S(2)}) %all-to-all-start.1) | async-done | bytes 4194336 | tf_op jit(solution)/shard_map/all_to_all | solution.py:540
  309.6 7.8 %shard_map.203 = bf16[3072,512]{1,0:T(8,128)(2,1)} custom-call(s32[32]{0:T(128)} %source.3, bf16[512,512]{1,0:T(8,128)(2,1)} %w_send.3, s32[32,128,128]{2,1,0:T(8,128)} %mask.3, bf16[8,32,16,512]{3,2,1,0:T(8,128)(2,1)} %all-to-all-done.1.pieces), custom_call_target="tpu_custom_call" | custom-call | tf_op jit(solution)/shard_map/pallas_call | solution.py:518
  (109 shorter events, 24.7 us)
Async XLA Ops:
  0.6 162.9 %copy-start = (bf16[512,512]{1,0:T(8,128)(2,1)S(1)}, bf16[512,512]{1,0:T(8,128)(2,1)}, u32[]{:S(2)}) copy-start(bf16[512,512]{1,0:T(8,128)(2,1)} %param.26) | copy-start | bytes 1572868
  9.6 8.2 %copy-start.3 = (bf16[512,512]{1,0:T(8,128)(2,1)S(1)}, bf16[512,512]{1,0:T(8,128)(2,1)}, u32[]{:S(2)}) copy-start(bf16[512,512]{1,0:T(8,128)(2,1)} %w_out.2) | copy-start | bytes 1572868
  9.6 57.6 %all-to-all-start = ((bf16[8,32,16,512]{3,2,1,0:T(8,128)(2,1)}), bf16[8,32,16,512]{3,2,1,0:T(8,128)(2,1)}, u32[]{:S(2)}, u32[]{:S(2)}) async-start(bf16[8,32,16,512]{3,2,1,0:T(8,128)(2,1)} %get-tuple-element.93), calls=%async_computation | async-start | bytes 8388608 | tf_op jit(solution)/shard_map/all_to_all | solution.py:540
  72.0 15.4 %copy-start.2 = (bf16[16,128,128]{2,1,0:T(8,128)(2,1)S(1)}, bf16[16,128,128]{2,1,0:T(8,128)(2,1)}, u32[]{:S(2)}) copy-start(bf16[16,128,128]{2,1,0:T(8,128)(2,1)} %get-tuple-element.108.rest_0_) | copy-start | bytes 1572868
  72.0 7.2 %collective-permute-start.3 = (bf16[2,16,16,256]{3,2,1,0:T(8,128)(2,1)S(1)}, bf16[2,16,16,256]{3,2,1,0:T(8,128)(2,1)S(1)}, u32[]{:S(2)}, u32[]{:S(2)}) collective-permute-start(bf16[2,16,16,256]{3,2,1,0:T(8,128)(2,1)S(1)} %get-tuple-element.115), channel_id=1, source_target_pairs={{0,1},{1,2},{2,3},{3,0},{4,5},{5,6},{6,7},{7,4},{8,9},{9,10},{10,1... | collective-permute-start | bytes 786440 | tf_op jit(solution)/shard_map/ppermute | solution.py:33
  73.4 5.9 %collective-permute-start.4 = (bf16[2,16,16,256]{3,2,1,0:T(8,128)(2,1)S(1)}, bf16[2,16,16,256]{3,2,1,0:T(8,128)(2,1)S(1)}, u32[]{:S(2)}, u32[]{:S(2)}) collective-permute-start(bf16[2,16,16,256]{3,2,1,0:T(8,128)(2,1)S(1)} %get-tuple-element.116), channel_id=1, source_target_pairs={{0,3},{1,0},{2,1},{3,2},{4,7},{5,4},{6,5},{7,6},{8,11},{9,8},{10,9... | collective-permute-start | bytes 786440 | tf_op jit(solution)/shard_map/ppermute | solution.py:33
  74.9 6.7 %collective-permute-start.5 = (bf16[2,16,16,256]{3,2,1,0:T(8,128)(2,1)S(1)}, bf16[2,16,16,256]{3,2,1,0:T(8,128)(2,1)S(1)}, u32[]{:S(2)}, u32[]{:S(2)}) collective-permute-start(bf16[2,16,16,256]{3,2,1,0:T(8,128)(2,1)S(1)} %get-tuple-element.119), channel_id=1, source_target_pairs={{0,4},{1,5},{2,6},{3,7},{4,8},{5,9},{6,10},{7,11},{8,12},{9,13},{1... | collective-permute-start | bytes 786440 | tf_op jit(solution)/shard_map/ppermute | solution.py:29
  76.1 5.5 %collective-permute-start.6 = (bf16[2,16,16,256]{3,2,1,0:T(8,128)(2,1)S(1)}, bf16[2,16,16,256]{3,2,1,0:T(8,128)(2,1)S(1)}, u32[]{:S(2)}, u32[]{:S(2)}) collective-permute-start(bf16[2,16,16,256]{3,2,1,0:T(8,128)(2,1)S(1)} %get-tuple-element.120), channel_id=1, source_target_pairs={{0,12},{1,13},{2,14},{3,15},{4,0},{5,1},{6,2},{7,3},{8,4},{9,5},{1... | collective-permute-start | bytes 786440 | tf_op jit(solution)/shard_map/ppermute | solution.py:29
  82.0 43.9 %copy-start.4 = (bf16[512,512]{1,0:T(8,128)(2,1)S(1)}, bf16[512,512]{1,0:T(8,128)(2,1)}, u32[]{:S(2)}) copy-start(bf16[512,512]{1,0:T(8,128)(2,1)} %w_agg.3) | copy-start | bytes 1572868
  82.0 43.8 %copy-start.5 = (bf16[512,512]{1,0:T(8,128)(2,1)S(1)}, bf16[512,512]{1,0:T(8,128)(2,1)}, u32[]{:S(2)}) copy-start(bf16[512,512]{1,0:T(8,128)(2,1)} %w_out.3) | copy-start | bytes 1572868
  82.0 43.8 %copy-start.6 = (bf16[512,512]{1,0:T(8,128)(2,1)S(1)}, bf16[512,512]{1,0:T(8,128)(2,1)}, u32[]{:S(2)}) copy-start(bf16[512,512]{1,0:T(8,128)(2,1)} %w_pass.1) | copy-start | bytes 1572868
  82.0 11.1 %collective-permute-start.7 = (bf16[4,16,16,256]{3,2,1,0:T(8,128)(2,1)S(1)}, bf16[4,16,16,256]{3,2,1,0:T(8,128)(2,1)S(1)}, u32[]{:S(2)}, u32[]{:S(2)}) collective-permute-start(bf16[4,16,16,256]{3,2,1,0:T(8,128)(2,1)S(1)} %get-tuple-element.121), channel_id=1, source_target_pairs={{0,1},{1,2},{2,3},{3,0},{4,5},{5,6},{6,7},{7,4},{8,9},{9,10},{10,1... | collective-permute-start | bytes 1572872 | tf_op jit(solution)/shard_map/ppermute | solution.py:33
  82.1 12.8 %collective-permute-start.8 = (bf16[4,16,16,256]{3,2,1,0:T(8,128)(2,1)S(1)}, bf16[4,16,16,256]{3,2,1,0:T(8,128)(2,1)S(1)}, u32[]{:S(2)}, u32[]{:S(2)}) collective-permute-start(bf16[4,16,16,256]{3,2,1,0:T(8,128)(2,1)S(1)} %get-tuple-element.122), channel_id=1, source_target_pairs={{0,3},{1,0},{2,1},{3,2},{4,7},{5,4},{6,5},{7,6},{8,11},{9,8},{10,9... | collective-permute-start | bytes 1572872 | tf_op jit(solution)/shard_map/ppermute | solution.py:33
  84.7 11.1 %collective-permute-start.9 = (bf16[4,16,16,256]{3,2,1,0:T(8,128)(2,1)S(1)}, bf16[4,16,16,256]{3,2,1,0:T(8,128)(2,1)S(1)}, u32[]{:S(2)}, u32[]{:S(2)}) collective-permute-start(bf16[4,16,16,256]{3,2,1,0:T(8,128)(2,1)S(1)} %get-tuple-element.124), channel_id=1, source_target_pairs={{0,4},{1,5},{2,6},{3,7},{4,8},{5,9},{6,10},{7,11},{8,12},{9,13},{1... | collective-permute-start | bytes 1572872 | tf_op jit(solution)/shard_map/ppermute | solution.py:29
  85.9 9.9 %collective-permute-start.10 = (bf16[4,16,16,256]{3,2,1,0:T(8,128)(2,1)S(1)}, bf16[4,16,16,256]{3,2,1,0:T(8,128)(2,1)S(1)}, u32[]{:S(2)}, u32[]{:S(2)}) collective-permute-start(bf16[4,16,16,256]{3,2,1,0:T(8,128)(2,1)S(1)} %get-tuple-element.125), channel_id=1, source_target_pairs={{0,12},{1,13},{2,14},{3,15},{4,0},{5,1},{6,2},{7,3},{8,4},{9,5},{1... | collective-permute-start | bytes 1572872 | tf_op jit(solution)/shard_map/ppermute | solution.py:29
  87.4 12.2 %collective-permute-start.2 = (bf16[16,128,128]{2,1,0:T(8,128)(2,1)S(1)}, bf16[16,128,128]{2,1,0:T(8,128)(2,1)S(1)}, u32[]{:S(2)}, u32[]{:S(2)}) collective-permute-start(bf16[16,128,128]{2,1,0:T(8,128)(2,1)S(1)} %copy-done.2), channel_id=1, source_target_pairs={{0,96},{16,112},{32,0},{48,16},{64,32},{80,48},{96,64},{112,80},{1... | collective-permute-start | bytes 1572872 | tf_op jit(solution)/shard_map/ppermute | solution.py:19
  93.1 10.5 %collective-permute-start.1 = (bf16[16,128,128]{2,1,0:T(8,128)(2,1)S(1)}, bf16[16,128,128]{2,1,0:T(8,128)(2,1)S(1)}, u32[]{:S(2)}, u32[]{:S(2)}) collective-permute-start(bf16[16,128,128]{2,1,0:T(8,128)(2,1)S(1)} %copy-done.2), channel_id=1, source_target_pairs={{0,64},{16,80},{32,96},{48,112},{64,0},{80,16},{96,32},{112,48},{1... | collective-permute-start | bytes 1572872 | tf_op jit(solution)/shard_map/ppermute | solution.py:19
  94.9 24.8 %collective-permute-start = (bf16[16,128,128]{2,1,0:T(8,128)(2,1)S(1)}, bf16[16,128,128]{2,1,0:T(8,128)(2,1)S(1)}, u32[]{:S(2)}, u32[]{:S(2)}) collective-permute-start(bf16[16,128,128]{2,1,0:T(8,128)(2,1)S(1)} %copy-done.2), channel_id=1, source_target_pairs={{0,32},{16,48},{32,64},{48,80},{64,96},{80,112},{96,0},{112,16},{1... | collective-permute-start | bytes 1572872 | tf_op jit(solution)/shard_map/ppermute | solution.py:19
  96.3 23.6 %collective-permute-start.11 = (bf16[16,16,256]{2,1,0:T(8,128)(2,1)S(1)}, bf16[16,16,256]{2,1,0:T(8,128)(2,1)S(1)}, u32[]{:S(2)}, u32[]{:S(2)}) collective-permute-start(bf16[16,16,256]{2,1,0:T(8,128)(2,1)S(1)} %get-tuple-element.127), channel_id=1, source_target_pairs={{0,4},{1,5},{2,6},{3,7},{4,8},{5,9},{6,10},{7,11},{8,12},{9,13},{1... | collective-permute-start | bytes 393224 | tf_op jit(solution)/shard_map/ppermute | solution.py:29
  97.0 23.9 %collective-permute-start.12 = (bf16[16,16,256]{2,1,0:T(8,128)(2,1)S(1)}, bf16[16,16,256]{2,1,0:T(8,128)(2,1)S(1)}, u32[]{:S(2)}, u32[]{:S(2)}) collective-permute-start(bf16[16,16,256]{2,1,0:T(8,128)(2,1)S(1)} %get-tuple-element.128), channel_id=1, source_target_pairs={{0,8},{1,9},{2,10},{3,11},{4,12},{5,13},{6,14},{7,15},{8,0},{9,1},... | collective-permute-start | bytes 393224 | tf_op jit(solution)/shard_map/ppermute | solution.py:29
  99.6 21.2 %collective-permute-start.13 = (bf16[16,16,256]{2,1,0:T(8,128)(2,1)S(1)}, bf16[16,16,256]{2,1,0:T(8,128)(2,1)S(1)}, u32[]{:S(2)}, u32[]{:S(2)}) collective-permute-start(bf16[16,16,256]{2,1,0:T(8,128)(2,1)S(1)} %get-tuple-element.129), channel_id=1, source_target_pairs={{0,12},{1,13},{2,14},{3,15},{4,0},{5,1},{6,2},{7,3},{8,4},{9,5},{1... | collective-permute-start | bytes 393224 | tf_op jit(solution)/shard_map/ppermute | solution.py:29
  103.7 17.2 %collective-permute-start.14 = (bf16[16,16,256]{2,1,0:T(8,128)(2,1)S(1)}, bf16[16,16,256]{2,1,0:T(8,128)(2,1)S(1)}, u32[]{:S(2)}, u32[]{:S(2)}) collective-permute-start(bf16[16,16,256]{2,1,0:T(8,128)(2,1)S(1)} %get-tuple-element.131), channel_id=1, source_target_pairs={{0,1},{1,2},{2,3},{3,0},{4,5},{5,6},{6,7},{7,4},{8,9},{9,10},{10,1... | collective-permute-start | bytes 393224 | tf_op jit(solution)/shard_map/ppermute | solution.py:33
  119.7 6.1 %collective-permute-start.15 = (bf16[16,16,256]{2,1,0:T(8,128)(2,1)S(1)}, bf16[16,16,256]{2,1,0:T(8,128)(2,1)S(1)}, u32[]{:S(2)}, u32[]{:S(2)}) collective-permute-start(bf16[16,16,256]{2,1,0:T(8,128)(2,1)S(1)} %get-tuple-element.132), channel_id=1, source_target_pairs={{0,2},{1,3},{2,0},{3,1},{4,6},{5,7},{6,4},{7,5},{8,10},{9,11},{10,... | collective-permute-start | bytes 393224 | tf_op jit(solution)/shard_map/ppermute | solution.py:33
  119.9 5.9 %collective-permute-start.16 = (bf16[16,16,256]{2,1,0:T(8,128)(2,1)S(1)}, bf16[16,16,256]{2,1,0:T(8,128)(2,1)S(1)}, u32[]{:S(2)}, u32[]{:S(2)}) collective-permute-start(bf16[16,16,256]{2,1,0:T(8,128)(2,1)S(1)} %get-tuple-element.133), channel_id=1, source_target_pairs={{0,3},{1,0},{2,1},{3,2},{4,7},{5,4},{6,5},{7,6},{8,11},{9,8},{10,9... | collective-permute-start | bytes 393224 | tf_op jit(solution)/shard_map/ppermute | solution.py:33
  127.2 5.0 %collective-permute-start.17 = (bf16[16,16,128]{2,1,0:T(8,128)(2,1)S(1)}, bf16[16,16,128]{2,1,0:T(8,128)(2,1)S(1)}, u32[]{:S(2)}, u32[]{:S(2)}) collective-permute-start(bf16[16,16,128]{2,1,0:T(8,128)(2,1)S(1)} %get-tuple-element.137), channel_id=1, source_target_pairs={{0,32},{16,48},{32,64},{48,80},{64,96},{80,112},{96,0},{112,16},{1... | collective-permute-start | bytes 196616 | tf_op jit(solution)/shard_map/ppermute | solution.py:19
  127.3 5.1 %collective-permute-start.18 = (bf16[16,16,128]{2,1,0:T(8,128)(2,1)S(1)}, bf16[16,16,128]{2,1,0:T(8,128)(2,1)S(1)}, u32[]{:S(2)}, u32[]{:S(2)}) collective-permute-start(bf16[16,16,128]{2,1,0:T(8,128)(2,1)S(1)} %get-tuple-element.138), channel_id=1, source_target_pairs={{0,64},{16,80},{32,96},{48,112},{64,0},{80,16},{96,32},{112,48},{1... | collective-permute-start | bytes 196616 | tf_op jit(solution)/shard_map/ppermute | solution.py:19
  129.3 3.9 %collective-permute-start.19 = (bf16[16,16,128]{2,1,0:T(8,128)(2,1)S(1)}, bf16[16,16,128]{2,1,0:T(8,128)(2,1)S(1)}, u32[]{:S(2)}, u32[]{:S(2)}) collective-permute-start(bf16[16,16,128]{2,1,0:T(8,128)(2,1)S(1)} %get-tuple-element.139), channel_id=1, source_target_pairs={{0,96},{16,112},{32,0},{48,16},{64,32},{80,48},{96,64},{112,80},{1... | collective-permute-start | bytes 196616 | tf_op jit(solution)/shard_map/ppermute | solution.py:19
  133.7 33.2 %copy-start.7 = (bf16[512,512]{1,0:T(8,128)(2,1)S(1)}, bf16[512,512]{1,0:T(8,128)(2,1)}, u32[]{:S(2)}) copy-start(bf16[512,512]{1,0:T(8,128)(2,1)} %w_agg.2) | copy-start | bytes 1572868
  133.7 9.4 %collective-permute-start.23 = (bf16[16,64,128]{2,1,0:T(8,128)(2,1)S(1)}, bf16[16,64,128]{2,1,0:T(8,128)(2,1)S(1)}, u32[]{:S(2)}, u32[]{:S(2)}) collective-permute-start(bf16[16,64,128]{2,1,0:T(8,128)(2,1)S(1)} %shard_map.190.rest_6_), channel_id=1, source_target_pairs={{0,15},{1,0},{2,1},{3,2},{4,3},{5,4},{6,5},{7,6},{8,7},{9,8},{10,9... | collective-permute-start | bytes 786440 | tf_op jit(solution)/shard_map/ppermute | solution.py:37
  139.3 9.1 %collective-permute-start.20 = (bf16[16,64,128]{2,1,0:T(8,128)(2,1)S(1)}, bf16[16,64,128]{2,1,0:T(8,128)(2,1)S(1)}, u32[]{:S(2)}, u32[]{:S(2)}) collective-permute-start(bf16[16,64,128]{2,1,0:T(8,128)(2,1)S(1)} %shard_map.190.rest_6_), channel_id=1, source_target_pairs={{0,1},{1,2},{2,3},{3,4},{4,5},{5,6},{6,7},{7,8},{8,9},{9,10},{10,1... | collective-permute-start | bytes 786440 | tf_op jit(solution)/shard_map/ppermute | solution.py:37
  139.3 12.0 %collective-permute-start.22 = (bf16[16,64,128]{2,1,0:T(8,128)(2,1)S(1)}, bf16[16,64,128]{2,1,0:T(8,128)(2,1)S(1)}, u32[]{:S(2)}, u32[]{:S(2)}) collective-permute-start(bf16[16,64,128]{2,1,0:T(8,128)(2,1)S(1)} %shard_map.190.rest_6_), channel_id=1, source_target_pairs={{0,16},{16,0},{32,48},{48,32},{64,80},{80,64},{96,112},{112,96},{1... | collective-permute-start | bytes 786440 | tf_op jit(solution)/shard_map/ppermute | solution.py:23
  143.2 8.2 %collective-permute-start.24 = (bf16[16,64,128]{2,1,0:T(8,128)(2,1)S(1)}, bf16[16,64,128]{2,1,0:T(8,128)(2,1)S(1)}, u32[]{:S(2)}, u32[]{:S(2)}) collective-permute-start(bf16[16,64,128]{2,1,0:T(8,128)(2,1)S(1)} %collective-permute-done.23.rest_8_), channel_id=1, source_target_pairs={{0,16},{16,0},{32,48},{48,32},{64,80},{80,64},{96,112},{112,96},{1... | collective-permute-start | bytes 786440 | tf_op jit(solution)/shard_map/ppermute | solution.py:23
  148.4 4.1 %collective-permute-start.21 = (bf16[16,64,128]{2,1,0:T(8,128)(2,1)S(1)}, bf16[16,64,128]{2,1,0:T(8,128)(2,1)S(1)}, u32[]{:S(2)}, u32[]{:S(2)}) collective-permute-start(bf16[16,64,128]{2,1,0:T(8,128)(2,1)S(1)} %collective-permute-done.20.rest_4_), channel_id=1, source_target_pairs={{0,16},{16,0},{32,48},{48,32},{64,80},{80,64},{96,112},{112,96},{1... | collective-permute-start | bytes 786440 | tf_op jit(solution)/shard_map/ppermute | solution.py:23
  156.9 1.6 collective-permute-start.25
  159.2 5.4 %collective-permute-start.26 = (bf16[16,16,128]{2,1,0:T(8,128)(2,1)S(1)}, bf16[16,16,128]{2,1,0:T(8,128)(2,1)S(1)}, u32[]{:S(2)}, u32[]{:S(2)}) collective-permute-start(bf16[16,16,128]{2,1,0:T(8,128)(2,1)S(1)} %get-tuple-element.143), channel_id=1, source_target_pairs={{0,32},{16,48},{32,64},{48,80},{64,96},{80,112},{96,0},{112,16},{1... | collective-permute-start | bytes 196616 | tf_op jit(solution)/shard_map/ppermute | solution.py:19
  160.3 6.2 %collective-permute-start.27 = (bf16[16,16,128]{2,1,0:T(8,128)(2,1)S(1)}, bf16[16,16,128]{2,1,0:T(8,128)(2,1)S(1)}, u32[]{:S(2)}, u32[]{:S(2)}) collective-permute-start(bf16[16,16,128]{2,1,0:T(8,128)(2,1)S(1)} %get-tuple-element.144), channel_id=1, source_target_pairs={{0,64},{16,80},{32,96},{48,112},{64,0},{80,16},{96,32},{112,48},{1... | collective-permute-start | bytes 196616 | tf_op jit(solution)/shard_map/ppermute | solution.py:19
  163.6 3.4 %collective-permute-start.28 = (bf16[16,16,128]{2,1,0:T(8,128)(2,1)S(1)}, bf16[16,16,128]{2,1,0:T(8,128)(2,1)S(1)}, u32[]{:S(2)}, u32[]{:S(2)}) collective-permute-start(bf16[16,16,128]{2,1,0:T(8,128)(2,1)S(1)} %get-tuple-element.145), channel_id=1, source_target_pairs={{0,96},{16,112},{32,0},{48,16},{64,32},{80,48},{96,64},{112,80},{1... | collective-permute-start | bytes 196616 | tf_op jit(solution)/shard_map/ppermute | solution.py:19
  168.4 4.4 %collective-permute-start.29 = (bf16[16,16,128]{2,1,0:T(8,128)(2,1)S(1)}, bf16[16,16,128]{2,1,0:T(8,128)(2,1)S(1)}, u32[]{:S(2)}, u32[]{:S(2)}) collective-permute-start(bf16[16,16,128]{2,1,0:T(8,128)(2,1)S(1)} %get-tuple-element.149), channel_id=1, source_target_pairs={{0,32},{16,48},{32,64},{48,80},{64,96},{80,112},{96,0},{112,16},{1... | collective-permute-start | bytes 196616 | tf_op jit(solution)/shard_map/ppermute | solution.py:19
  168.5 5.7 %collective-permute-start.30 = (bf16[16,16,128]{2,1,0:T(8,128)(2,1)S(1)}, bf16[16,16,128]{2,1,0:T(8,128)(2,1)S(1)}, u32[]{:S(2)}, u32[]{:S(2)}) collective-permute-start(bf16[16,16,128]{2,1,0:T(8,128)(2,1)S(1)} %get-tuple-element.150), channel_id=1, source_target_pairs={{0,64},{16,80},{32,96},{48,112},{64,0},{80,16},{96,32},{112,48},{1... | collective-permute-start | bytes 196616 | tf_op jit(solution)/shard_map/ppermute | solution.py:19
  171.8 3.4 %collective-permute-start.31 = (bf16[16,16,128]{2,1,0:T(8,128)(2,1)S(1)}, bf16[16,16,128]{2,1,0:T(8,128)(2,1)S(1)}, u32[]{:S(2)}, u32[]{:S(2)}) collective-permute-start(bf16[16,16,128]{2,1,0:T(8,128)(2,1)S(1)} %get-tuple-element.151), channel_id=1, source_target_pairs={{0,96},{16,112},{32,0},{48,16},{64,32},{80,48},{96,64},{112,80},{1... | collective-permute-start | bytes 196616 | tf_op jit(solution)/shard_map/ppermute | solution.py:19
  175.8 3.5 %collective-permute-start.32 = (bf16[16,64,128]{2,1,0:T(8,128)(2,1)S(1)}, bf16[16,64,128]{2,1,0:T(8,128)(2,1)S(1)}, u32[]{:S(2)}, u32[]{:S(2)}) collective-permute-start(bf16[16,64,128]{2,1,0:T(8,128)(2,1)S(1)} %shard_map.194.rest_4_), channel_id=1, source_target_pairs={{0,16},{16,0},{32,48},{48,32},{64,80},{80,64},{96,112},{112,96},{1... | collective-permute-start | bytes 786440 | tf_op jit(solution)/shard_map/ppermute | solution.py:23
  183.4 2.4 collective-permute-start.33
  185.9 7.6 %collective-permute-start.34 = (bf16[16,64,128]{2,1,0:T(8,128)(2,1)S(1)}, bf16[16,64,128]{2,1,0:T(8,128)(2,1)S(1)}, u32[]{:S(2)}, u32[]{:S(2)}) collective-permute-start(bf16[16,64,128]{2,1,0:T(8,128)(2,1)S(1)} %get-tuple-element.154), channel_id=1, source_target_pairs={{0,15},{1,0},{2,1},{3,2},{4,3},{5,4},{6,5},{7,6},{8,7},{9,8},{10,9... | collective-permute-start | bytes 786440 | tf_op jit(solution)/shard_map/ppermute | solution.py:37
  186.3 10.5 %collective-permute-start.35 = (bf16[16,64,128]{2,1,0:T(8,128)(2,1)S(1)}, bf16[16,64,128]{2,1,0:T(8,128)(2,1)S(1)}, u32[]{:S(2)}, u32[]{:S(2)}) collective-permute-start(bf16[16,64,128]{2,1,0:T(8,128)(2,1)S(1)} %get-tuple-element.158), channel_id=1, source_target_pairs={{0,1},{1,2},{2,3},{3,4},{4,5},{5,6},{6,7},{7,8},{8,9},{9,10},{10,1... | collective-permute-start | bytes 786440 | tf_op jit(solution)/shard_map/ppermute | solution.py:37
  187.4 13.5 %collective-permute-start.41 = (bf16[256,512]{1,0:T(8,128)(2,1)S(1)}, bf16[256,512]{1,0:T(8,128)(2,1)S(1)}, u32[]{:S(2)}, u32[]{:S(2)}) collective-permute-start(bf16[256,512]{1,0:T(8,128)(2,1)S(1)} %get-tuple-element.172.p0), channel_id=1, source_target_pairs={{0,96},{16,112},{32,0},{48,16},{64,32},{80,48},{96,64},{112,80},{1... | collective-permute-start | bytes 786440 | tf_op jit(solution)/shard_map/ppermute | solution.py:19
  189.6 11.7 %collective-permute-start.40 = (bf16[256,512]{1,0:T(8,128)(2,1)S(1)}, bf16[256,512]{1,0:T(8,128)(2,1)S(1)}, u32[]{:S(2)}, u32[]{:S(2)}) collective-permute-start(bf16[256,512]{1,0:T(8,128)(2,1)S(1)} %get-tuple-element.172.p0), channel_id=1, source_target_pairs={{0,64},{16,80},{32,96},{48,112},{64,0},{80,16},{96,32},{112,48},{1... | collective-permute-start | bytes 786440 | tf_op jit(solution)/shard_map/ppermute | solution.py:19
  190.1 15.1 %collective-permute-start.39 = (bf16[256,512]{1,0:T(8,128)(2,1)S(1)}, bf16[256,512]{1,0:T(8,128)(2,1)S(1)}, u32[]{:S(2)}, u32[]{:S(2)}) collective-permute-start(bf16[256,512]{1,0:T(8,128)(2,1)S(1)} %get-tuple-element.172.p0), channel_id=1, source_target_pairs={{0,32},{16,48},{32,64},{48,80},{64,96},{80,112},{96,0},{112,16},{1... | collective-permute-start | bytes 786440 | tf_op jit(solution)/shard_map/ppermute | solution.py:19
  197.5 9.6 %collective-permute-start.36 = (bf16[16,16,128]{2,1,0:T(8,128)(2,1)S(1)}, bf16[16,16,128]{2,1,0:T(8,128)(2,1)S(1)}, u32[]{:S(2)}, u32[]{:S(2)}) collective-permute-start(bf16[16,16,128]{2,1,0:T(8,128)(2,1)S(1)} %get-tuple-element.160), channel_id=1, source_target_pairs={{0,32},{16,48},{32,64},{48,80},{64,96},{80,112},{96,0},{112,16},{1... | collective-permute-start | bytes 196616 | tf_op jit(solution)/shard_map/ppermute | solution.py:19
  198.4 8.7 %collective-permute-start.37 = (bf16[16,16,128]{2,1,0:T(8,128)(2,1)S(1)}, bf16[16,16,128]{2,1,0:T(8,128)(2,1)S(1)}, u32[]{:S(2)}, u32[]{:S(2)}) collective-permute-start(bf16[16,16,128]{2,1,0:T(8,128)(2,1)S(1)} %get-tuple-element.161), channel_id=1, source_target_pairs={{0,64},{16,80},{32,96},{48,112},{64,0},{80,16},{96,32},{112,48},{1... | collective-permute-start | bytes 196616 | tf_op jit(solution)/shard_map/ppermute | solution.py:19
  200.9 6.1 %collective-permute-start.38 = (bf16[16,16,128]{2,1,0:T(8,128)(2,1)S(1)}, bf16[16,16,128]{2,1,0:T(8,128)(2,1)S(1)}, u32[]{:S(2)}, u32[]{:S(2)}) collective-permute-start(bf16[16,16,128]{2,1,0:T(8,128)(2,1)S(1)} %get-tuple-element.162), channel_id=1, source_target_pairs={{0,96},{16,112},{32,0},{48,16},{64,32},{80,48},{96,64},{112,80},{1... | collective-permute-start | bytes 196616 | tf_op jit(solution)/shard_map/ppermute | solution.py:19
  208.4 4.7 %collective-permute-start.44 = (bf16[16,16,256]{2,1,0:T(8,128)(2,1)S(1)}, bf16[16,16,256]{2,1,0:T(8,128)(2,1)S(1)}, u32[]{:S(2)}, u32[]{:S(2)}) collective-permute-start(bf16[16,16,256]{2,1,0:T(8,128)(2,1)S(1)} %get-tuple-element.168.refs_0_), channel_id=1, source_target_pairs={{0,12},{1,13},{2,14},{3,15},{4,0},{5,1},{6,2},{7,3},{8,4},{9,5},{1... | collective-permute-start | bytes 393224 | tf_op jit(solution)/shard_map/ppermute | solution.py:29
  208.5 5.5 %collective-permute-start.43 = (bf16[16,16,256]{2,1,0:T(8,128)(2,1)S(1)}, bf16[16,16,256]{2,1,0:T(8,128)(2,1)S(1)}, u32[]{:S(2)}, u32[]{:S(2)}) collective-permute-start(bf16[16,16,256]{2,1,0:T(8,128)(2,1)S(1)} %get-tuple-element.168.refs_0_), channel_id=1, source_target_pairs={{0,8},{1,9},{2,10},{3,11},{4,12},{5,13},{6,14},{7,15},{8,0},{9,1},... | collective-permute-start | bytes 393224 | tf_op jit(solution)/shard_map/ppermute | solution.py:29
  208.6 8.9 %collective-permute-start.42 = (bf16[16,16,256]{2,1,0:T(8,128)(2,1)S(1)}, bf16[16,16,256]{2,1,0:T(8,128)(2,1)S(1)}, u32[]{:S(2)}, u32[]{:S(2)}) collective-permute-start(bf16[16,16,256]{2,1,0:T(8,128)(2,1)S(1)} %get-tuple-element.168.refs_0_), channel_id=1, source_target_pairs={{0,4},{1,5},{2,6},{3,7},{4,8},{5,9},{6,10},{7,11},{8,12},{9,13},{1... | collective-permute-start | bytes 393224 | tf_op jit(solution)/shard_map/ppermute | solution.py:29
  210.0 7.5 %collective-permute-start.47 = (bf16[16,16,256]{2,1,0:T(8,128)(2,1)S(1)}, bf16[16,16,256]{2,1,0:T(8,128)(2,1)S(1)}, u32[]{:S(2)}, u32[]{:S(2)}) collective-permute-start(bf16[16,16,256]{2,1,0:T(8,128)(2,1)S(1)} %get-tuple-element.169.refs_4_), channel_id=1, source_target_pairs={{0,3},{1,0},{2,1},{3,2},{4,7},{5,4},{6,5},{7,6},{8,11},{9,8},{10,9... | collective-permute-start | bytes 393224 | tf_op jit(solution)/shard_map/ppermute | solution.py:33
  213.1 5.4 %collective-permute-start.46 = (bf16[16,16,256]{2,1,0:T(8,128)(2,1)S(1)}, bf16[16,16,256]{2,1,0:T(8,128)(2,1)S(1)}, u32[]{:S(2)}, u32[]{:S(2)}) collective-permute-start(bf16[16,16,256]{2,1,0:T(8,128)(2,1)S(1)} %get-tuple-element.169.refs_4_), channel_id=1, source_target_pairs={{0,2},{1,3},{2,0},{3,1},{4,6},{5,7},{6,4},{7,5},{8,10},{9,11},{10,... | collective-permute-start | bytes 393224 | tf_op jit(solution)/shard_map/ppermute | solution.py:33
  213.1 6.4 %collective-permute-start.45 = (bf16[16,16,256]{2,1,0:T(8,128)(2,1)S(1)}, bf16[16,16,256]{2,1,0:T(8,128)(2,1)S(1)}, u32[]{:S(2)}, u32[]{:S(2)}) collective-permute-start(bf16[16,16,256]{2,1,0:T(8,128)(2,1)S(1)} %get-tuple-element.169.refs_4_), channel_id=1, source_target_pairs={{0,1},{1,2},{2,3},{3,0},{4,5},{5,6},{6,7},{7,4},{8,9},{9,10},{10,1... | collective-permute-start | bytes 393224 | tf_op jit(solution)/shard_map/ppermute | solution.py:33
  219.6 9.1 %collective-permute-start.50 = (bf16[4,16,16,256]{3,2,1,0:T(8,128)(2,1)S(1)}, bf16[4,16,16,256]{3,2,1,0:T(8,128)(2,1)S(1)}, u32[]{:S(2)}, u32[]{:S(2)}) collective-permute-start(bf16[4,16,16,256]{3,2,1,0:T(8,128)(2,1)S(1)} %get-tuple-element.170.rest_0_), channel_id=1, source_target_pairs={{0,3},{1,0},{2,1},{3,2},{4,7},{5,4},{6,5},{7,6},{8,11},{9,8},{10,9... | collective-permute-start | bytes 1572872 | tf_op jit(solution)/shard_map/ppermute | solution.py:33
  220.6 10.7 %collective-permute-start.49 = (bf16[4,16,16,256]{3,2,1,0:T(8,128)(2,1)S(1)}, bf16[4,16,16,256]{3,2,1,0:T(8,128)(2,1)S(1)}, u32[]{:S(2)}, u32[]{:S(2)}) collective-permute-start(bf16[4,16,16,256]{3,2,1,0:T(8,128)(2,1)S(1)} %get-tuple-element.170.rest_0_), channel_id=1, source_target_pairs={{0,2},{1,3},{2,0},{3,1},{4,6},{5,7},{6,4},{7,5},{8,10},{9,11},{10,... | collective-permute-start | bytes 1572872 | tf_op jit(solution)/shard_map/ppermute | solution.py:33
  220.6 26.5 %collective-permute-start.48 = (bf16[4,16,16,256]{3,2,1,0:T(8,128)(2,1)S(1)}, bf16[4,16,16,256]{3,2,1,0:T(8,128)(2,1)S(1)}, u32[]{:S(2)}, u32[]{:S(2)}) collective-permute-start(bf16[4,16,16,256]{3,2,1,0:T(8,128)(2,1)S(1)} %get-tuple-element.170.rest_0_), channel_id=1, source_target_pairs={{0,1},{1,2},{2,3},{3,0},{4,5},{5,6},{6,7},{7,4},{8,9},{9,10},{10,1... | collective-permute-start | bytes 1572872 | tf_op jit(solution)/shard_map/ppermute | solution.py:33
  221.3 25.9 %collective-permute-start.53 = (bf16[4,16,16,256]{3,2,1,0:T(8,128)(2,1)S(1)}, bf16[4,16,16,256]{3,2,1,0:T(8,128)(2,1)S(1)}, u32[]{:S(2)}, u32[]{:S(2)}) collective-permute-start(bf16[4,16,16,256]{3,2,1,0:T(8,128)(2,1)S(1)} %get-tuple-element.171.rest_4_), channel_id=1, source_target_pairs={{0,12},{1,13},{2,14},{3,15},{4,0},{5,1},{6,2},{7,3},{8,4},{9,5},{1... | collective-permute-start | bytes 1572872 | tf_op jit(solution)/shard_map/ppermute | solution.py:29
  223.8 23.4 %collective-permute-start.52 = (bf16[4,16,16,256]{3,2,1,0:T(8,128)(2,1)S(1)}, bf16[4,16,16,256]{3,2,1,0:T(8,128)(2,1)S(1)}, u32[]{:S(2)}, u32[]{:S(2)}) collective-permute-start(bf16[4,16,16,256]{3,2,1,0:T(8,128)(2,1)S(1)} %get-tuple-element.171.rest_4_), channel_id=1, source_target_pairs={{0,8},{1,9},{2,10},{3,11},{4,12},{5,13},{6,14},{7,15},{8,0},{9,1},... | collective-permute-start | bytes 1572872 | tf_op jit(solution)/shard_map/ppermute | solution.py:29
  228.8 18.4 %collective-permute-start.51 = (bf16[4,16,16,256]{3,2,1,0:T(8,128)(2,1)S(1)}, bf16[4,16,16,256]{3,2,1,0:T(8,128)(2,1)S(1)}, u32[]{:S(2)}, u32[]{:S(2)}) collective-permute-start(bf16[4,16,16,256]{3,2,1,0:T(8,128)(2,1)S(1)} %get-tuple-element.171.rest_4_), channel_id=1, source_target_pairs={{0,4},{1,5},{2,6},{3,7},{4,8},{5,9},{6,10},{7,11},{8,12},{9,13},{1... | collective-permute-start | bytes 1572872 | tf_op jit(solution)/shard_map/ppermute | solution.py:29
  250.3 59.3 %all-to-all-start.1 = ((bf16[8,32,16,512]{3,2,1,0:T(8,128)(2,1)}), bf16[8,32,16,512]{3,2,1,0:T(8,128)(2,1)}, u32[]{:S(2)}, u32[]{:S(2)}) async-start(bf16[8,32,16,512]{3,2,1,0:T(8,128)(2,1)} %shard_map.200), calls=%async_computation.1 | async-start | bytes 8388608 | tf_op jit(solution)/shard_map/all_to_all | solution.py:540
  261.3 2.7 collective-permute-start.54
  (7 other events, 39.4 us)
